TPU v7x, 128 devices: a whole 4x4x4 slice. The times are simulated.
128 devices in a mesh: batch: 2 (over core), table: 64 (over y, x, z).
Axes of the slice: x: 4, y: 4, z: 4, core: 2. Of those that a mesh axis runs over, the one named last changes fastest.
Arguments:
- gate_pre: bfloat16 [32768, 4096], P(('batch', 'table')), may hold values from -6 to 6
- pick_logits: float32 [32768, 32], P(('batch', 'table')), may hold values from -8 to 260
- requests: int32 [2048, 64], P(('batch', 'table')), may hold values from -1 to 127, as said below
- slot_of_pick: int32 [32768, 32], P(('batch', 'table')), may hold values from 0 to 1023, as said below
- values: bfloat16 [8192, 4096], P('table'), may hold values from -6 to 6
- first_moment: float32 [8192, 4096], P('table'), may hold values from -2 to 2
- second_moment: float32 [8192, 4096], P('table'), may hold values from 0.01 to 1
- out_grad: bfloat16 [32768, 4096], P(('batch', 'table')), may hold values from -24 to 24
Outputs:
- layer_out: bfloat16 [32768, 4096], P(('batch', 'table'))
- gate_grad: bfloat16 [32768, 4096], P(('batch', 'table'))
- logit_grad: float32 [32768, 32], P(('batch', 'table'))
- value_next: bfloat16 [8192, 4096], P('table')
- first_next: float32 [8192, 4096], P('table')
- second_next: float32 [8192, 4096], P('table')
Inputs may be any that keep to these rules, and one draw needn't show every extreme that they name: `requests`: row d * 16 + j, column p holds the j-th of the distinct rows, numbered within owner p's block of 128 rows, that device d of the batch+table order asks owner p for, or -1. Each device asks each owner for 2 to 16 rows, listed first in its column. In every draw some owner gets 16 rows from every device, and some device asks 16 rows of every owner. `slot_of_pick`: entry (i, k) names slot j * 64 + p of token i's own device, that is the entry of requests in row d * 16 + j, column p, which is never -1. The 32 slots of a token differ, and every entry of a device's requests that is not -1 is named by some pick of that device's tokens.
All inputs are finite; a program needn't handle non-finite values.
Results may differ from a plain program's by a relative error of at most 0.0071.
Values may be sent and summed in bfloat16 or wider, within the bound.
No kernel may reach another device: no remote copies, remote signals or barrier semaphores. Data moves between devices by JAX's collectives and lax.ppermute only.
A program may use at most 192 MiB of HBM per device.

v0:
```python
import jax
import jax.numpy as jnp
from jax import lax
from jax.sharding import PartitionSpec as P

learn_rate = 0.001


def sum_rows(grads, request_lists, row_count):
    target = jnp.where(request_lists >= 0, request_lists, row_count).reshape(-1)
    width_here = grads.shape[-1]
    total = (
        jnp.zeros((row_count, width_here), jnp.float32)
        .at[target]
        .add(grads.reshape(target.shape[0], width_here), mode="drop")
    )
    touch_count = jnp.zeros((row_count,), jnp.float32).at[target].add(1.0, mode="drop")
    return (total, touch_count)


def adam_rows(value_part, first_part, second_part, row_grad, touch_count):
    touched = (touch_count > 0.0)[:, None]
    first_new = 0.9 * first_part + 0.1 * row_grad
    second_new = 0.95 * second_part + 0.05 * row_grad * row_grad
    value_new = (
        value_part.astype(jnp.float32) - learn_rate * first_new / (jnp.sqrt(second_new) + 1e-08)
    ).astype(jnp.bfloat16)
    return (
        jnp.where(touched, value_new, value_part),
        jnp.where(touched, first_new, first_part),
        jnp.where(touched, second_new, second_part),
    )


def local(
    gate_pre, pick_logits, requests, slot_of_pick, values, first_moment, second_moment, out_grad
):
    tokens_here = gate_pre.shape[0]
    model_width = gate_pre.shape[1]
    table_size = lax.axis_size("table")
    capacity = requests.shape[0]
    slot_count = capacity * table_size
    row_count = values.shape[0]
    weights = jax.nn.softmax(pick_logits, axis=-1)
    token_index = jnp.arange(tokens_here, dtype=jnp.int32)[:, None]
    packed = (
        jnp.zeros((tokens_here, slot_count), jnp.float32)
        .at[token_index, slot_of_pick]
        .add(weights)
        .astype(jnp.bfloat16)
    )
    asked_rows = lax.all_to_all(requests, "table", split_axis=1, concat_axis=1, tiled=True)
    found_rows = jnp.where(
        (asked_rows >= 0)[..., None],
        values[jnp.maximum(asked_rows, 0)],
        jnp.zeros((), jnp.bfloat16),
    )
    returned = lax.all_to_all(found_rows, "table", split_axis=1, concat_axis=1, tiled=True)
    fetched = returned.reshape(slot_count, model_width)
    memory = jnp.dot(packed, fetched, preferred_element_type=jnp.float32)
    gate_wide = gate_pre.astype(jnp.float32)
    sigmoid_gate = jax.nn.sigmoid(gate_wide)
    silu_gate = gate_wide * sigmoid_gate
    grad_wide = out_grad.astype(jnp.float32)
    layer_out = (silu_gate * memory).astype(jnp.bfloat16)
    gated = (grad_wide * silu_gate).astype(jnp.bfloat16)
    gate_grad = (
        grad_wide * memory * sigmoid_gate * (1.0 + gate_wide * (1.0 - sigmoid_gate))
    ).astype(jnp.bfloat16)
    score_table = lax.dot_general(
        gated, fetched, (((1,), (1,)), ((), ())), preferred_element_type=jnp.float32
    )
    pick_score = jnp.take_along_axis(score_table, slot_of_pick, axis=1)
    logit_grad = weights * (pick_score - jnp.sum(weights * pick_score, axis=-1, keepdims=True))
    slot_grad = lax.dot_general(
        packed, gated, (((0,), (0,)), ((), ())), preferred_element_type=jnp.float32
    )
    slot_grad = slot_grad.reshape(capacity, table_size, model_width)
    arrived = lax.all_to_all(slot_grad, "table", split_axis=1, concat_axis=1, tiled=True)
    row_grad, touch_count = sum_rows(arrived, asked_rows, row_count)
    row_grad, touch_count = lax.psum((row_grad, touch_count), "batch")
    value_next, first_next, second_next = adam_rows(
        values, first_moment, second_moment, row_grad, touch_count
    )
    return (layer_out, gate_grad, logit_grad, value_next, first_next, second_next)


def solution(mesh):
    placed = (
        P(("batch", "table"), None),
        P(("batch", "table"), None),
        P(("batch", "table"), None),
        P(("batch", "table"), None),
        P("table", None),
        P("table", None),
        P("table", None),
        P(("batch", "table"), None),
    )
    return jax.shard_map(
        local,
        mesh=mesh,
        in_specs=placed,
        out_specs=(
            P(("batch", "table"), None),
            P(("batch", "table"), None),
            P(("batch", "table"), None),
            P("table", None),
            P("table", None),
            P("table", None),
        ),
        check_vma=False,
    )
```

profile of v0, /device:TPU:1, one launch (start us, length us, event | category | flops | bytes accessed | tf_op | source)
XLA Modules:
  0.0 693.7 jit_solution(5256133016962218)
XLA Ops:
  7.2 0.8 copy.52
  7.9 20.2 %all_to_all.22 = s32[16,64,1]{0,2,1:T(1,128)S(1)} all-to-all(s32[16,64,1]{0,2,1:T(1,128)S(1)} %bitcast.27), channel_id=1, replica_groups=mesh['batch'=2,'table'=64] {'table'}, dimensions={1} | all-to-all | bytes 8192 | tf_op jit(solution)/shard_map/all_to_all | solution.py:52
  28.4 16.6 %gather_fusion = bf16[1024,4096]{1,0:T(8,128)(2,1)} fusion(bf16[128,4096]{1,0:T(8,128)(2,1)} %param.12, s32[1024]{0:T(1024)S(1)} %broadcast_clamp_fusion), kind=kCustom, calls=%fused_computation | custom fusion | bytes 16781312 | tf_op jit(solution)/shard_map/gather | solution.py:55
  44.9 16.3 %copy_select_fusion = bf16[16,64,4096]{2,0,1:T(8,128)(2,1)} fusion(bf16[16,64,4096]{2,1,0:T(8,128)(2,1)} %bitcast.22, pred[16,64]{0,1:T(8,128)(4,1)S(1)} %copy.54), kind=kLoop, calls=%fused_computation.5 | loop fusion | flops 4194304 | bytes 16778240 | tf_op jit(solution)/shard_map/jit(_where)/select_n | solution.py:53
  61.3 6.1 all-to-all-start.1
  68.5 115.3 %all-to-all-done.1 = bf16[16,64,4096]{2,0,1:T(8,128)(2,1)} async-done(((bf16[16,64,4096]{2,0,1:T(8,128)(2,1)}), bf16[16,64,4096]{2,0,1:T(8,128)(2,1)}, u32[]{:S(2)}, u32[]{:S(2)}) %all-to-all-start.1) | async-done | bytes 8388640 | tf_op jit(solution)/shard_map/all_to_all | solution.py:58
  183.8 11.3 %copy.57 = bf16[16,64,4096]{2,1,0:T(8,128)(2,1)} copy(bf16[16,64,4096]{2,0,1:T(8,128)(2,1)} %all-to-all-done.1) | data formatting | bytes 16777216 | tf_op jit(solution)/shard_map/all_to_all | solution.py:58
  195.1 6.8 fusion.23
  202.0 65.0 %gather_fusion.1 = f32[8192]{0:T(1024)S(1)} fusion(f32[256,1024]{1,0:T(8,128)S(1)} %fusion.23, s32[8192]{0:T(1024)S(1)} %reshape.82), kind=kCustom, calls=%fused_computation.1 | custom fusion | bytes 131072 | tf_op jit(solution)/shard_map/jit(take_along_axis)/gather | solution.py:73
  267.1 0.2 multiply_reduce_fusion
  267.4 56.7 %scatter_custom_fusion.2 = f32[262144]{0:T(1024)S(1)} fusion(s32[8192]{0:T(1024)S(1)} %reshape.104, f32[8192]{0:T(1024)S(1)} %reshape.106, f32[]{:T(128)} %constant.16.clone.1), kind=kCustom, calls=%fused_computation.29 | custom fusion | flops 8192 | bytes 1048580
  324.4 4.9 fusion.21
  329.3 18.7 %copy.59 = f32[16,64,4096]{2,0,1:T(8,128)} copy(f32[16,64,4096]{2,1,0:T(8,128)S(1)} %bitcast.24) | data formatting | bytes 33554432 | tf_op jit(solution)/shard_map/reshape | solution.py:78
  348.0 9.8 %all-to-all-start.2 = ((f32[16,64,4096]{2,0,1:T(8,128)}), f32[16,64,4096]{2,0,1:T(8,128)}, u32[]{:S(2)}, u32[]{:S(2)}) async-start(f32[16,64,4096]{2,0,1:T(8,128)} %copy.59), calls=%async_computation.2 | async-start | bytes 33554432 | tf_op jit(solution)/shard_map/all_to_all | solution.py:79
  358.0 234.1 %all-to-all-done.2 = f32[16,64,4096]{2,0,1:T(8,128)} async-done(((f32[16,64,4096]{2,0,1:T(8,128)}), f32[16,64,4096]{2,0,1:T(8,128)}, u32[]{:S(2)}, u32[]{:S(2)}) %all-to-all-start.2) | async-done | bytes 16777248 | tf_op jit(solution)/shard_map/all_to_all | solution.py:79
  592.1 17.7 %copy.60 = f32[16,64,4096]{2,1,0:T(8,128)} copy(f32[16,64,4096]{2,0,1:T(8,128)} %all-to-all-done.2) | data formatting | bytes 33554432 | tf_op jit(solution)/shard_map/all_to_all | solution.py:79
  609.8 27.9 %scatter_custom_fusion.1 = f32[128,4096]{1,0:T(8,128)} fusion(s32[1024]{0:T(1024)S(1)} %bitcast.28, f32[1024,4096]{1,0:T(8,128)} %bitcast.23, f32[]{:T(128)} %constant.16.clone.1), kind=kCustom, calls=%fused_computation.27 | custom fusion | flops 4194304 | bytes 2097664 | tf_op jit(solution)/shard_map/scatter-add | solution.py:15
  637.7 7.6 %scatter_custom_fusion = f32[128]{0:T(128)S(1)} fusion(s32[1024]{0:T(1024)S(1)} %bitcast.29, f32[1024]{0:T(1024)S(1)} %broadcast.79, f32[]{:T(128)} %constant.16.clone.1), kind=kCustom, calls=%fused_computation.50 | custom fusion | flops 1024 | bytes 516 | tf_op jit(solution)/shard_map/scatter-add | solution.py:17
  645.4 8.9 %psum.14 = f32[128]{0:T(128)S(1)} all-reduce(f32[128]{0:T(128)S(1)} %scatter_custom_fusion), channel_id=1, replica_groups=mesh['batch'=2,'table'=64] {'batch'}, use_global_device_ids=true, to_apply=%region_5.6 | all-reduce | flops 128 | bytes 1024 | tf_op jit(solution)/shard_map/psum | solution.py:81
  654.4 0.7 copy.61
  655.1 10.4 %fusion.2 = (bf16[256,4096]{1,0:T(8,128)(2,1)}, bf16[256,4096]{1,0:T(8,128)(2,1)}) fusion(bf16[256,4096]{1,0:T(8,128)(2,1)} %param.15, bf16[256,4096]{1,0:T(8,128)(2,1)} %param.8, bf16[256,1024]{1,0:T(8,128)(2,1)} %copy-done.4, bf16[1024,4096]{1,0:T(8,128)(2,1)} %bitcast.26), kind=kOutput, calls=%fused_computation.13 | convolution fusion | flops 2163212288 | bytes 17301504 | tf_op jit(solution)/shard_map/dot_general | solution.py:60
  665.5 13.4 %all-reduce.2.cloned.1.call-done = f32[128,4096]{1,0:T(8,128)} async-done(((f32[128,4096]{1,0:T(8,128)}), f32[128,4096]{1,0:T(8,128)}) %all-reduce.2.cloned.1.call-update) | async-done | bytes 2097168 | tf_op jit(solution)/shard_map/psum | solution.py:81
  679.0 4.8 fusion.11
  683.8 2.8 fusion.10
  (51 shorter events, 2.0 us)
Async XLA Ops:
  61.3 6.1 copy-start.6
  61.3 6.3 copy-start.7
  61.3 6.4 copy-start.8
  61.3 6.9 copy-start.5
  61.3 122.5 %all-to-all-start.1 = ((bf16[16,64,4096]{2,0,1:T(8,128)(2,1)}), bf16[16,64,4096]{2,0,1:T(8,128)(2,1)}, u32[]{:S(2)}, u32[]{:S(2)}) async-start(bf16[16,64,4096]{2,0,1:T(8,128)(2,1)} %copy_select_fusion), calls=%async_computation.1 | async-start | bytes 16777216 | tf_op jit(solution)/shard_map/all_to_all | solution.py:58
  183.8 11.3 %copy-start.9 = (bf16[256,4096]{1,0:T(8,128)(2,1)S(1)}, bf16[256,4096]{1,0:T(8,128)(2,1)}, u32[]{:S(2)}) copy-start(bf16[256,4096]{1,0:T(8,128)(2,1)} %param.15) | copy-start | bytes 6291460
  324.3 4.9 copy-start.4
  348.0 244.1 %all-to-all-start.2 = ((f32[16,64,4096]{2,0,1:T(8,128)}), f32[16,64,4096]{2,0,1:T(8,128)}, u32[]{:S(2)}, u32[]{:S(2)}) async-start(f32[16,64,4096]{2,0,1:T(8,128)} %copy.59), calls=%async_computation.2 | async-start | bytes 33554432 | tf_op jit(solution)/shard_map/all_to_all | solution.py:79
  357.8 321.1 %all-reduce.2.cloned.1.call-start = ((), (), s32[]{:S(2)}) async-start(), calls=%async_computation.3 | async-start | bytes 4194304 | tf_op jit(solution)/shard_map/psum | solution.py:81
  655.1 23.9 %copy-start = (bf16[128,4096]{1,0:T(8,128)(2,1)S(1)}, bf16[128,4096]{1,0:T(8,128)(2,1)}, u32[]{:S(2)}) copy-start(bf16[128,4096]{1,0:T(8,128)(2,1)} %param.12) | copy-start | bytes 3145732
  655.1 23.9 %copy-start.1 = (f32[128,4096]{1,0:T(8,128)S(1)}, f32[128,4096]{1,0:T(8,128)}, u32[]{:S(2)}) copy-start(f32[128,4096]{1,0:T(8,128)} %param.14) | copy-start | bytes 6291460
  679.0 4.9 copy-start.2
  679.0 4.9 copy-start.3
Sparse Core Ops, SparseCore 0:
  637.9 41.0 all-reduce.1
where the time goes:
time: 697 us; the launch traced here: 694 us
  waiting for transfers between devices  363 us (52%)
  local copies, waits for them, and re-layouts  132 us (19%)
  other arithmetic  117 us (17%)
  blocking collectives  29.1 us (4%)
  matrix products  22.2 us (3%)
  starting transfers between devices  16 us (2%)
  between operations  14.5 us (2%)
    all_to_all x1, waiting for transfers between devices, local(): lax.all_to_all(slot_grad, 'table', split_axis=1, concat_axis=1, tiled=True)  234 us
    all_to_all x1, waiting for transfers between devices, local(): lax.all_to_all(found_rows, 'table', split_axis=1, concat_axis=1, tiled=True)  115 us
    gather x2, local copies, waits for them, and re-layouts, local(): pick_score = jnp.take_along_axis(score_table, slot_of_pick, axis=1)  65.1 us
    unnamed x4, other arithmetic  56.8 us
    scatter-add x1, other arithmetic, sum_rows(): total = jnp.zeros((row_count, width_here), jnp.float32).at[target].add(gr...  27.9 us
    all_to_all x1, blocking collectives, local(): lax.all_to_all(requests, 'table', split_axis=1, concat_axis=1, tiled=True)  20.2 us
    reshape x1, local copies, waits for them, and re-layouts, local(): slot_grad = slot_grad.reshape(capacity, table_size, model_width)  18.7 us
    all_to_all x1, local copies, waits for them, and re-layouts, local(): lax.all_to_all(slot_grad, 'table', split_axis=1, concat_axis=1, tiled=True)  17.7 us
  transfers between devices with their start and end apart: 3, of which 3 were waited for; matrix products, arithmetic and copies ran while one was open for 3% of the time, Pallas kernels for 0%

commit v1 on v0

v1 whole, which is shorter than its diff:
```python
import functools

import jax
import jax.numpy as jnp
from jax import lax
from jax.experimental import pallas as pl
from jax.experimental.pallas import tpu as pltpu
from jax.sharding import PartitionSpec as P

learn_rate = 0.001
LANES = 128
COLS = 512
RING = 4
CAPACITY = 16
CUBE = 8
BITS = (4, 2, 1)
ORDERS = ((0, 1, 2), (1, 2, 0), (2, 0, 1))
VMEM_BYTES = 60 * 1024 * 1024


WIDTH = 4096
CHUNK = 768
ROW_BLOCK = LANES


def chunk_width(chunk, total):
    return min(CHUNK, total - chunk * CHUNK)


def slot_place(owner, shift):
    spot = (owner // RING**2, owner // RING % RING, owner % RING)
    places = []
    for core in range(2):
        shifted = [(one + core) % RING for one in spot]
        cube = sum(bit * (one // 2) for bit, one in zip(BITS, shifted))
        chip = sum(bit * (one % 2) for bit, one in zip(BITS, shifted))
        places.append((cube, chip))
    (cube_0, chip_0), (cube_1, chip_1) = places
    cube = cube_0 + shift * (cube_1 - cube_0)
    chip = chip_0 + shift * (chip_1 - chip_0)
    return cube, chip


def pack_kernel(logit_ref, slot_ref, packed_ref, weight_ref):
    tokens, picks = logit_ref.shape
    slot_count = packed_ref.shape[1]
    logits = logit_ref[...]
    raised = jnp.exp(logits - jnp.max(logits, axis=-1, keepdims=True))
    weight_ref[...] = raised / jnp.sum(raised, axis=-1, keepdims=True)
    rows = 16

    @pl.loop(0, tokens // rows)
    def _(step):
        here = pl.ds(pl.multiple_of(step * rows, rows), rows)
        weight = weight_ref[here, :]
        slot = slot_ref[here, :]
        lane = lax.broadcasted_iota(jnp.int32, (rows, slot_count), 1)
        total = jnp.zeros((rows, slot_count), jnp.float32)
        for k in range(picks):
            total = jnp.where(lane == slot[:, k : k + 1], weight[:, k : k + 1], total)
        packed_ref[here, :] = total.astype(jnp.bfloat16)


def pack_call(logits, slot, slot_count):
    tokens, picks = logits.shape
    return pl.pallas_call(
        pack_kernel,
        out_shape=[
            jax.ShapeDtypeStruct((tokens, slot_count), jnp.bfloat16),
            jax.ShapeDtypeStruct((tokens, picks), jnp.float32),
        ],
        compiler_params=pltpu.CompilerParams(vmem_limit_bytes=VMEM_BYTES),
        cost_estimate=pl.CostEstimate(
            flops=2**25, bytes_accessed=2**20, transcendentals=tokens * picks
        ),
        name="pack_weights",
    )(logits, slot)


def gated_kernel(core_ref, gate_a, grad_a, gate_b, grad_b, mine_ref, theirs_ref):
    for gate_ref, grad_ref, out_ref in ((gate_a, grad_a, mine_ref), (gate_b, grad_b, theirs_ref)):
        gate = gate_ref[...].astype(jnp.float32)
        silu = gate * jax.nn.sigmoid(gate)
        out_ref[...] = (grad_ref[...].astype(jnp.float32) * silu).astype(jnp.bfloat16)


def gated_call(core, gate, grad):
    tokens, width = gate.shape
    steps = width // 2 // COLS
    mine = pl.BlockSpec((tokens, COLS), lambda i, core: (0, core[0] * steps + i))
    theirs = pl.BlockSpec((tokens, COLS), lambda i, core: (0, (1 - core[0]) * steps + i))
    half = pl.BlockSpec((tokens, COLS), lambda i, core: (0, i))
    return pl.pallas_call(
        gated_kernel,
        grid_spec=pltpu.PrefetchScalarGridSpec(
            num_scalar_prefetch=1,
            grid=(steps,),
            in_specs=[mine, mine, theirs, theirs],
            out_specs=[half, half],
        ),
        out_shape=[jax.ShapeDtypeStruct((tokens, width // 2), jnp.bfloat16)] * 2,
        compiler_params=pltpu.CompilerParams(vmem_limit_bytes=VMEM_BYTES),
        cost_estimate=pl.CostEstimate(
            flops=4 * tokens * width, bytes_accessed=6 * tokens * width, transcendentals=tokens * width
        ),
        name="gated_halves",
    )(core, gate, grad, gate, grad)


def slot_grad_kernel(
    core_ref, list_ref, packed_ref, packed_other_ref, gated_ref, gated_other_ref, slot_grad_ref
):
    owners = packed_ref.shape[1] // CAPACITY
    groups = ((packed_ref, gated_ref), (packed_other_ref, gated_other_ref))
    for group, (weights, gated) in enumerate(groups):
        found = lax.dot_general(
            weights[...], gated[...], (((0,), (0,)), ((), ())), preferred_element_type=jnp.float32
        ).astype(jnp.bfloat16)
        for owner in range(owners):
            cube, chip = slot_place(owner, core_ref[0])
            start = (cube * 2 + group) * ROW_BLOCK + chip * CAPACITY
            slot_grad_ref[pl.ds(pl.multiple_of(start, CAPACITY), CAPACITY), :] = found[
                owner * CAPACITY : (owner + 1) * CAPACITY, :
            ]

    @pl.when(pl.program_id(0) == pl.num_programs(0) - 1)
    def _():
        ones = jnp.ones((LANES, LANES), jnp.bfloat16)
        row = lax.broadcasted_iota(jnp.int32, (LANES, LANES), 0)
        lane = lax.broadcasted_iota(jnp.int32, (LANES, LANES), 1)
        start = WIDTH // 2 - (len(ORDERS) - 1) * CHUNK
        for block in range(list_ref.shape[0]):
            diagonal = jnp.where(row == lane, list_ref[block : block + 1, :], 0.0)
            slot_grad_ref[block * LANES : (block + 1) * LANES, start : start + LANES] = jnp.dot(
                diagonal.astype(jnp.bfloat16), ones, preferred_element_type=jnp.float32
            ).astype(jnp.bfloat16)


def slot_grad_call(core, lists, packed, packed_other, gated, gated_other):
    tokens, half = gated.shape
    slot_count = packed.shape[1]
    whole = lambda i: (0, 0)
    by_cols = lambda i: (0, i)
    weights = pl.BlockSpec((tokens, slot_count), whole)
    columns = pl.BlockSpec((tokens, CHUNK), by_cols)
    return pl.pallas_call(
        slot_grad_kernel,
        grid=(len(ORDERS),),
        in_specs=[
            pl.BlockSpec(memory_space=pltpu.SMEM),
            pl.BlockSpec(lists.shape, whole),
            weights, weights, columns, columns,
        ],
        out_specs=pl.BlockSpec((2 * slot_count, CHUNK), by_cols),
        out_shape=jax.ShapeDtypeStruct((2 * slot_count, half + LANES), jnp.bfloat16),
        compiler_params=pltpu.CompilerParams(vmem_limit_bytes=VMEM_BYTES),
        cost_estimate=pl.CostEstimate(
            flops=4 * tokens * slot_count * half, bytes_accessed=14 * 2**20, transcendentals=0
        ),
        name="slot_gradients",
    )(core, lists, packed, packed_other, gated, gated_other)


def relative(order, position):
    return sum(BITS[axis] for bit, axis in enumerate(order) if position >> bit & 1)


def asked_at(owner, peer, group):
    start = (peer * 2 + group) * ROW_BLOCK + owner * CAPACITY
    return pl.ds(pl.multiple_of(start, CAPACITY), CAPACITY)


def asked_rows(ref, owner, groups):
    return jnp.concatenate(
        [ref[asked_at(owner, peer, group), :] for peer in range(CUBE) for group in groups], axis=0
    )


def chosen_rows(id_ref, owner, groups):
    ids = asked_rows(id_ref, owner, groups)
    lane = lax.broadcasted_iota(jnp.int32, ids.shape, 1)
    return (ids.astype(jnp.float32) == lane.astype(jnp.float32)).astype(jnp.bfloat16)


def select_kernel(group, spot_ref, id_ref, *refs):
    out_ref = refs[-1]
    for chunk, order in enumerate(ORDERS):
        near, far = refs[2 * chunk], refs[2 * chunk + 1]
        rows = near.shape[0] * 2 // CUBE

        @pl.when(pl.program_id(0) == chunk)
        def _(order=order, near=near, far=far, rows=rows):
            for position in range(CUBE):
                source = near if position < CUBE // 2 else far
                start = position % (CUBE // 2) * rows
                owner = spot_ref[0] ^ relative(order, position)
                found = jnp.dot(
                    chosen_rows(id_ref, owner, (group,)),
                    source[start : start + rows, :],
                    preferred_element_type=jnp.float32,
                ).astype(jnp.bfloat16)
                for peer in range(CUBE):
                    at = pl.ds(
                        pl.multiple_of(peer * ROW_BLOCK + owner * CAPACITY, CAPACITY), CAPACITY
                    )
                    out_ref[at, : found.shape[1]] = found[peer * CAPACITY : (peer + 1) * CAPACITY, :]


def select_call(group, spot, arrived, parts):
    rows, wide = arrived.shape
    whole = lambda i: (0, 0)
    return pl.pallas_call(
        functools.partial(select_kernel, group),
        grid=(len(ORDERS),),
        in_specs=[
            pl.BlockSpec(memory_space=pltpu.SMEM),
            pl.BlockSpec((rows, LANES), lambda i: (0, wide // LANES - 1)),
        ]
        + [pl.BlockSpec(part.shape, whole) for part in parts],
        out_specs=pl.BlockSpec((rows // 2, CHUNK), lambda i: (0, i)),
        out_shape=jax.ShapeDtypeStruct((rows // 2, wide - LANES), jnp.bfloat16),
        compiler_params=pltpu.CompilerParams(vmem_limit_bytes=VMEM_BYTES),
        cost_estimate=pl.CostEstimate(
            flops=rows * LANES * wide, bytes_accessed=3 * rows * wide, transcendentals=0
        ),
        name="select_rows",
    )(spot, arrived, *parts)


def partial_kernel(chunk, spot_ref, id_ref, arrived_ref, keep_ref, send_ref):
    rows = keep_ref.shape[0] * 2 // CUBE
    cols = keep_ref.shape[1]
    for position in range(CUBE):
        owner = spot_ref[0] ^ relative(ORDERS[chunk], position)
        chosen = chosen_rows(id_ref, owner, (0, 1))
        by_rows = (((0,), (0,)), ((), ()))
        total = lax.dot_general(
            chosen, asked_rows(arrived_ref, owner, (0, 1))[:, :cols], by_rows,
            preferred_element_type=jnp.float32,
        )
        target = keep_ref if position < CUBE // 2 else send_ref
        start = position % (CUBE // 2) * rows
        target[start : start + rows, :] = total.astype(target.dtype)
        if chunk == len(ORDERS) - 1:
            hits = lax.dot_general(
                chosen, jnp.ones(chosen.shape, jnp.bfloat16), by_rows, preferred_element_type=jnp.float32
            )
            target[start : start + rows, cols - LANES :] = hits.astype(target.dtype)


def partial_call(chunk, spot, arrived, row_count):
    rows, wide = arrived.shape
    cols = chunk_width(chunk, wide)
    half = CUBE // 2 * row_count
    whole = lambda i: (0, 0)
    return pl.pallas_call(
        functools.partial(partial_kernel, chunk),
        grid=(1,),
        in_specs=[
            pl.BlockSpec(memory_space=pltpu.SMEM),
            pl.BlockSpec((rows, LANES), lambda i: (0, wide // LANES - 1)),
            pl.BlockSpec((rows, CHUNK), lambda i: (0, chunk)),
        ],
        out_specs=[pl.BlockSpec((half, cols), whole)] * 2,
        out_shape=[
            jax.ShapeDtypeStruct((half, cols), jnp.float32),
            jax.ShapeDtypeStruct((half, cols), jnp.bfloat16),
        ],
        compiler_params=pltpu.CompilerParams(vmem_limit_bytes=VMEM_BYTES),
        cost_estimate=pl.CostEstimate(
            flops=2 * rows * LANES * cols, bytes_accessed=8 * rows * cols, transcendentals=0
        ),
        name="partial_sums",
    )(spot, arrived, arrived)


def adam_kernel(
    core_ref, hits_ref, own_ref, other_ref, value_ref, first_ref, second_ref,
    value_out, first_out, second_out,
):
    touched = hits_ref[...][:, :1] > 0.0
    own = pl.program_id(0) < pl.num_programs(0) // 2
    row_grad = jnp.where(own, own_ref[...], other_ref[...])
    first = first_ref[...]
    second = second_ref[...]
    value = value_ref[...].astype(jnp.float32)
    first_new = 0.9 * first + 0.1 * row_grad
    second_new = 0.95 * second + 0.05 * row_grad * row_grad
    value_new = value - learn_rate * first_new / (jnp.sqrt(second_new) + 1e-08)
    value_out[...] = jnp.where(touched, value_new, value).astype(jnp.bfloat16)
    first_out[...] = jnp.where(touched, first_new, first)
    second_out[...] = jnp.where(touched, second_new, second)


def adam_call(core, own, other, values, first, second):
    rows, width = values.shape
    steps = width // 2 // COLS
    columns = pl.BlockSpec(
        (rows, COLS),
        lambda i, core: (0, lax.rem(core[0] + i // steps, 2) * steps + lax.rem(i, steps)),
    )
    return pl.pallas_call(
        adam_kernel,
        grid_spec=pltpu.PrefetchScalarGridSpec(
            num_scalar_prefetch=1,
            grid=(2 * steps,),
            in_specs=[
                pl.BlockSpec((rows, LANES), lambda i, core: (0, width // 2 // LANES)),
                pl.BlockSpec((rows, COLS), lambda i, core: (0, jnp.minimum(i, steps - 1))),
                pl.BlockSpec((rows, COLS), lambda i, core: (0, jnp.maximum(i - steps, 0))),
                columns, columns, columns,
            ],
            out_specs=[columns] * 3,
        ),
        out_shape=[
            jax.ShapeDtypeStruct(values.shape, values.dtype),
            jax.ShapeDtypeStruct(first.shape, first.dtype),
            jax.ShapeDtypeStruct(second.shape, second.dtype),
        ],
        compiler_params=pltpu.CompilerParams(vmem_limit_bytes=VMEM_BYTES),
        cost_estimate=pl.CostEstimate(
            flops=10 * rows * width, bytes_accessed=28 * rows * width, transcendentals=rows * width
        ),
        name="adam_rows",
    )(core, own, own, other, values, first, second)


def read_kernel(own, core_ref, packed_ref, fetched_ref, gate_ref, grad_ref, *refs):
    if own:
        weight_ref, slot_ref, before_ref, _, _, out_ref, gate_grad_ref, logit_grad_ref = refs[:8]
    else:
        out_ref, gate_grad_ref, score_out_ref = refs[:3]
    ordered_ref, score_ref = refs[-2:]
    step = pl.program_id(0)
    shift = core_ref[0] if own else 1 - core_ref[0]
    for owner in range(ordered_ref.shape[0] // CAPACITY):
        cube, chip = slot_place(owner, shift)
        at = pl.ds(pl.multiple_of(cube * ROW_BLOCK + chip * CAPACITY, CAPACITY), CAPACITY)
        ordered_ref[owner * CAPACITY : (owner + 1) * CAPACITY, :] = fetched_ref[at, :]
    fetched = ordered_ref[...]
    memory = jnp.dot(packed_ref[...], fetched, preferred_element_type=jnp.float32)
    gate = gate_ref[...].astype(jnp.float32)
    sig = jax.nn.sigmoid(gate)
    silu = gate * sig
    grad = grad_ref[...].astype(jnp.float32)
    out_ref[...] = (silu * memory).astype(jnp.bfloat16)
    gated = (grad * silu).astype(jnp.bfloat16)
    gate_grad_ref[...] = (grad * memory * sig * (1.0 + gate * (1.0 - sig))).astype(jnp.bfloat16)
    score = lax.dot_general(
        gated, fetched, (((1,), (1,)), ((), ())), preferred_element_type=jnp.float32
    )

    @pl.when(step == 0)
    def _():
        score_ref[...] = score + before_ref[...] if own else score

    @pl.when(step > 0)
    def _():
        score_ref[...] += score

    @pl.when(step == pl.num_programs(0) - 1)
    def _():
        if not own:
            score_out_ref[...] = score_ref[...]
            return
        picks = weight_ref.shape[1]
        slot = slot_ref[...]
        low = lax.rem(slot, LANES)
        high = slot // LANES
        wide = jnp.zeros(slot.shape, jnp.float32)
        for part in range(score_ref.shape[1] // LANES):
            here = score_ref[:, part * LANES : (part + 1) * LANES]
            wide = jnp.where(high == part, jnp.take_along_axis(here, low, axis=1), wide)
        pick_score = wide[:, :picks]
        weight = weight_ref[...]
        mean_score = jnp.sum(weight * pick_score, axis=-1, keepdims=True)
        wide = jnp.pad(weight * (pick_score - mean_score), ((0, 0), (0, LANES - picks)))
        logit_grad_ref[...] = wide.T[:picks, :]


def read_call(core, packed, fetched, gate, grad, last=None):
    tokens, width = gate.shape
    slot_count = packed.shape[1]
    steps = width // 2 // COLS
    own = last is not None
    whole = lambda i, core: (0, 0)

    def by_cols(i, core):
        half = core[0] if own else 1 - core[0]
        return (0, half * steps + i)

    columns = pl.BlockSpec((tokens, COLS), by_cols)
    in_specs = [
        pl.BlockSpec((tokens, slot_count), whole),
        pl.BlockSpec((slot_count, COLS), lambda i, core: (0, i)),
        columns,
        columns,
    ]
    out_specs = [columns, columns]
    out_shape = [jax.ShapeDtypeStruct((tokens, width), jnp.bfloat16)] * 2
    args = [packed, fetched, gate, grad]
    aliases = {}
    if own:
        weight, slot, layer_out, gate_grad, score = last
        picks = weight.shape[1]
        slot = jnp.pad(slot, ((0, 0), (0, LANES - picks)))
        args += [weight, slot, score, layer_out, gate_grad]
        in_specs += [pl.BlockSpec(one.shape, whole) for one in (weight, slot, score)]
        in_specs += [pl.BlockSpec(memory_space=pl.ANY)] * 2
        out_specs.append(pl.BlockSpec((picks, tokens), whole))
        out_shape.append(jax.ShapeDtypeStruct((picks, tokens), jnp.float32))
        aliases = {8: 0, 9: 1}
    else:
        out_specs.append(pl.BlockSpec((tokens, slot_count), whole))
        out_shape.append(jax.ShapeDtypeStruct((tokens, slot_count), jnp.float32))
    return pl.pallas_call(
        functools.partial(read_kernel, own),
        grid_spec=pltpu.PrefetchScalarGridSpec(
            num_scalar_prefetch=1,
            grid=(steps,),
            in_specs=in_specs,
            out_specs=out_specs,
            scratch_shapes=[
                pltpu.VMEM((slot_count, COLS), jnp.bfloat16),
                pltpu.VMEM((tokens, slot_count), jnp.float32),
            ],
        ),
        out_shape=out_shape,
        input_output_aliases=aliases,
        compiler_params=pltpu.CompilerParams(vmem_limit_bytes=VMEM_BYTES),
        cost_estimate=pl.CostEstimate(
            flops=2 * tokens * slot_count * width, bytes_accessed=9 * 2**20, transcendentals=tokens * width // 2
        ),
        name="read_and_scores",
    )(core, *args)


def place_of(core, shifted):
    spot = [(one - core) % RING for one in shifted]
    return (spot[0] * RING + spot[1]) * RING + spot[2]


def shifted_of(core, index):
    return [(one + core) % RING for one in (index // RING**2, index // RING % RING, index % RING)]


def swap(x, axis):
    pairs = []
    for core in range(2):
        for index in range(RING**3):
            shifted = shifted_of(core, index)
            shifted[axis] ^= 1
            pairs.append((core * RING**3 + index, core * RING**3 + place_of(core, shifted)))
    return lax.ppermute(x, ("batch", "table"), pairs)


def swap_cores(x):
    return lax.ppermute(x, "batch", [(0, 1), (1, 0)])


def cube_exchange(x):
    groups = []
    for core in range(2):
        found = {}
        for index in range(RING**3):
            shifted = shifted_of(core, index)
            group = tuple((one + 1) % RING // 2 for one in shifted)
            order = sum(bit * (one // 2) for bit, one in zip(BITS, shifted))
            found.setdefault(group, {})[order] = core * RING**3 + index
        groups += [[members[n] for n in range(CUBE)] for _, members in sorted(found.items())]
    return lax.all_to_all(
        x, ("batch", "table"), split_axis=0, concat_axis=0, axis_index_groups=groups, tiled=True
    )


def after(first, then):
    count = len(first)
    return lax.optimization_barrier((*first, *then))[count:]


def local(
    gate_pre, pick_logits, requests, slot_of_pick, values, first_moment, second_moment, out_grad
):
    capacity, table_size = requests.shape
    slot_count = capacity * table_size
    row_count, width = values.shape
    half_width = width // 2
    core = lax.axis_index("batch")
    shifted = shifted_of(core, lax.axis_index("table"))
    inside = sum(bit * (one % 2) for bit, one in zip(BITS, shifted))
    spot = inside.astype(jnp.int32).reshape(1)
    which = core.astype(jnp.int32).reshape(1)

    mine = lax.dynamic_slice(values, (0, core * half_width), (row_count, half_width))
    parts = [mine[:, chunk * CHUNK : (chunk + 1) * CHUNK] for chunk in range(len(ORDERS))]
    swapped = [swap(part, order[0]) for part, order in zip(parts, ORDERS)]

    lists = jnp.stack([requests, swap_cores(requests)]).reshape(2, capacity, RING, RING, RING)
    for axis in range(2, 5):
        turned = jnp.concatenate(
            [lax.slice_in_dim(lists, RING - 1, RING, axis=axis), lax.slice_in_dim(lists, 0, RING - 1, axis=axis)],
            axis=axis,
        )
        lists = jnp.where(core == 0, lists, turned)
    lists = lists.reshape(2, capacity, 2, 2, 2, 2, 2, 2).transpose(2, 4, 6, 0, 3, 5, 7, 1)
    lists = lists.reshape(2 * CUBE, ROW_BLOCK).astype(jnp.float32)

    gated, gated_theirs = gated_call(which, gate_pre, out_grad)
    gated_other = swap_cores(gated_theirs)
    swapped = after([gated], swapped)
    parts = [jnp.concatenate(pair, axis=0) for pair in zip(parts, swapped)]
    swapped = [swap(part, order[1]) for part, order in zip(parts, ORDERS)]
    slot = (slot_of_pick % table_size) * capacity + slot_of_pick // table_size
    (slot,) = after(parts, [slot])
    packed, weight = pack_call(pick_logits, slot, slot_count)
    packed_other = swap_cores(packed)
    slot_grad = slot_grad_call(which, lists, packed, packed_other, gated, gated_other)
    swapped = after([slot_grad], swapped)
    (slot_grad,) = after(swapped, [slot_grad])
    arrived = cube_exchange(slot_grad)
    parts = [jnp.concatenate(pair, axis=0) for pair in zip(parts, swapped)]
    swapped = [swap(part, order[2]) for part, order in zip(parts, ORDERS)]
    gathered = [half for pair in zip(parts, swapped) for half in pair]
    (arrived,) = after(swapped, [arrived])

    found_other = select_call(1, spot, arrived, gathered)
    fetched_theirs = cube_exchange(found_other)
    (arrived,) = after([found_other], [arrived])
    found = select_call(0, spot, arrived, gathered)
    (arrived,) = after([found], [arrived])
    halves = [partial_call(chunk, spot, arrived, row_count) for chunk in range(len(ORDERS))]
    (fetched_theirs,) = after([keep for keep, _ in halves], [fetched_theirs])
    (found,) = after([fetched_theirs], [found])
    fetched = cube_exchange(found)
    fetched_other = swap_cores(fetched_theirs)

    received = [swap(send, order[2]) for (_, send), order in zip(halves, ORDERS)]
    half = CUBE // 4 * row_count
    for step in (1, 0):
        totals = [keep + other.astype(jnp.float32) for (keep, _), other in zip(halves, received)]
        halves = [(total[:half], total[half:].astype(jnp.bfloat16)) for total in totals]
        received = [swap(send, order[step]) for (_, send), order in zip(halves, ORDERS)]
        half //= 2
    (fetched_other,) = after([send for _, send in halves], [fetched_other])
    layer_out, gate_grad, score = read_call(which, packed, fetched_other, gate_pre, out_grad)
    received = after([score], received)
    totals = [keep + other.astype(jnp.float32) for (keep, _), other in zip(halves, received)]
    own = jnp.concatenate(totals, axis=1)
    value_next, first_next, second_next = adam_call(
        which, own, swap_cores(own), values, first_moment, second_moment
    )
    (fetched,) = after([value_next], [fetched])
    layer_out, gate_grad, logit_grad = read_call(
        which, packed, fetched, gate_pre, out_grad, (weight, slot, layer_out, gate_grad, score)
    )
    return (layer_out, gate_grad, logit_grad.T, value_next, first_next, second_next)


def solution(mesh):
    tokens = P(("batch", "table"), None)
    rows = P("table", None)
    return jax.shard_map(
        local,
        mesh=mesh,
        in_specs=(tokens, tokens, tokens, tokens, rows, rows, rows, tokens),
        out_specs=(tokens, tokens, tokens, rows, rows, rows),
        check_vma=False,
    )
```

time: 697 us -> 231 us (0.33)
  waiting for transfers between devices: 363 us -> 98.8 us
  local copies, waits for them, and re-layouts: 132 us -> 8.84 us
  other arithmetic: 117 us -> 8.87 us
  Pallas kernels: 0 us -> 64 us
  starting transfers between devices: 16 us -> 48.2 us
  blocking collectives: 29.1 us -> 0 us
  matrix products: 22.2 us -> 0 us
  between operations: 14.5 us -> 1.2 us
    all_to_all x2 -> x3, waiting for transfers between devices: 349 us -> 20.8 us  [cube_exchange(): lax.all_to_all(x, ('batch', 'table'), split_axis=0, concat_axis=0, axis_i...]
    gather x3 -> x0, local copies, waits for them, and re-layouts: 81.7 us -> none  [the longest x2 65.1 us: local(): pick_score = jnp.take_along_axis(score_table, slot_of_pick, axis=1)]
    ppermute x0 -> x23, waiting for transfers between devices: none -> 78 us  [the longest x18 76.7 us: swap(): return lax.ppermute(x, ('batch', 'table'), pairs)]
    pallas_call x0 -> x11, Pallas kernels: none -> 64 us  [the longest x2 15.8 us: read_call(): pl.pallas_call(functools.partial(read_kernel, own), grid_spec=pltpu.Prefe...]
    unnamed x4 -> x0, other arithmetic: 56.8 us -> none
    scatter-add x2 -> x0, other arithmetic: 35.5 us -> none  [the longest x1 27.9 us: sum_rows(): total = jnp.zeros((row_count, width_here), jnp.float32).at[target].add(gr...]
    ppermute x0 -> x23, starting transfers between devices: none -> 33.9 us  [the longest x18 27.3 us: swap(): return lax.ppermute(x, ('batch', 'table'), pairs)]
    all_to_all x4 -> x0, local copies, waits for them, and re-layouts: 29.1 us -> none  [the longest x1 17.7 us: local(): lax.all_to_all(slot_grad, 'table', split_axis=1, concat_axis=1, tiled=True)]
  transfers between devices with their start and end apart: 3 -> 26, of which waited for: 3 -> 8; matrix products, arithmetic and copies ran while one was open for 3% -> 6% of each run, Pallas kernels for 0% -> 22%
where the time goes in v1:
time: 231 us; the launch traced here: 230 us
  waiting for transfers between devices  98.8 us (43%)
  Pallas kernels  64 us (28%)
  starting transfers between devices  48.2 us (21%)
  other arithmetic  8.87 us (4%)
  local copies, waits for them, and re-layouts  8.84 us (4%)
    ppermute x18, waiting for transfers between devices, swap(): return lax.ppermute(x, ('batch', 'table'), pairs)  76.7 us
    ppermute x18, starting transfers between devices, swap(): return lax.ppermute(x, ('batch', 'table'), pairs)  27.3 us
    all_to_all x3, waiting for transfers between devices, cube_exchange(): lax.all_to_all(x, ('batch', 'table'), split_axis=0, concat_axis=0, axis_i...  20.8 us
    pallas_call x2, Pallas kernels, read_call(): pl.pallas_call(functools.partial(read_kernel, own), grid_spec=pltpu.Prefe...  15.8 us
    all_to_all x3, starting transfers between devices, cube_exchange(): lax.all_to_all(x, ('batch', 'table'), split_axis=0, concat_axis=0, axis_i...  14.3 us
    pallas_call x3, Pallas kernels, partial_call(): pl.pallas_call(functools.partial(partial_kernel, chunk), grid=(1,), in_sp...  11.7 us
    pallas_call x2, Pallas kernels, select_call(): pl.pallas_call(functools.partial(select_kernel, group), grid=(len(ORDERS)...  11.3 us
    pallas_call x1, Pallas kernels, adam_call(): pl.pallas_call(adam_kernel, grid_spec=pltpu.PrefetchScalarGridSpec(num_sc...  8.04 us
  transfers between devices with their start and end apart: 26, of which 8 were waited for; matrix products, arithmetic and copies ran while one was open for 6% of the time, Pallas kernels for 22%

profile of v1, /device:TPU:1, one launch (start us, length us, event | category | flops | bytes accessed | tf_op | source)
XLA Modules:
  0.0 229.9 jit_solution(984157642415817768)
XLA Ops:
  3.9 2.9 %collective-permute-start = (bf16[128,768]{1,0:T(8,128)(2,1)S(1)}, bf16[128,768]{1,0:T(8,128)(2,1)S(1)}, u32[]{:S(2)}, u32[]{:S(2)}) collective-permute-start(bf16[128,768]{1,0:T(8,128)(2,1)S(1)} %get-tuple-element.81), channel_id=1, source_target_pairs={{0,16},{1,17},{2,18},{3,19},{4,20},{5,21},{6,22},{7,23},{8,24},{9,... | collective-permute-start | bytes 589832 | tf_op jit(solution)/shard_map/ppermute | solution.py:454
  10.2 3.8 %collective-permute-start.2 = (bf16[128,512]{1,0:T(8,128)(2,1)S(1)}, bf16[128,512]{1,0:T(8,128)(2,1)S(1)}, u32[]{:S(2)}, u32[]{:S(2)}) collective-permute-start(bf16[128,512]{1,0:T(8,128)(2,1)S(1)} %constant_dynamic-slice_fusion.2), channel_id=1, source_target_pairs={{0,1},{1,0},{2,3},{3,2},{4,5},{5,4},{6,7},{7,6},{8,9},{9,8},{10,11... | collective-permute-start | bytes 393224 | tf_op jit(solution)/shard_map/ppermute | solution.py:454
  14.1 4.4 %gated_halves.1 = (bf16[256,2048]{1,0:T(8,128)(2,1)}, bf16[256,2048]{1,0:T(8,128)(2,1)}) custom-call(s32[1]{0:T(128)} %bitcast.core_ref, bf16[256,4096]{1,0:T(8,128)(2,1)} %gate_ref.3, bf16[256,4096]{1,0:T(8,128)(2,1)} %grad_ref.3, bf16[256,4096]{1,0:T(8,128)(2,1)} %gate_ref.3, bf16[256,4096]{1,0:T(8,128)(2,1)} %grad_ref.3), custom_call_target="tpu_custom_call" | custom-call | flops 4194304 | bytes 6291456 | tf_op jit(solution)/shard_map/gated_halves/pallas_call | solution.py:93
  22.5 5.7 %pack_weights.1 = (bf16[256,1024]{1,0:T(8,128)(2,1)}, f32[256,32]{1,0:T(8,128)}) custom-call(f32[256,32]{1,0:T(8,128)} %copy.27.logit_ref, s32[256,32]{1,0:T(8,128)} %fusion.1.slot_ref), custom_call_target="tpu_custom_call" | custom-call | flops 33554432 | bytes 1048576 | tf_op jit(solution)/shard_map/pack_weights/pallas_call | solution.py:66
  33.0 7.2 %slot_gradients.1 = bf16[2048,2176]{1,0:T(8,128)(2,1)} custom-call(s32[1]{0:T(128)} %bitcast.core_ref, f32[16,128]{1,0:T(8,128)} %convert_element_type.42.list_ref, bf16[256,1024]{1,0:T(8,128)(2,1)} %get-tuple-element.48.packed_ref, bf16[256,1024]{1,0:T(8,128)(2,1)} %copy-done.12, bf16[256,2048]{1,0:T(8,128)(2,1)} %get-tuple-element.43.gated_ref, ...), custom_call_target="tpu_custom_call" | custom-call | flops 2147483648 | bytes 14680064 | tf_op jit(solution)/shard_map/slot_gradients/pallas_call | solution.py:146
  40.2 5.0 %all-to-all-start = ((bf16[8,256,2176]{2,1,0:T(8,128)(2,1)}), bf16[8,256,2176]{2,1,0:T(8,128)(2,1)}, u32[]{:S(2)}, u32[]{:S(2)}) async-start(bf16[8,256,2176]{2,1,0:T(8,128)(2,1)} %bitcast.19), calls=%async_computation | async-start | bytes 17825792 | tf_op jit(solution)/shard_map/all_to_all | solution.py:471
  48.2 2.6 %collective-permute-start.9 = (bf16[512,768]{1,0:T(8,128)(2,1)S(1)}, bf16[512,768]{1,0:T(8,128)(2,1)}, u32[]{:S(2)}, u32[]{:S(2)}) collective-permute-start(bf16[512,768]{1,0:T(8,128)(2,1)S(1)} %pad_maximum_fusion.1.refs_0_), channel_id=1, source_target_pairs={{0,1},{1,0},{2,3},{3,2},{4,5},{5,4},{6,7},{7,6},{8,9},{9,8},{10,11... | collective-permute-start | bytes 2359304 | tf_op jit(solution)/shard_map/ppermute | solution.py:454
  54.4 12.9 %collective-permute-done.11.refs_5_ = bf16[512,512]{1,0:T(8,128)(2,1)S(1)} collective-permute-done((bf16[512,512]{1,0:T(8,128)(2,1)S(1)}, bf16[512,512]{1,0:T(8,128)(2,1)S(1)}, u32[]{:S(2)}, u32[]{:S(2)}) %collective-permute-start.11) | collective-permute-done | bytes 524320 | tf_op jit(solution)/shard_map/ppermute | solution.py:454
  67.6 34.6 %collective-permute-done.9.refs_1_ = bf16[512,768]{1,0:T(8,128)(2,1)} collective-permute-done((bf16[512,768]{1,0:T(8,128)(2,1)S(1)}, bf16[512,768]{1,0:T(8,128)(2,1)}, u32[]{:S(2)}, u32[]{:S(2)}) %collective-permute-start.9) | collective-permute-done | bytes 786464 | tf_op jit(solution)/shard_map/ppermute | solution.py:454
  102.2 7.1 %all-to-all-done = bf16[8,256,2176]{2,1,0:T(8,128)(2,1)} async-done(((bf16[8,256,2176]{2,1,0:T(8,128)(2,1)}), bf16[8,256,2176]{2,1,0:T(8,128)(2,1)}, u32[]{:S(2)}, u32[]{:S(2)}) %all-to-all-start) | async-done | bytes 8912928 | tf_op jit(solution)/shard_map/all_to_all | solution.py:471
  109.3 5.6 %select_rows.2 = bf16[1024,2048]{1,0:T(8,128)(2,1)} custom-call(s32[1]{0:T(128)} %bitcast.1.spot_ref, bf16[2048,2176]{1,0:T(8,128)(2,1)} %bitcast.11.id_ref.arrived_ref, bf16[512,768]{1,0:T(8,128)(2,1)} %copy-done.2, bf16[512,768]{1,0:T(8,128)(2,1)} %collective-permute-done.9.refs_1_, bf16[512,768]{1,0:T(8,128)(2,1)} %copy-done.1, ...), custom_call_target="tpu_custom_call" | custom-call | flops 570425344 | bytes 13369344 | tf_op jit(solution)/shard_map/select_rows/pallas_call | solution.py:212
  115.0 4.6 %all-to-all-start.1 = ((bf16[8,128,2048]{2,1,0:T(8,128)(2,1)}), bf16[8,128,2048]{2,1,0:T(8,128)(2,1)}, u32[]{:S(2)}, u32[]{:S(2)}) async-start(bf16[8,128,2048]{2,1,0:T(8,128)(2,1)} %bitcast.21), calls=%async_computation.1 | async-start | bytes 8388608 | tf_op jit(solution)/shard_map/all_to_all | solution.py:471
  119.5 5.6 %select_rows.3 = bf16[1024,2048]{1,0:T(8,128)(2,1)} custom-call(s32[1]{0:T(128)} %bitcast.1.spot_ref, bf16[2048,2176]{1,0:T(8,128)(2,1)} %bitcast.11.id_ref.arrived_ref, bf16[512,768]{1,0:T(8,128)(2,1)} %copy-done.2, bf16[512,768]{1,0:T(8,128)(2,1)} %collective-permute-done.9.refs_1_, bf16[512,768]{1,0:T(8,128)(2,1)} %copy-done.1, ...), custom_call_target="tpu_custom_call" | custom-call | flops 570425344 | bytes 13369344 | tf_op jit(solution)/shard_map/select_rows/pallas_call | solution.py:212
  125.2 3.7 %partial_sums.5 = (f32[512,640]{1,0:T(8,128)}, bf16[512,640]{1,0:T(8,128)(2,1)}) custom-call(s32[1]{0:T(128)} %bitcast.1.spot_ref, bf16[2048,2176]{1,0:T(8,128)(2,1)} %bitcast.11.id_ref.arrived_ref, bf16[2048,2176]{1,0:T(8,128)(2,1)} %bitcast.11.id_ref.arrived_ref), custom_call_target="tpu_custom_call" | custom-call | flops 335544320 | bytes 10485760 | tf_op jit(solution)/shard_map/partial_sums/pallas_call | solution.py:256
  128.9 3.9 %partial_sums.4 = (f32[512,768]{1,0:T(8,128)}, bf16[512,768]{1,0:T(8,128)(2,1)}) custom-call(s32[1]{0:T(128)} %bitcast.1.spot_ref, bf16[2048,2176]{1,0:T(8,128)(2,1)} %bitcast.11.id_ref.arrived_ref, bf16[2048,2176]{1,0:T(8,128)(2,1)} %bitcast.11.id_ref.arrived_ref), custom_call_target="tpu_custom_call" | custom-call | flops 402653184 | bytes 12582912 | tf_op jit(solution)/shard_map/partial_sums/pallas_call | solution.py:256
  132.8 4.0 %partial_sums.3 = (f32[512,768]{1,0:T(8,128)}, bf16[512,768]{1,0:T(8,128)(2,1)}) custom-call(s32[1]{0:T(128)} %bitcast.1.spot_ref, bf16[2048,2176]{1,0:T(8,128)(2,1)} %bitcast.11.id_ref.arrived_ref, bf16[2048,2176]{1,0:T(8,128)(2,1)} %bitcast.11.id_ref.arrived_ref), custom_call_target="tpu_custom_call" | custom-call | flops 402653184 | bytes 12582912 | tf_op jit(solution)/shard_map/partial_sums/pallas_call | solution.py:256
  136.9 13.7 %all-to-all-done.1 = bf16[8,128,2048]{2,1,0:T(8,128)(2,1)} async-done(((bf16[8,128,2048]{2,1,0:T(8,128)(2,1)}), bf16[8,128,2048]{2,1,0:T(8,128)(2,1)}, u32[]{:S(2)}, u32[]{:S(2)}) %all-to-all-start.1) | async-done | bytes 4194336 | tf_op jit(solution)/shard_map/all_to_all | solution.py:471
  150.5 4.5 %collective-permute-start.18 = (bf16[1024,2048]{1,0:T(8,128)(2,1)}, bf16[1024,2048]{1,0:T(8,128)(2,1)}, u32[]{:S(2)}, u32[]{:S(2)}) collective-permute-start(bf16[1024,2048]{1,0:T(8,128)(2,1)} %bitcast.13), channel_id=1, source_target_pairs={{0,64},{64,0},{1,65},{65,1},{2,66},{66,2},{3,67},{67,3},{4,68},{68... | collective-permute-start | bytes 12582920 | tf_op jit(solution)/shard_map/ppermute | solution.py:458
  157.0 8.7 %collective-permute-done.16 = bf16[512,640]{1,0:T(8,128)(2,1)S(1)} collective-permute-done((bf16[512,640]{1,0:T(8,128)(2,1)S(1)}, bf16[512,640]{1,0:T(8,128)(2,1)S(1)}, u32[]{:S(2)}, u32[]{:S(2)}) %collective-permute-start.16) | collective-permute-done | bytes 655392 | tf_op jit(solution)/shard_map/ppermute | solution.py:454
  166.3 4.7 %all-to-all-start.2 = ((bf16[8,128,2048]{2,1,0:T(8,128)(2,1)}), bf16[8,128,2048]{2,1,0:T(8,128)(2,1)}, u32[]{:S(2)}, u32[]{:S(2)}) async-start(bf16[8,128,2048]{2,1,0:T(8,128)(2,1)} %bitcast.20), calls=%async_computation.2 | async-start | bytes 8388608 | tf_op jit(solution)/shard_map/all_to_all | solution.py:471
  178.1 20.1 %collective-permute-done.15 = bf16[256,768]{1,0:T(8,128)(2,1)S(1)} collective-permute-done((bf16[256,768]{1,0:T(8,128)(2,1)S(1)}, bf16[256,768]{1,0:T(8,128)(2,1)S(1)}, u32[]{:S(2)}, u32[]{:S(2)}) %collective-permute-start.15) | collective-permute-done | bytes 393248 | tf_op jit(solution)/shard_map/ppermute | solution.py:454
  201.8 7.4 %read_and_scores.2 = (bf16[256,4096]{1,0:T(8,128)(2,1)}, bf16[256,4096]{1,0:T(8,128)(2,1)}, f32[256,1024]{1,0:T(8,128)}) custom-call(s32[1]{0:T(128)} %bitcast.core_ref, bf16[256,1024]{1,0:T(8,128)(2,1)} %get-tuple-element.48.packed_ref, bf16[1024,2048]{1,0:T(8,128)(2,1)} %collective-permute-done.18.fetched_ref, bf16[256,4096]{1,0:T(8,128)(2,1)} %gate_ref.3, ...), custom_call_target="tpu_custom_call" | custom-call | flops 2147483648 | bytes 9437184 | tf_op jit(solution)/shard_map/read_and_scores/pallas_call | solution.py:416
  213.4 8.0 %adam_rows.1 = (bf16[128,4096]{1,0:T(8,128)(2,1)}, f32[128,4096]{1,0:T(8,128)}, f32[128,4096]{1,0:T(8,128)}) custom-call(s32[1]{0:T(128)} %bitcast.core_ref, f32[128,2176]{1,0:T(8,128)} %copy-done, f32[128,2176]{1,0:T(8,128)} %copy-done, f32[128,2176]{1,0:T(8,128)} %copy-done.10, bf16[128,4096]{1,0:T(8,128)(2,1)} %value_ref.1, f32[128,4096]{1,0:T(8,128)} %first_ref.1, ...), custom_call_target="tpu_custom_call" | custom-call | flops 5242880 | bytes 14680064 | tf_op jit(solution)/shard_map/adam_rows/pallas_call | solution.py:302
  221.4 8.4 %read_and_scores.3 = (bf16[256,4096]{1,0:T(8,128)(2,1)}, bf16[256,4096]{1,0:T(8,128)(2,1)}, f32[32,256]{1,0:T(8,128)}) custom-call(s32[1]{0:T(128)} %bitcast.core_ref, bf16[256,1024]{1,0:T(8,128)(2,1)} %get-tuple-element.48.packed_ref, bf16[1024,2048]{1,0:T(8,128)(2,1)} %bitcast.15.fetched_ref, ...), custom_call_target="tpu_custom_call", output_to_operand_aliasing={{0}: (8, {}), {1}: (9, {})} | custom-call | flops 2147483648 | bytes 9437184 | tf_op jit(solution)/shard_map/read_and_scores/pallas_call | solution.py:416
  (110 shorter events, 39.6 us)
Async XLA Ops:
  1.4 18.7 %collective-permute-start.3 = (s32[16,64]{0,1:T(8,128)S(1)}, s32[16,64]{0,1:T(8,128)S(1)}, u32[]{:S(2)}, u32[]{:S(2)}) collective-permute-start(s32[16,64]{0,1:T(8,128)S(1)} %copy.28), channel_id=1, source_target_pairs={{0,64},{64,0},{1,65},{65,1},{2,66},{66,2},{3,67},{67,3},{4,68},{68... | collective-permute-start | bytes 12296 | tf_op jit(solution)/shard_map/ppermute | solution.py:458
  3.9 16.3 %collective-permute-start = (bf16[128,768]{1,0:T(8,128)(2,1)S(1)}, bf16[128,768]{1,0:T(8,128)(2,1)S(1)}, u32[]{:S(2)}, u32[]{:S(2)}) collective-permute-start(bf16[128,768]{1,0:T(8,128)(2,1)S(1)} %get-tuple-element.81), channel_id=1, source_target_pairs={{0,16},{1,17},{2,18},{3,19},{4,20},{5,21},{6,22},{7,23},{8,24},{9,... | collective-permute-start | bytes 589832 | tf_op jit(solution)/shard_map/ppermute | solution.py:454
  6.8 13.4 %collective-permute-start.1 = (bf16[128,768]{1,0:T(8,128)(2,1)S(1)}, bf16[128,768]{1,0:T(8,128)(2,1)S(1)}, u32[]{:S(2)}, u32[]{:S(2)}) collective-permute-start(bf16[128,768]{1,0:T(8,128)(2,1)S(1)} %get-tuple-element.80), channel_id=1, source_target_pairs={{0,4},{1,5},{2,6},{3,7},{4,0},{5,1},{6,2},{7,3},{8,12},{9,13},{10,... | collective-permute-start | bytes 589832 | tf_op jit(solution)/shard_map/ppermute | solution.py:454
  10.2 10.0 %collective-permute-start.2 = (bf16[128,512]{1,0:T(8,128)(2,1)S(1)}, bf16[128,512]{1,0:T(8,128)(2,1)S(1)}, u32[]{:S(2)}, u32[]{:S(2)}) collective-permute-start(bf16[128,512]{1,0:T(8,128)(2,1)S(1)} %constant_dynamic-slice_fusion.2), channel_id=1, source_target_pairs={{0,1},{1,0},{2,3},{3,2},{4,5},{5,4},{6,7},{7,6},{8,9},{9,8},{10,11... | collective-permute-start | bytes 393224 | tf_op jit(solution)/shard_map/ppermute | solution.py:454
  18.4 12.8 %collective-permute-start.5 = (bf16[256,2048]{1,0:T(8,128)(2,1)}, bf16[256,2048]{1,0:T(8,128)(2,1)S(1)}, u32[]{:S(2)}, u32[]{:S(2)}) collective-permute-start(bf16[256,2048]{1,0:T(8,128)(2,1)} %get-tuple-element.49), channel_id=1, source_target_pairs={{0,64},{64,0},{1,65},{65,1},{2,66},{66,2},{3,67},{67,3},{4,68},{68... | collective-permute-start | bytes 3145736 | tf_op jit(solution)/shard_map/ppermute | solution.py:458
  28.8 11.4 %collective-permute-start.7 = (bf16[256,768]{1,0:T(8,128)(2,1)}, bf16[256,768]{1,0:T(8,128)(2,1)S(1)}, u32[]{:S(2)}, u32[]{:S(2)}) collective-permute-start(bf16[256,768]{1,0:T(8,128)(2,1)} %pad_maximum_fusion.5), channel_id=1, source_target_pairs={{0,1},{1,0},{2,3},{3,2},{4,5},{5,4},{6,7},{7,6},{8,9},{9,8},{10,11... | collective-permute-start | bytes 1179656 | tf_op jit(solution)/shard_map/ppermute | solution.py:454
  28.9 11.3 %collective-permute-start.6 = (bf16[256,768]{1,0:T(8,128)(2,1)}, bf16[256,768]{1,0:T(8,128)(2,1)}, u32[]{:S(2)}, u32[]{:S(2)}) collective-permute-start(bf16[256,768]{1,0:T(8,128)(2,1)} %pad_maximum_fusion.4), channel_id=1, source_target_pairs={{0,4},{1,5},{2,6},{3,7},{4,0},{5,1},{6,2},{7,3},{8,12},{9,13},{10,... | collective-permute-start | bytes 1179656 | tf_op jit(solution)/shard_map/ppermute | solution.py:454
  29.2 11.0 %collective-permute-start.8 = (bf16[256,512]{1,0:T(8,128)(2,1)}, bf16[256,512]{1,0:T(8,128)(2,1)}, u32[]{:S(2)}, u32[]{:S(2)}) collective-permute-start(bf16[256,512]{1,0:T(8,128)(2,1)} %pad_maximum_fusion.6), channel_id=1, source_target_pairs={{0,16},{1,17},{2,18},{3,19},{4,20},{5,21},{6,22},{7,23},{8,24},{9,... | collective-permute-start | bytes 786440 | tf_op jit(solution)/shard_map/ppermute | solution.py:454
  40.2 69.1 %all-to-all-start = ((bf16[8,256,2176]{2,1,0:T(8,128)(2,1)}), bf16[8,256,2176]{2,1,0:T(8,128)(2,1)}, u32[]{:S(2)}, u32[]{:S(2)}) async-start(bf16[8,256,2176]{2,1,0:T(8,128)(2,1)} %bitcast.19), calls=%async_computation | async-start | bytes 17825792 | tf_op jit(solution)/shard_map/all_to_all | solution.py:471
  46.7 21.0 %collective-permute-start.10 = (bf16[512,768]{1,0:T(8,128)(2,1)S(1)}, bf16[512,768]{1,0:T(8,128)(2,1)S(1)}, u32[]{:S(2)}, u32[]{:S(2)}) collective-permute-start(bf16[512,768]{1,0:T(8,128)(2,1)S(1)} %pad_maximum_fusion.2.refs_2_), channel_id=1, source_target_pairs={{0,16},{1,17},{2,18},{3,19},{4,20},{5,21},{6,22},{7,23},{8,24},{9,... | collective-permute-start | bytes 2359304 | tf_op jit(solution)/shard_map/ppermute | solution.py:454
  48.2 54.0 %collective-permute-start.9 = (bf16[512,768]{1,0:T(8,128)(2,1)S(1)}, bf16[512,768]{1,0:T(8,128)(2,1)}, u32[]{:S(2)}, u32[]{:S(2)}) collective-permute-start(bf16[512,768]{1,0:T(8,128)(2,1)S(1)} %pad_maximum_fusion.1.refs_0_), channel_id=1, source_target_pairs={{0,1},{1,0},{2,3},{3,2},{4,5},{5,4},{6,7},{7,6},{8,9},{9,8},{10,11... | collective-permute-start | bytes 2359304 | tf_op jit(solution)/shard_map/ppermute | solution.py:454
  51.8 15.4 %collective-permute-start.11 = (bf16[512,512]{1,0:T(8,128)(2,1)S(1)}, bf16[512,512]{1,0:T(8,128)(2,1)S(1)}, u32[]{:S(2)}, u32[]{:S(2)}) collective-permute-start(bf16[512,512]{1,0:T(8,128)(2,1)S(1)} %pad_maximum_fusion.3.refs_4_), channel_id=1, source_target_pairs={{0,4},{1,5},{2,6},{3,7},{4,0},{5,1},{6,2},{7,3},{8,12},{9,13},{10,... | collective-permute-start | bytes 1572872 | tf_op jit(solution)/shard_map/ppermute | solution.py:454
  115.0 35.6 %all-to-all-start.1 = ((bf16[8,128,2048]{2,1,0:T(8,128)(2,1)}), bf16[8,128,2048]{2,1,0:T(8,128)(2,1)}, u32[]{:S(2)}, u32[]{:S(2)}) async-start(bf16[8,128,2048]{2,1,0:T(8,128)(2,1)} %bitcast.21), calls=%async_computation.1 | async-start | bytes 8388608 | tf_op jit(solution)/shard_map/all_to_all | solution.py:471
  150.5 51.3 %collective-permute-start.18 = (bf16[1024,2048]{1,0:T(8,128)(2,1)}, bf16[1024,2048]{1,0:T(8,128)(2,1)}, u32[]{:S(2)}, u32[]{:S(2)}) collective-permute-start(bf16[1024,2048]{1,0:T(8,128)(2,1)} %bitcast.13), channel_id=1, source_target_pairs={{0,64},{64,0},{1,65},{65,1},{2,66},{66,2},{3,67},{67,3},{4,68},{68... | collective-permute-start | bytes 12582920 | tf_op jit(solution)/shard_map/ppermute | solution.py:458
  155.0 10.6 %collective-permute-start.16 = (bf16[512,640]{1,0:T(8,128)(2,1)S(1)}, bf16[512,640]{1,0:T(8,128)(2,1)S(1)}, u32[]{:S(2)}, u32[]{:S(2)}) collective-permute-start(bf16[512,640]{1,0:T(8,128)(2,1)S(1)} %copy-done.15), channel_id=1, source_target_pairs={{0,4},{1,5},{2,6},{3,7},{4,0},{5,1},{6,2},{7,3},{8,12},{9,13},{10,... | collective-permute-start | bytes 1966088 | tf_op jit(solution)/shard_map/ppermute | solution.py:454
  156.6 14.4 %collective-permute-start.14 = (bf16[512,768]{1,0:T(8,128)(2,1)}, bf16[512,768]{1,0:T(8,128)(2,1)}, u32[]{:S(2)}, u32[]{:S(2)}) collective-permute-start(bf16[512,768]{1,0:T(8,128)(2,1)} %get-tuple-element.60), channel_id=1, source_target_pairs={{0,16},{1,17},{2,18},{3,19},{4,20},{5,21},{6,22},{7,23},{8,24},{9,... | collective-permute-start | bytes 2359304 | tf_op jit(solution)/shard_map/ppermute | solution.py:454
  156.6 16.0 %collective-permute-start.12 = (bf16[512,768]{1,0:T(8,128)(2,1)}, bf16[512,768]{1,0:T(8,128)(2,1)}, u32[]{:S(2)}, u32[]{:S(2)}) collective-permute-start(bf16[512,768]{1,0:T(8,128)(2,1)} %get-tuple-element.58), channel_id=1, source_target_pairs={{0,1},{1,0},{2,3},{3,2},{4,5},{5,4},{6,7},{7,6},{8,9},{9,8},{10,11... | collective-permute-start | bytes 2359304 | tf_op jit(solution)/shard_map/ppermute | solution.py:454
  165.9 9.8 %collective-permute-start.17 = (bf16[256,640]{1,0:T(8,128)(2,1)S(1)}, bf16[256,640]{1,0:T(8,128)(2,1)S(1)}, u32[]{:S(2)}, u32[]{:S(2)}) collective-permute-start(bf16[256,640]{1,0:T(8,128)(2,1)S(1)} %slice.136), channel_id=1, source_target_pairs={{0,16},{1,17},{2,18},{3,19},{4,20},{5,21},{6,22},{7,23},{8,24},{9,... | collective-permute-start | bytes 983048 | tf_op jit(solution)/shard_map/ppermute | solution.py:454
  166.3 55.1 %all-to-all-start.2 = ((bf16[8,128,2048]{2,1,0:T(8,128)(2,1)}), bf16[8,128,2048]{2,1,0:T(8,128)(2,1)}, u32[]{:S(2)}, u32[]{:S(2)}) async-start(bf16[8,128,2048]{2,1,0:T(8,128)(2,1)} %bitcast.20), calls=%async_computation.2 | async-start | bytes 8388608 | tf_op jit(solution)/shard_map/all_to_all | solution.py:471
  172.5 25.7 %collective-permute-start.15 = (bf16[256,768]{1,0:T(8,128)(2,1)S(1)}, bf16[256,768]{1,0:T(8,128)(2,1)S(1)}, u32[]{:S(2)}, u32[]{:S(2)}) collective-permute-start(bf16[256,768]{1,0:T(8,128)(2,1)S(1)} %slice.134), channel_id=1, source_target_pairs={{0,1},{1,0},{2,3},{3,2},{4,5},{5,4},{6,7},{7,6},{8,9},{9,8},{10,11... | collective-permute-start | bytes 1179656 | tf_op jit(solution)/shard_map/ppermute | solution.py:454
  174.0 24.3 %collective-permute-start.13 = (bf16[256,768]{1,0:T(8,128)(2,1)S(1)}, bf16[256,768]{1,0:T(8,128)(2,1)S(1)}, u32[]{:S(2)}, u32[]{:S(2)}) collective-permute-start(bf16[256,768]{1,0:T(8,128)(2,1)S(1)} %slice.135), channel_id=1, source_target_pairs={{0,4},{1,5},{2,6},{3,7},{4,0},{5,1},{6,2},{7,3},{8,12},{9,13},{10,... | collective-permute-start | bytes 1179656 | tf_op jit(solution)/shard_map/ppermute | solution.py:454
  175.7 33.5 %collective-permute-start.21 = (bf16[128,640]{1,0:T(8,128)(2,1)S(1)}, bf16[128,640]{1,0:T(8,128)(2,1)S(1)}, u32[]{:S(2)}, u32[]{:S(2)}) collective-permute-start(bf16[128,640]{1,0:T(8,128)(2,1)S(1)} %slice.139), channel_id=1, source_target_pairs={{0,1},{1,0},{2,3},{3,2},{4,5},{5,4},{6,7},{7,6},{8,9},{9,8},{10,11... | collective-permute-start | bytes 491528 | tf_op jit(solution)/shard_map/ppermute | solution.py:454
  198.4 10.8 %collective-permute-start.20 = (bf16[128,768]{1,0:T(8,128)(2,1)S(1)}, bf16[128,768]{1,0:T(8,128)(2,1)S(1)}, u32[]{:S(2)}, u32[]{:S(2)}) collective-permute-start(bf16[128,768]{1,0:T(8,128)(2,1)S(1)} %slice.137), channel_id=1, source_target_pairs={{0,4},{1,5},{2,6},{3,7},{4,0},{5,1},{6,2},{7,3},{8,12},{9,13},{10,... | collective-permute-start | bytes 589832 | tf_op jit(solution)/shard_map/ppermute | solution.py:454
  200.3 9.0 %collective-permute-start.19 = (bf16[128,768]{1,0:T(8,128)(2,1)S(1)}, bf16[128,768]{1,0:T(8,128)(2,1)S(1)}, u32[]{:S(2)}, u32[]{:S(2)}) collective-permute-start(bf16[128,768]{1,0:T(8,128)(2,1)S(1)} %slice.138), channel_id=1, source_target_pairs={{0,16},{1,17},{2,18},{3,19},{4,20},{5,21},{6,22},{7,23},{8,24},{9,... | collective-permute-start | bytes 589832 | tf_op jit(solution)/shard_map/ppermute | solution.py:454
  (18 other events, 351.5 us)

commit v2 on v1

--- a/solution.py
+++ b/solution.py
@@ -18,7 +18,6 @@
 VMEM_BYTES = 60 * 1024 * 1024
 
 
-WIDTH = 4096
 CHUNK = 768
 ROW_BLOCK = LANES
 
@@ -108,57 +107,67 @@
 
 
 def slot_grad_kernel(
-    core_ref, list_ref, packed_ref, packed_other_ref, gated_ref, gated_other_ref, slot_grad_ref
+    core_ref, packed_ref, packed_other_ref, gated_ref, gated_other_ref, slot_grad_ref, turned_ref
 ):
-    owners = packed_ref.shape[1] // CAPACITY
+    slot_count = packed_ref.shape[1]
     groups = ((packed_ref, gated_ref), (packed_other_ref, gated_other_ref))
-    for group, (weights, gated) in enumerate(groups):
-        found = lax.dot_general(
-            weights[...], gated[...], (((0,), (0,)), ((), ())), preferred_element_type=jnp.float32
+
+    @pl.when(pl.program_id(0) == 0)
+    def _():
+        for group, (weights, _) in enumerate(groups):
+            turned_ref[group] = weights[...].T
+
+    for group, (_, gated) in enumerate(groups):
+        found = jnp.dot(
+            turned_ref[group], gated[...], preferred_element_type=jnp.float32
         ).astype(jnp.bfloat16)
-        for owner in range(owners):
+        for owner in range(slot_count // CAPACITY):
             cube, chip = slot_place(owner, core_ref[0])
             start = (cube * 2 + group) * ROW_BLOCK + chip * CAPACITY
             slot_grad_ref[pl.ds(pl.multiple_of(start, CAPACITY), CAPACITY), :] = found[
                 owner * CAPACITY : (owner + 1) * CAPACITY, :
             ]
 
-    @pl.when(pl.program_id(0) == pl.num_programs(0) - 1)
-    def _():
-        ones = jnp.ones((LANES, LANES), jnp.bfloat16)
-        row = lax.broadcasted_iota(jnp.int32, (LANES, LANES), 0)
-        lane = lax.broadcasted_iota(jnp.int32, (LANES, LANES), 1)
-        start = WIDTH // 2 - (len(ORDERS) - 1) * CHUNK
-        for block in range(list_ref.shape[0]):
-            diagonal = jnp.where(row == lane, list_ref[block : block + 1, :], 0.0)
-            slot_grad_ref[block * LANES : (block + 1) * LANES, start : start + LANES] = jnp.dot(
-                diagonal.astype(jnp.bfloat16), ones, preferred_element_type=jnp.float32
-            ).astype(jnp.bfloat16)
-
-
-def slot_grad_call(core, lists, packed, packed_other, gated, gated_other):
+
+def slot_grad_call(core, packed, packed_other, gated, gated_other):
     tokens, half = gated.shape
     slot_count = packed.shape[1]
     whole = lambda i: (0, 0)
     by_cols = lambda i: (0, i)
     weights = pl.BlockSpec((tokens, slot_count), whole)
-    columns = pl.BlockSpec((tokens, CHUNK), by_cols)
+    columns = pl.BlockSpec((tokens, COLS), by_cols)
     return pl.pallas_call(
         slot_grad_kernel,
-        grid=(len(ORDERS),),
-        in_specs=[
-            pl.BlockSpec(memory_space=pltpu.SMEM),
-            pl.BlockSpec(lists.shape, whole),
-            weights, weights, columns, columns,
-        ],
-        out_specs=pl.BlockSpec((2 * slot_count, CHUNK), by_cols),
-        out_shape=jax.ShapeDtypeStruct((2 * slot_count, half + LANES), jnp.bfloat16),
+        grid=(half // COLS,),
+        in_specs=[pl.BlockSpec(memory_space=pltpu.SMEM), weights, weights, columns, columns],
+        out_specs=pl.BlockSpec((2 * slot_count, COLS), by_cols),
+        out_shape=jax.ShapeDtypeStruct((2 * slot_count, half), jnp.bfloat16),
+        scratch_shapes=[pltpu.VMEM((2, slot_count, tokens), jnp.bfloat16)],
         compiler_params=pltpu.CompilerParams(vmem_limit_bytes=VMEM_BYTES),
         cost_estimate=pl.CostEstimate(
             flops=4 * tokens * slot_count * half, bytes_accessed=14 * 2**20, transcendentals=0
         ),
         name="slot_gradients",
-    )(core, lists, packed, packed_other, gated, gated_other)
+    )(core, packed, packed_other, gated, gated_other)
+
+
+def spread_kernel(list_ref, spread_ref):
+    ones = jnp.ones((LANES, LANES), jnp.bfloat16)
+    row = lax.broadcasted_iota(jnp.int32, (LANES, LANES), 0)
+    lane = lax.broadcasted_iota(jnp.int32, (LANES, LANES), 1)
+    for block in range(list_ref.shape[0]):
+        diagonal = jnp.where(row == lane, list_ref[block : block + 1, :], 0.0)
+        spread_ref[block * LANES : (block + 1) * LANES, :] = jnp.dot(
+            diagonal.astype(jnp.bfloat16), ones, preferred_element_type=jnp.float32
+        ).astype(jnp.bfloat16)
+
+
+def spread_call(lists):
+    return pl.pallas_call(
+        spread_kernel,
+        out_shape=jax.ShapeDtypeStruct((lists.size, LANES), jnp.bfloat16),
+        name="spread_lists",
+    )(lists)
 
 
 def relative(order, position):
@@ -206,15 +215,15 @@
                     out_ref[at, : found.shape[1]] = found[peer * CAPACITY : (peer + 1) * CAPACITY, :]
 
 
-def select_call(group, spot, arrived, parts):
-    rows, wide = arrived.shape
+def select_call(group, spot, ids, parts, half_width):
+    rows, wide = ids.shape[0], half_width + LANES
     whole = lambda i: (0, 0)
     return pl.pallas_call(
         functools.partial(select_kernel, group),
         grid=(len(ORDERS),),
         in_specs=[
             pl.BlockSpec(memory_space=pltpu.SMEM),
-            pl.BlockSpec((rows, LANES), lambda i: (0, wide // LANES - 1)),
+            pl.BlockSpec(ids.shape, whole),
         ]
         + [pl.BlockSpec(part.shape, whole) for part in parts],
         out_specs=pl.BlockSpec((rows // 2, CHUNK), lambda i: (0, i)),
@@ -224,7 +233,7 @@
             flops=rows * LANES * wide, bytes_accessed=3 * rows * wide, transcendentals=0
         ),
         name="select_rows",
-    )(spot, arrived, *parts)
+    )(spot, ids, *parts)
 
 
 def partial_kernel(chunk, spot_ref, id_ref, arrived_ref, keep_ref, send_ref):
@@ -248,8 +257,8 @@
             target[start : start + rows, cols - LANES :] = hits.astype(target.dtype)
 
 
-def partial_call(chunk, spot, arrived, row_count):
-    rows, wide = arrived.shape
+def partial_call(chunk, spot, ids, arrived, row_count):
+    rows, wide = arrived.shape[0], arrived.shape[1] + LANES
     cols = chunk_width(chunk, wide)
     half = CUBE // 2 * row_count
     whole = lambda i: (0, 0)
@@ -258,7 +267,7 @@
         grid=(1,),
         in_specs=[
             pl.BlockSpec(memory_space=pltpu.SMEM),
-            pl.BlockSpec((rows, LANES), lambda i: (0, wide // LANES - 1)),
+            pl.BlockSpec(ids.shape, whole),
             pl.BlockSpec((rows, CHUNK), lambda i: (0, chunk)),
         ],
         out_specs=[pl.BlockSpec((half, cols), whole)] * 2,
@@ -271,7 +280,7 @@
             flops=2 * rows * LANES * cols, bytes_accessed=8 * rows * cols, transcendentals=0
         ),
         name="partial_sums",
-    )(spot, arrived, arrived)
+    )(spot, ids, arrived)
 
 
 def adam_kernel(
@@ -444,12 +453,12 @@
     return [(one + core) % RING for one in (index // RING**2, index // RING % RING, index % RING)]
 
 
-def swap(x, axis):
+def swap(x, axis, crossing=0):
     pairs = []
     for core in range(2):
         for index in range(RING**3):
             shifted = shifted_of(core, index)
-            shifted[axis] ^= 1
+            shifted[axis] = ((shifted[axis] + crossing) ^ 1) - crossing
             pairs.append((core * RING**3 + index, core * RING**3 + place_of(core, shifted)))
     return lax.ppermute(x, ("batch", "table"), pairs)
 
@@ -505,36 +514,49 @@
     lists = lists.reshape(2, capacity, 2, 2, 2, 2, 2, 2).transpose(2, 4, 6, 0, 3, 5, 7, 1)
     lists = lists.reshape(2 * CUBE, ROW_BLOCK).astype(jnp.float32)
 
+    lists = lists[None]
+    crossed = swap(lists, 0, 1)
     gated, gated_theirs = gated_call(which, gate_pre, out_grad)
     gated_other = swap_cores(gated_theirs)
-    swapped = after([gated], swapped)
+    crossed, *swapped = after([gated], [crossed, *swapped])
+    lists = jnp.concatenate([lists, crossed], axis=0)
+    crossed = swap(lists, 1, 1)
     parts = [jnp.concatenate(pair, axis=0) for pair in zip(parts, swapped)]
     swapped = [swap(part, order[1]) for part, order in zip(parts, ORDERS)]
     slot = (slot_of_pick % table_size) * capacity + slot_of_pick // table_size
     (slot,) = after(parts, [slot])
     packed, weight = pack_call(pick_logits, slot, slot_count)
     packed_other = swap_cores(packed)
-    slot_grad = slot_grad_call(which, lists, packed, packed_other, gated, gated_other)
-    swapped = after([slot_grad], swapped)
+    (crossed,) = after([packed], [crossed])
+    lists = jnp.concatenate([lists, crossed], axis=0)
+    crossed = swap(lists, 2, 1)
+    slot_grad = slot_grad_call(which, packed, packed_other, gated, gated_other)
+    crossed, *swapped = after([slot_grad], [crossed, *swapped])
+    lists = jnp.concatenate([lists, crossed], axis=0)
     (slot_grad,) = after(swapped, [slot_grad])
     arrived = cube_exchange(slot_grad)
     parts = [jnp.concatenate(pair, axis=0) for pair in zip(parts, swapped)]
     swapped = [swap(part, order[2]) for part, order in zip(parts, ORDERS)]
     gathered = [half for pair in zip(parts, swapped) for half in pair]
-    (arrived,) = after(swapped, [arrived])
-
-    found_other = select_call(1, spot, arrived, gathered)
+    own_cube = sum(bit * (one // 2) for bit, one in zip(BITS, shifted))
+    lists = lists.reshape(CUBE, CUBE, 2, ROW_BLOCK)
+    lists = lax.dynamic_slice(lists, (0, own_cube, 0, 0), (CUBE, 1, 2, ROW_BLOCK))
+    lists = lists.reshape(2, 2, 2, 2, ROW_BLOCK).transpose(2, 1, 0, 3, 4)
+    for axis in range(3):
+        lists = jnp.where(shifted[axis] // 2 == 0, lists, jnp.flip(lists, axis))
+    ids = spread_call(lists.reshape(2 * CUBE, ROW_BLOCK))
+    found_other = select_call(1, spot, ids, gathered, half_width)
+    found = select_call(0, spot, ids, gathered, half_width)
+    (arrived,) = after([found, found_other], [arrived])
+    (found_other,) = after([arrived], [found_other])
     fetched_theirs = cube_exchange(found_other)
-    (arrived,) = after([found_other], [arrived])
-    found = select_call(0, spot, arrived, gathered)
-    (arrived,) = after([found], [arrived])
-    halves = [partial_call(chunk, spot, arrived, row_count) for chunk in range(len(ORDERS))]
-    (fetched_theirs,) = after([keep for keep, _ in halves], [fetched_theirs])
+    halves = [partial_call(chunk, spot, ids, arrived, row_count) for chunk in range(len(ORDERS))]
+    received = [swap(send, order[2]) for (_, send), order in zip(halves, ORDERS)]
+    (fetched_theirs,) = after(received, [fetched_theirs])
     (found,) = after([fetched_theirs], [found])
     fetched = cube_exchange(found)
     fetched_other = swap_cores(fetched_theirs)
 
-    received = [swap(send, order[2]) for (_, send), order in zip(halves, ORDERS)]
     half = CUBE // 4 * row_count
     for step in (1, 0):
         totals = [keep + other.astype(jnp.float32) for (keep, _), other in zip(halves, received)]

time: 231 us -> 230 us (level)
  waiting for transfers between devices: 98.8 us -> 90.2 us
  starting transfers between devices: 48.2 us -> 54.1 us
    all_to_all x3, waiting for transfers between devices: 20.8 us -> 4.6 us  [cube_exchange(): lax.all_to_all(x, ('batch', 'table'), split_axis=0, concat_axis=0, axis_i...]
    ppermute x18 -> x21, waiting for transfers between devices: 76.7 us -> 84.2 us  [swap(): return lax.ppermute(x, ('batch', 'table'), pairs)]
    ppermute x18 -> x21, starting transfers between devices: 27.3 us -> 32.7 us  [swap(): return lax.ppermute(x, ('batch', 'table'), pairs)]
    pallas_call x1 -> x2, Pallas kernels: 7.2 us -> 8.98 us  [the longest x1 7.18 us: slot_grad_call(): pl.pallas_call(slot_grad_kernel, grid=(half // COLS,), in_specs=[pl.Block...]
  transfers between devices with their start and end apart: 26 -> 29, of which waited for: 8 -> 9; matrix products, arithmetic and copies ran while one was open for 6% -> 6% of each run, Pallas kernels for 22% -> 25%
where the time goes in v2:
time: 230 us; the launch traced here: 228 us
  waiting for transfers between devices  90.2 us (39%)
  Pallas kernels  65.4 us (28%)
  starting transfers between devices  54.1 us (24%)
  local copies, waits for them, and re-layouts  8.91 us (4%)
  other arithmetic  8.44 us (4%)
    ppermute x21, waiting for transfers between devices, swap(): return lax.ppermute(x, ('batch', 'table'), pairs)  84.2 us
    ppermute x21, starting transfers between devices, swap(): return lax.ppermute(x, ('batch', 'table'), pairs)  32.7 us
    pallas_call x2, Pallas kernels, read_call(): pl.pallas_call(functools.partial(read_kernel, own), grid_spec=pltpu.Prefe...  15.8 us
    all_to_all x3, starting transfers between devices, cube_exchange(): lax.all_to_all(x, ('batch', 'table'), split_axis=0, concat_axis=0, axis_i...  14.2 us
    pallas_call x3, Pallas kernels, partial_call(): pl.pallas_call(functools.partial(partial_kernel, chunk), grid=(1,), in_sp...  11.4 us
    pallas_call x2, Pallas kernels, select_call(): pl.pallas_call(functools.partial(select_kernel, group), grid=(len(ORDERS)...  11.3 us
    pallas_call x1, Pallas kernels, adam_call(): pl.pallas_call(adam_kernel, grid_spec=pltpu.PrefetchScalarGridSpec(num_sc...  8.04 us
    ppermute x5, starting transfers between devices, swap_cores(): return lax.ppermute(x, 'batch', [(0, 1), (1, 0)])  7.2 us
  transfers between devices with their start and end apart: 29, of which 9 were waited for; matrix products, arithmetic and copies ran while one was open for 6% of the time, Pallas kernels for 25%

profile of v2, /device:TPU:1, one launch (start us, length us, event | category | flops | bytes accessed | tf_op | source)
XLA Modules:
  0.0 228.5 jit_solution(15962832792304067428)
XLA Ops:
  3.8 3.9 %collective-permute-start.4 = (bf16[128,512]{1,0:T(8,128)(2,1)S(1)}, bf16[128,512]{1,0:T(8,128)(2,1)S(1)}, u32[]{:S(2)}, u32[]{:S(2)}) collective-permute-start(bf16[128,512]{1,0:T(8,128)(2,1)S(1)} %constant_dynamic-slice_fusion.2), channel_id=1, source_target_pairs={{0,1},{1,0},{2,3},{3,2},{4,5},{5,4},{6,7},{7,6},{8,9},{9,8},{10,11... | collective-permute-start | bytes 393224 | tf_op jit(solution)/shard_map/ppermute | solution.py:463
  14.1 4.3 %gated_halves.1 = (bf16[256,2048]{1,0:T(8,128)(2,1)}, bf16[256,2048]{1,0:T(8,128)(2,1)}) custom-call(s32[1]{0:T(128)} %bitcast.core_ref, bf16[256,4096]{1,0:T(8,128)(2,1)} %gate_ref.3, bf16[256,4096]{1,0:T(8,128)(2,1)} %grad_ref.3, bf16[256,4096]{1,0:T(8,128)(2,1)} %gate_ref.3, bf16[256,4096]{1,0:T(8,128)(2,1)} %grad_ref.3), custom_call_target="tpu_custom_call" | custom-call | flops 4194304 | bytes 6291456 | tf_op jit(solution)/shard_map/gated_halves/pallas_call | solution.py:92
  22.4 5.7 %pack_weights.1 = (bf16[256,1024]{1,0:T(8,128)(2,1)}, f32[256,32]{1,0:T(8,128)}) custom-call(f32[256,32]{1,0:T(8,128)} %copy.29.logit_ref, s32[256,32]{1,0:T(8,128)} %fusion.1.slot_ref), custom_call_target="tpu_custom_call" | custom-call | flops 33554432 | bytes 1048576 | tf_op jit(solution)/shard_map/pack_weights/pallas_call | solution.py:65
  28.1 2.8 %collective-permute-start.6 = (bf16[256,1024]{1,0:T(8,128)(2,1)}, bf16[256,1024]{1,0:T(8,128)(2,1)S(1)}, u32[]{:S(2)}, u32[]{:S(2)}) collective-permute-start(bf16[256,1024]{1,0:T(8,128)(2,1)} %get-tuple-element.50.packed_ref), channel_id=1, source_target_pairs={{0,64},{64,0},{1,65},{65,1},{2,66},{66,2},{3,67},{67,3},{4,68},{68... | collective-permute-start | bytes 1572872 | tf_op jit(solution)/shard_map/ppermute | solution.py:467
  37.4 7.2 %slot_gradients.1 = bf16[2048,2048]{1,0:T(8,128)(2,1)} custom-call(s32[1]{0:T(128)} %bitcast.core_ref, bf16[256,1024]{1,0:T(8,128)(2,1)} %get-tuple-element.50.packed_ref, bf16[256,1024]{1,0:T(8,128)(2,1)} %copy-done.11, bf16[256,2048]{1,0:T(8,128)(2,1)} %get-tuple-element.45.gated_ref, bf16[256,2048]{1,0:T(8,128)(2,1)} %copy-done.10), custom_call_target="tpu_custom_call" | custom-call | flops 2147483648 | bytes 14680064 | tf_op jit(solution)/shard_map/slot_gradients/pallas_call | solution.py:139
  45.4 5.0 %all-to-all-start = ((bf16[8,256,2048]{2,1,0:T(8,128)(2,1)}), bf16[8,256,2048]{2,1,0:T(8,128)(2,1)}, u32[]{:S(2)}, u32[]{:S(2)}) async-start(bf16[8,256,2048]{2,1,0:T(8,128)(2,1)} %bitcast.28), calls=%async_computation | async-start | bytes 16777216 | tf_op jit(solution)/shard_map/all_to_all | solution.py:480
  52.8 3.4 %collective-permute-start.12 = (bf16[512,768]{1,0:T(8,128)(2,1)S(1)}, bf16[512,768]{1,0:T(8,128)(2,1)}, u32[]{:S(2)}, u32[]{:S(2)}) collective-permute-start(bf16[512,768]{1,0:T(8,128)(2,1)S(1)} %pad_maximum_fusion.1.refs_0_), channel_id=1, source_target_pairs={{0,1},{1,0},{2,3},{3,2},{4,5},{5,4},{6,7},{7,6},{8,9},{9,8},{10,11... | collective-permute-start | bytes 2359304 | tf_op jit(solution)/shard_map/ppermute | solution.py:463
  62.1 10.6 %collective-permute-done.14.refs_5_ = bf16[512,512]{1,0:T(8,128)(2,1)S(1)} collective-permute-done((bf16[512,512]{1,0:T(8,128)(2,1)S(1)}, bf16[512,512]{1,0:T(8,128)(2,1)S(1)}, u32[]{:S(2)}, u32[]{:S(2)}) %collective-permute-start.14) | collective-permute-done | bytes 524320 | tf_op jit(solution)/shard_map/ppermute | solution.py:463
  72.9 32.7 %collective-permute-done.12.refs_1_ = bf16[512,768]{1,0:T(8,128)(2,1)} collective-permute-done((bf16[512,768]{1,0:T(8,128)(2,1)S(1)}, bf16[512,768]{1,0:T(8,128)(2,1)}, u32[]{:S(2)}, u32[]{:S(2)}) %collective-permute-start.12) | collective-permute-done | bytes 786464 | tf_op jit(solution)/shard_map/ppermute | solution.py:463
  105.5 5.6 %select_rows.3 = bf16[1024,2048]{1,0:T(8,128)(2,1)} custom-call(s32[1]{0:T(128)} %bitcast.9.spot_ref, bf16[2048,128]{1,0:T(8,128)(2,1)} %spread_lists.1.id_ref, bf16[512,768]{1,0:T(8,128)(2,1)} %copy-done.2, bf16[512,768]{1,0:T(8,128)(2,1)} %collective-permute-done.12.refs_1_, bf16[512,768]{1,0:T(8,128)(2,1)} %copy-done.1, bf16[512,768]{1,0:T(8,128)(2,1)} %copy-done.4, ...), custom_call_target="tpu_custom_call" | custom-call | flops 570425344 | bytes 13369344 | tf_op jit(solution)/shard_map/select_rows/pallas_call | solution.py:221
  111.2 5.6 %select_rows.2 = bf16[1024,2048]{1,0:T(8,128)(2,1)} custom-call(s32[1]{0:T(128)} %bitcast.9.spot_ref, bf16[2048,128]{1,0:T(8,128)(2,1)} %spread_lists.1.id_ref, bf16[512,768]{1,0:T(8,128)(2,1)} %copy-done.2, bf16[512,768]{1,0:T(8,128)(2,1)} %collective-permute-done.12.refs_1_, bf16[512,768]{1,0:T(8,128)(2,1)} %copy-done.1, bf16[512,768]{1,0:T(8,128)(2,1)} %copy-done.4, ...), custom_call_target="tpu_custom_call" | custom-call | flops 570425344 | bytes 13369344 | tf_op jit(solution)/shard_map/select_rows/pallas_call | solution.py:221
  116.8 4.6 %all-to-all-start.1 = ((bf16[8,128,2048]{2,1,0:T(8,128)(2,1)}), bf16[8,128,2048]{2,1,0:T(8,128)(2,1)}, u32[]{:S(2)}, u32[]{:S(2)}) async-start(bf16[8,128,2048]{2,1,0:T(8,128)(2,1)} %bitcast.30), calls=%async_computation.1 | async-start | bytes 8388608 | tf_op jit(solution)/shard_map/all_to_all | solution.py:480
  121.3 3.9 %partial_sums.4 = (f32[512,768]{1,0:T(8,128)}, bf16[512,768]{1,0:T(8,128)(2,1)}) custom-call(s32[1]{0:T(128)} %bitcast.9.spot_ref, bf16[2048,128]{1,0:T(8,128)(2,1)} %spread_lists.1.id_ref, bf16[2048,2048]{1,0:T(8,128)(2,1)} %bitcast.19.arrived_ref), custom_call_target="tpu_custom_call" | custom-call | flops 402653184 | bytes 12582912 | tf_op jit(solution)/shard_map/partial_sums/pallas_call | solution.py:265
  125.4 3.9 %partial_sums.3 = (f32[512,768]{1,0:T(8,128)}, bf16[512,768]{1,0:T(8,128)(2,1)}) custom-call(s32[1]{0:T(128)} %bitcast.9.spot_ref, bf16[2048,128]{1,0:T(8,128)(2,1)} %spread_lists.1.id_ref, bf16[2048,2048]{1,0:T(8,128)(2,1)} %bitcast.19.arrived_ref), custom_call_target="tpu_custom_call" | custom-call | flops 402653184 | bytes 12582912 | tf_op jit(solution)/shard_map/partial_sums/pallas_call | solution.py:265
  129.3 3.5 %collective-permute-start.15 = (bf16[512,768]{1,0:T(8,128)(2,1)}, bf16[512,768]{1,0:T(8,128)(2,1)}, u32[]{:S(2)}, u32[]{:S(2)}) collective-permute-start(bf16[512,768]{1,0:T(8,128)(2,1)} %get-tuple-element.61), channel_id=1, source_target_pairs={{0,1},{1,0},{2,3},{3,2},{4,5},{5,4},{6,7},{7,6},{8,9},{9,8},{10,11... | collective-permute-start | bytes 2359304 | tf_op jit(solution)/shard_map/ppermute | solution.py:463
  132.8 3.6 %partial_sums.5 = (f32[512,640]{1,0:T(8,128)}, bf16[512,640]{1,0:T(8,128)(2,1)}) custom-call(s32[1]{0:T(128)} %bitcast.9.spot_ref, bf16[2048,128]{1,0:T(8,128)(2,1)} %spread_lists.1.id_ref, bf16[2048,2048]{1,0:T(8,128)(2,1)} %bitcast.19.arrived_ref), custom_call_target="tpu_custom_call" | custom-call | flops 335544320 | bytes 10485760 | tf_op jit(solution)/shard_map/partial_sums/pallas_call | solution.py:265
  138.7 16.1 %collective-permute-done.19 = bf16[512,640]{1,0:T(8,128)(2,1)S(1)} collective-permute-done((bf16[512,640]{1,0:T(8,128)(2,1)}, bf16[512,640]{1,0:T(8,128)(2,1)S(1)}, u32[]{:S(2)}, u32[]{:S(2)}) %collective-permute-start.19) | collective-permute-done | bytes 655392 | tf_op jit(solution)/shard_map/ppermute | solution.py:463
  154.8 4.6 %all-to-all-done.1 = bf16[8,128,2048]{2,1,0:T(8,128)(2,1)} async-done(((bf16[8,128,2048]{2,1,0:T(8,128)(2,1)}), bf16[8,128,2048]{2,1,0:T(8,128)(2,1)}, u32[]{:S(2)}, u32[]{:S(2)}) %all-to-all-start.1) | async-done | bytes 4194336 | tf_op jit(solution)/shard_map/all_to_all | solution.py:480
  159.3 2.8 %collective-permute-start.21 = (bf16[1024,2048]{1,0:T(8,128)(2,1)}, bf16[1024,2048]{1,0:T(8,128)(2,1)}, u32[]{:S(2)}, u32[]{:S(2)}) collective-permute-start(bf16[1024,2048]{1,0:T(8,128)(2,1)} %bitcast.21), channel_id=1, source_target_pairs={{0,64},{64,0},{1,65},{65,1},{2,66},{66,2},{3,67},{67,3},{4,68},{68... | collective-permute-start | bytes 12582920 | tf_op jit(solution)/shard_map/ppermute | solution.py:467
  164.0 4.7 %all-to-all-start.2 = ((bf16[8,128,2048]{2,1,0:T(8,128)(2,1)}), bf16[8,128,2048]{2,1,0:T(8,128)(2,1)}, u32[]{:S(2)}, u32[]{:S(2)}) async-start(bf16[8,128,2048]{2,1,0:T(8,128)(2,1)} %bitcast.29), calls=%async_computation.2 | async-start | bytes 8388608 | tf_op jit(solution)/shard_map/all_to_all | solution.py:480
  175.2 21.1 %collective-permute-done.18 = bf16[256,768]{1,0:T(8,128)(2,1)S(1)} collective-permute-done((bf16[256,768]{1,0:T(8,128)(2,1)S(1)}, bf16[256,768]{1,0:T(8,128)(2,1)S(1)}, u32[]{:S(2)}, u32[]{:S(2)}) %collective-permute-start.18) | collective-permute-done | bytes 393248 | tf_op jit(solution)/shard_map/ppermute | solution.py:463
  200.4 7.4 %read_and_scores.2 = (bf16[256,4096]{1,0:T(8,128)(2,1)}, bf16[256,4096]{1,0:T(8,128)(2,1)}, f32[256,1024]{1,0:T(8,128)}) custom-call(s32[1]{0:T(128)} %bitcast.core_ref, bf16[256,1024]{1,0:T(8,128)(2,1)} %get-tuple-element.50.packed_ref, bf16[1024,2048]{1,0:T(8,128)(2,1)} %collective-permute-done.21.fetched_ref, bf16[256,4096]{1,0:T(8,128)(2,1)} %gate_ref.3, ...), custom_call_target="tpu_custom_call" | custom-call | flops 2147483648 | bytes 9437184 | tf_op jit(solution)/shard_map/read_and_scores/pallas_call | solution.py:425
  211.9 8.0 %adam_rows.1 = (bf16[128,4096]{1,0:T(8,128)(2,1)}, f32[128,4096]{1,0:T(8,128)}, f32[128,4096]{1,0:T(8,128)}) custom-call(s32[1]{0:T(128)} %bitcast.core_ref, f32[128,2176]{1,0:T(8,128)} %copy-done, f32[128,2176]{1,0:T(8,128)} %copy-done, f32[128,2176]{1,0:T(8,128)} %copy-done.9, bf16[128,4096]{1,0:T(8,128)(2,1)} %value_ref.1, f32[128,4096]{1,0:T(8,128)} %first_ref.1, ...), custom_call_target="tpu_custom_call" | custom-call | flops 5242880 | bytes 14680064 | tf_op jit(solution)/shard_map/adam_rows/pallas_call | solution.py:311
  220.0 8.4 %read_and_scores.3 = (bf16[256,4096]{1,0:T(8,128)(2,1)}, bf16[256,4096]{1,0:T(8,128)(2,1)}, f32[32,256]{1,0:T(8,128)}) custom-call(s32[1]{0:T(128)} %bitcast.core_ref, bf16[256,1024]{1,0:T(8,128)(2,1)} %get-tuple-element.50.packed_ref, bf16[1024,2048]{1,0:T(8,128)(2,1)} %bitcast.23.fetched_ref, ...), custom_call_target="tpu_custom_call", output_to_operand_aliasing={{0}: (8, {}), {1}: (9, {})} | custom-call | flops 2147483648 | bytes 9437184 | tf_op jit(solution)/shard_map/read_and_scores/pallas_call | solution.py:425
  (128 shorter events, 47.8 us)
Async XLA Ops:
  1.4 17.1 %collective-permute-start = (s32[16,64]{0,1:T(8,128)S(1)}, s32[16,64]{0,1:T(8,128)S(1)}, u32[]{:S(2)}, u32[]{:S(2)}) collective-permute-start(s32[16,64]{0,1:T(8,128)S(1)} %copy.21), channel_id=1, source_target_pairs={{0,64},{64,0},{1,65},{65,1},{2,66},{66,2},{3,67},{67,3},{4,68},{68... | collective-permute-start | bytes 12296 | tf_op jit(solution)/shard_map/ppermute | solution.py:467
  3.8 17.8 %collective-permute-start.4 = (bf16[128,512]{1,0:T(8,128)(2,1)S(1)}, bf16[128,512]{1,0:T(8,128)(2,1)S(1)}, u32[]{:S(2)}, u32[]{:S(2)}) collective-permute-start(bf16[128,512]{1,0:T(8,128)(2,1)S(1)} %constant_dynamic-slice_fusion.2), channel_id=1, source_target_pairs={{0,1},{1,0},{2,3},{3,2},{4,5},{5,4},{6,7},{7,6},{8,9},{9,8},{10,11... | collective-permute-start | bytes 393224 | tf_op jit(solution)/shard_map/ppermute | solution.py:463
  8.8 12.8 %collective-permute-start.3 = (bf16[128,768]{1,0:T(8,128)(2,1)S(1)}, bf16[128,768]{1,0:T(8,128)(2,1)S(1)}, u32[]{:S(2)}, u32[]{:S(2)}) collective-permute-start(bf16[128,768]{1,0:T(8,128)(2,1)S(1)} %get-tuple-element.84), channel_id=1, source_target_pairs={{0,4},{1,5},{2,6},{3,7},{4,0},{5,1},{6,2},{7,3},{8,12},{9,13},{10,... | collective-permute-start | bytes 589832 | tf_op jit(solution)/shard_map/ppermute | solution.py:463
  11.3 10.3 %collective-permute-start.2 = (bf16[128,768]{1,0:T(8,128)(2,1)S(1)}, bf16[128,768]{1,0:T(8,128)(2,1)S(1)}, u32[]{:S(2)}, u32[]{:S(2)}) collective-permute-start(bf16[128,768]{1,0:T(8,128)(2,1)S(1)} %get-tuple-element.85), channel_id=1, source_target_pairs={{0,16},{1,17},{2,18},{3,19},{4,20},{5,21},{6,22},{7,23},{8,24},{9,... | collective-permute-start | bytes 589832 | tf_op jit(solution)/shard_map/ppermute | solution.py:463
  18.4 18.0 %collective-permute-start.7 = (bf16[256,2048]{1,0:T(8,128)(2,1)}, bf16[256,2048]{1,0:T(8,128)(2,1)S(1)}, u32[]{:S(2)}, u32[]{:S(2)}) collective-permute-start(bf16[256,2048]{1,0:T(8,128)(2,1)} %get-tuple-element.53), channel_id=1, source_target_pairs={{0,64},{64,0},{1,65},{65,1},{2,66},{66,2},{3,67},{67,3},{4,68},{68... | collective-permute-start | bytes 3145736 | tf_op jit(solution)/shard_map/ppermute | solution.py:467
  30.9 13.7 %collective-permute-start.10 = (bf16[256,768]{1,0:T(8,128)(2,1)S(1)}, bf16[256,768]{1,0:T(8,128)(2,1)}, u32[]{:S(2)}, u32[]{:S(2)}) collective-permute-start(bf16[256,768]{1,0:T(8,128)(2,1)S(1)} %pad_maximum_fusion.5), channel_id=1, source_target_pairs={{0,1},{1,0},{2,3},{3,2},{4,5},{5,4},{6,7},{7,6},{8,9},{9,8},{10,11... | collective-permute-start | bytes 1179656 | tf_op jit(solution)/shard_map/ppermute | solution.py:463
  30.9 13.7 %collective-permute-start.9 = (bf16[256,768]{1,0:T(8,128)(2,1)S(1)}, bf16[256,768]{1,0:T(8,128)(2,1)S(1)}, u32[]{:S(2)}, u32[]{:S(2)}) collective-permute-start(bf16[256,768]{1,0:T(8,128)(2,1)S(1)} %pad_maximum_fusion.4), channel_id=1, source_target_pairs={{0,4},{1,5},{2,6},{3,7},{4,0},{5,1},{6,2},{7,3},{8,12},{9,13},{10,... | collective-permute-start | bytes 1179656 | tf_op jit(solution)/shard_map/ppermute | solution.py:463
  33.7 10.9 %collective-permute-start.11 = (bf16[256,512]{1,0:T(8,128)(2,1)}, bf16[256,512]{1,0:T(8,128)(2,1)}, u32[]{:S(2)}, u32[]{:S(2)}) collective-permute-start(bf16[256,512]{1,0:T(8,128)(2,1)} %pad_maximum_fusion.6), channel_id=1, source_target_pairs={{0,16},{1,17},{2,18},{3,19},{4,20},{5,21},{6,22},{7,23},{8,24},{9,... | collective-permute-start | bytes 786440 | tf_op jit(solution)/shard_map/ppermute | solution.py:463
  45.4 71.4 %all-to-all-start = ((bf16[8,256,2048]{2,1,0:T(8,128)(2,1)}), bf16[8,256,2048]{2,1,0:T(8,128)(2,1)}, u32[]{:S(2)}, u32[]{:S(2)}) async-start(bf16[8,256,2048]{2,1,0:T(8,128)(2,1)} %bitcast.28), calls=%async_computation | async-start | bytes 16777216 | tf_op jit(solution)/shard_map/all_to_all | solution.py:480
  51.9 21.0 %collective-permute-start.13 = (bf16[512,768]{1,0:T(8,128)(2,1)S(1)}, bf16[512,768]{1,0:T(8,128)(2,1)S(1)}, u32[]{:S(2)}, u32[]{:S(2)}) collective-permute-start(bf16[512,768]{1,0:T(8,128)(2,1)S(1)} %pad_maximum_fusion.2.refs_2_), channel_id=1, source_target_pairs={{0,16},{1,17},{2,18},{3,19},{4,20},{5,21},{6,22},{7,23},{8,24},{9,... | collective-permute-start | bytes 2359304 | tf_op jit(solution)/shard_map/ppermute | solution.py:463
  52.8 52.7 %collective-permute-start.12 = (bf16[512,768]{1,0:T(8,128)(2,1)S(1)}, bf16[512,768]{1,0:T(8,128)(2,1)}, u32[]{:S(2)}, u32[]{:S(2)}) collective-permute-start(bf16[512,768]{1,0:T(8,128)(2,1)S(1)} %pad_maximum_fusion.1.refs_0_), channel_id=1, source_target_pairs={{0,1},{1,0},{2,3},{3,2},{4,5},{5,4},{6,7},{7,6},{8,9},{9,8},{10,11... | collective-permute-start | bytes 2359304 | tf_op jit(solution)/shard_map/ppermute | solution.py:463
  57.2 15.4 %collective-permute-start.14 = (bf16[512,512]{1,0:T(8,128)(2,1)S(1)}, bf16[512,512]{1,0:T(8,128)(2,1)S(1)}, u32[]{:S(2)}, u32[]{:S(2)}) collective-permute-start(bf16[512,512]{1,0:T(8,128)(2,1)S(1)} %pad_maximum_fusion.3.refs_4_), channel_id=1, source_target_pairs={{0,4},{1,5},{2,6},{3,7},{4,0},{5,1},{6,2},{7,3},{8,12},{9,13},{10,... | collective-permute-start | bytes 1572872 | tf_op jit(solution)/shard_map/ppermute | solution.py:463
  116.8 42.6 %all-to-all-start.1 = ((bf16[8,128,2048]{2,1,0:T(8,128)(2,1)}), bf16[8,128,2048]{2,1,0:T(8,128)(2,1)}, u32[]{:S(2)}, u32[]{:S(2)}) async-start(bf16[8,128,2048]{2,1,0:T(8,128)(2,1)} %bitcast.30), calls=%async_computation.1 | async-start | bytes 8388608 | tf_op jit(solution)/shard_map/all_to_all | solution.py:480
  125.3 29.5 %collective-permute-start.17 = (bf16[512,768]{1,0:T(8,128)(2,1)}, bf16[512,768]{1,0:T(8,128)(2,1)}, u32[]{:S(2)}, u32[]{:S(2)}) collective-permute-start(bf16[512,768]{1,0:T(8,128)(2,1)} %get-tuple-element.63), channel_id=1, source_target_pairs={{0,16},{1,17},{2,18},{3,19},{4,20},{5,21},{6,22},{7,23},{8,24},{9,... | collective-permute-start | bytes 2359304 | tf_op jit(solution)/shard_map/ppermute | solution.py:463
  129.3 25.4 %collective-permute-start.15 = (bf16[512,768]{1,0:T(8,128)(2,1)}, bf16[512,768]{1,0:T(8,128)(2,1)}, u32[]{:S(2)}, u32[]{:S(2)}) collective-permute-start(bf16[512,768]{1,0:T(8,128)(2,1)} %get-tuple-element.61), channel_id=1, source_target_pairs={{0,1},{1,0},{2,3},{3,2},{4,5},{5,4},{6,7},{7,6},{8,9},{9,8},{10,11... | collective-permute-start | bytes 2359304 | tf_op jit(solution)/shard_map/ppermute | solution.py:463
  136.4 18.3 %collective-permute-start.19 = (bf16[512,640]{1,0:T(8,128)(2,1)}, bf16[512,640]{1,0:T(8,128)(2,1)S(1)}, u32[]{:S(2)}, u32[]{:S(2)}) collective-permute-start(bf16[512,640]{1,0:T(8,128)(2,1)} %get-tuple-element.65), channel_id=1, source_target_pairs={{0,4},{1,5},{2,6},{3,7},{4,0},{5,1},{6,2},{7,3},{8,12},{9,13},{10,... | collective-permute-start | bytes 1966088 | tf_op jit(solution)/shard_map/ppermute | solution.py:463
  159.3 41.1 %collective-permute-start.21 = (bf16[1024,2048]{1,0:T(8,128)(2,1)}, bf16[1024,2048]{1,0:T(8,128)(2,1)}, u32[]{:S(2)}, u32[]{:S(2)}) collective-permute-start(bf16[1024,2048]{1,0:T(8,128)(2,1)} %bitcast.21), channel_id=1, source_target_pairs={{0,64},{64,0},{1,65},{65,1},{2,66},{66,2},{3,67},{67,3},{4,68},{68... | collective-permute-start | bytes 12582920 | tf_op jit(solution)/shard_map/ppermute | solution.py:467
  163.6 10.7 %collective-permute-start.20 = (bf16[256,640]{1,0:T(8,128)(2,1)S(1)}, bf16[256,640]{1,0:T(8,128)(2,1)S(1)}, u32[]{:S(2)}, u32[]{:S(2)}) collective-permute-start(bf16[256,640]{1,0:T(8,128)(2,1)S(1)} %slice.136), channel_id=1, source_target_pairs={{0,16},{1,17},{2,18},{3,19},{4,20},{5,21},{6,22},{7,23},{8,24},{9,... | collective-permute-start | bytes 983048 | tf_op jit(solution)/shard_map/ppermute | solution.py:463
  164.0 56.0 %all-to-all-start.2 = ((bf16[8,128,2048]{2,1,0:T(8,128)(2,1)}), bf16[8,128,2048]{2,1,0:T(8,128)(2,1)}, u32[]{:S(2)}, u32[]{:S(2)}) async-start(bf16[8,128,2048]{2,1,0:T(8,128)(2,1)} %bitcast.29), calls=%async_computation.2 | async-start | bytes 8388608 | tf_op jit(solution)/shard_map/all_to_all | solution.py:480
  170.2 26.2 %collective-permute-start.18 = (bf16[256,768]{1,0:T(8,128)(2,1)S(1)}, bf16[256,768]{1,0:T(8,128)(2,1)S(1)}, u32[]{:S(2)}, u32[]{:S(2)}) collective-permute-start(bf16[256,768]{1,0:T(8,128)(2,1)S(1)} %slice.134), channel_id=1, source_target_pairs={{0,1},{1,0},{2,3},{3,2},{4,5},{5,4},{6,7},{7,6},{8,9},{9,8},{10,11... | collective-permute-start | bytes 1179656 | tf_op jit(solution)/shard_map/ppermute | solution.py:463
  171.9 26.8 %collective-permute-start.16 = (bf16[256,768]{1,0:T(8,128)(2,1)S(1)}, bf16[256,768]{1,0:T(8,128)(2,1)S(1)}, u32[]{:S(2)}, u32[]{:S(2)}) collective-permute-start(bf16[256,768]{1,0:T(8,128)(2,1)S(1)} %slice.135), channel_id=1, source_target_pairs={{0,4},{1,5},{2,6},{3,7},{4,0},{5,1},{6,2},{7,3},{8,12},{9,13},{10,... | collective-permute-start | bytes 1179656 | tf_op jit(solution)/shard_map/ppermute | solution.py:463
  174.4 33.4 %collective-permute-start.24 = (bf16[128,640]{1,0:T(8,128)(2,1)S(1)}, bf16[128,640]{1,0:T(8,128)(2,1)S(1)}, u32[]{:S(2)}, u32[]{:S(2)}) collective-permute-start(bf16[128,640]{1,0:T(8,128)(2,1)S(1)} %slice.139), channel_id=1, source_target_pairs={{0,1},{1,0},{2,3},{3,2},{4,5},{5,4},{6,7},{7,6},{8,9},{9,8},{10,11... | collective-permute-start | bytes 491528 | tf_op jit(solution)/shard_map/ppermute | solution.py:463
  196.4 11.4 %collective-permute-start.23 = (bf16[128,768]{1,0:T(8,128)(2,1)S(1)}, bf16[128,768]{1,0:T(8,128)(2,1)S(1)}, u32[]{:S(2)}, u32[]{:S(2)}) collective-permute-start(bf16[128,768]{1,0:T(8,128)(2,1)S(1)} %slice.137), channel_id=1, source_target_pairs={{0,4},{1,5},{2,6},{3,7},{4,0},{5,1},{6,2},{7,3},{8,12},{9,13},{10,... | collective-permute-start | bytes 589832 | tf_op jit(solution)/shard_map/ppermute | solution.py:463
  198.8 9.0 %collective-permute-start.22 = (bf16[128,768]{1,0:T(8,128)(2,1)S(1)}, bf16[128,768]{1,0:T(8,128)(2,1)S(1)}, u32[]{:S(2)}, u32[]{:S(2)}) collective-permute-start(bf16[128,768]{1,0:T(8,128)(2,1)S(1)} %slice.138), channel_id=1, source_target_pairs={{0,16},{1,17},{2,18},{3,19},{4,20},{5,21},{6,22},{7,23},{8,24},{9,... | collective-permute-start | bytes 589832 | tf_op jit(solution)/shard_map/ppermute | solution.py:463
  (21 other events, 223.0 us)

commit v3 on v1

--- a/solution.py
+++ b/solution.py
@@ -526,22 +526,23 @@
     found_other = select_call(1, spot, arrived, gathered)
     fetched_theirs = cube_exchange(found_other)
     (arrived,) = after([found_other], [arrived])
+    halves = [partial_call(chunk, spot, arrived, row_count) for chunk in range(len(ORDERS))]
+    (arrived,) = after([keep for keep, _ in halves], [arrived])
     found = select_call(0, spot, arrived, gathered)
-    (arrived,) = after([found], [arrived])
-    halves = [partial_call(chunk, spot, arrived, row_count) for chunk in range(len(ORDERS))]
-    (fetched_theirs,) = after([keep for keep, _ in halves], [fetched_theirs])
-    (found,) = after([fetched_theirs], [found])
+    received = [swap(send, order[2]) for (_, send), order in zip(halves, ORDERS)]
+    received = after([found], received)
+    half = CUBE // 4 * row_count
+    totals = [keep + other.astype(jnp.float32) for (keep, _), other in zip(halves, received)]
+    halves = [(total[:half], total[half:].astype(jnp.bfloat16)) for total in totals]
+    received = [swap(send, order[1]) for (_, send), order in zip(halves, ORDERS)]
+    (found,) = after([fetched_theirs, *received], [found])
     fetched = cube_exchange(found)
     fetched_other = swap_cores(fetched_theirs)
 
-    received = [swap(send, order[2]) for (_, send), order in zip(halves, ORDERS)]
-    half = CUBE // 4 * row_count
-    for step in (1, 0):
-        totals = [keep + other.astype(jnp.float32) for (keep, _), other in zip(halves, received)]
-        halves = [(total[:half], total[half:].astype(jnp.bfloat16)) for total in totals]
-        received = [swap(send, order[step]) for (_, send), order in zip(halves, ORDERS)]
-        half //= 2
-    (fetched_other,) = after([send for _, send in halves], [fetched_other])
+    half //= 2
+    totals = [keep + other.astype(jnp.float32) for (keep, _), other in zip(halves, received)]
+    halves = [(total[:half], total[half:].astype(jnp.bfloat16)) for total in totals]
+    received = [swap(send, order[0]) for (_, send), order in zip(halves, ORDERS)]
     layer_out, gate_grad, score = read_call(which, packed, fetched_other, gate_pre, out_grad)
     received = after([score], received)
     totals = [keep + other.astype(jnp.float32) for (keep, _), other in zip(halves, received)]

time: 231 us -> 243 us (1.052)
  blocking collectives: 0 us -> 31.6 us
  waiting for transfers between devices: 98.8 us -> 74.2 us
  local copies, waits for them, and re-layouts: 8.84 us -> 13.1 us
    all_to_all x0 -> x1, blocking collectives: none -> 31.6 us  [cube_exchange(): lax.all_to_all(x, ('batch', 'table'), split_axis=0, concat_axis=0, axis_i...]
    all_to_all x3 -> x2, waiting for transfers between devices: 20.8 us -> 7.24 us  [cube_exchange(): lax.all_to_all(x, ('batch', 'table'), split_axis=0, concat_axis=0, axis_i...]
    ppermute x18, waiting for transfers between devices: 76.7 us -> 65.6 us  [swap(): return lax.ppermute(x, ('batch', 'table'), pairs)]
    all_to_all x3 -> x2, starting transfers between devices: 14.3 us -> 9.6 us  [cube_exchange(): lax.all_to_all(x, ('batch', 'table'), split_axis=0, concat_axis=0, axis_i...]
    unnamed x35 -> x57, local copies, waits for them, and re-layouts: 5.24 us -> 8.79 us
  transfers between devices with their start and end apart: 26 -> 25, of which waited for: 8 -> 8; matrix products, arithmetic and copies ran while one was open for 6% -> 7% of each run, Pallas kernels for 22% -> 21%
where the time goes in v3:
time: 243 us; the launch traced here: 242 us
  waiting for transfers between devices  74.2 us (31%)
  Pallas kernels  64 us (26%)
  starting transfers between devices  47.2 us (19%)
  blocking collectives  31.6 us (13%)
  local copies, waits for them, and re-layouts  13.1 us (5%)
  other arithmetic  10.7 us (4%)
    ppermute x18, waiting for transfers between devices, swap(): return lax.ppermute(x, ('batch', 'table'), pairs)  65.6 us
    all_to_all x1, blocking collectives, cube_exchange(): lax.all_to_all(x, ('batch', 'table'), split_axis=0, concat_axis=0, axis_i...  31.6 us
    ppermute x18, starting transfers between devices, swap(): return lax.ppermute(x, ('batch', 'table'), pairs)  28.6 us
    pallas_call x2, Pallas kernels, read_call(): pl.pallas_call(functools.partial(read_kernel, own), grid_spec=pltpu.Prefe...  15.8 us
    pallas_call x3, Pallas kernels, partial_call(): pl.pallas_call(functools.partial(partial_kernel, chunk), grid=(1,), in_sp...  11.7 us
    pallas_call x2, Pallas kernels, select_call(): pl.pallas_call(functools.partial(select_kernel, group), grid=(len(ORDERS)...  11.3 us
    all_to_all x2, starting transfers between devices, cube_exchange(): lax.all_to_all(x, ('batch', 'table'), split_axis=0, concat_axis=0, axis_i...  9.6 us
    ppermute x5, starting transfers between devices, swap_cores(): return lax.ppermute(x, 'batch', [(0, 1), (1, 0)])  8.99 us
  transfers between devices with their start and end apart: 25, of which 8 were waited for; matrix products, arithmetic and copies ran while one was open for 7% of the time, Pallas kernels for 21%

profile of v3, /device:TPU:1, one launch (start us, length us, event | category | flops | bytes accessed | tf_op | source)
XLA Modules:
  0.0 242.1 jit_solution(14376165915700624142)
XLA Ops:
  3.8 3.9 %collective-permute-start.2 = (bf16[128,512]{1,0:T(8,128)(2,1)S(1)}, bf16[128,512]{1,0:T(8,128)(2,1)S(1)}, u32[]{:S(2)}, u32[]{:S(2)}) collective-permute-start(bf16[128,512]{1,0:T(8,128)(2,1)S(1)} %constant_dynamic-slice_fusion.2), channel_id=1, source_target_pairs={{0,1},{1,0},{2,3},{3,2},{4,5},{5,4},{6,7},{7,6},{8,9},{9,8},{10,11... | collective-permute-start | bytes 393224 | tf_op jit(solution)/shard_map/ppermute | solution.py:454
  11.3 2.7 %collective-permute-start = (bf16[128,768]{1,0:T(8,128)(2,1)S(1)}, bf16[128,768]{1,0:T(8,128)(2,1)S(1)}, u32[]{:S(2)}, u32[]{:S(2)}) collective-permute-start(bf16[128,768]{1,0:T(8,128)(2,1)S(1)} %get-tuple-element.83), channel_id=1, source_target_pairs={{0,16},{1,17},{2,18},{3,19},{4,20},{5,21},{6,22},{7,23},{8,24},{9,... | collective-permute-start | bytes 589832 | tf_op jit(solution)/shard_map/ppermute | solution.py:454
  14.1 4.4 %gated_halves.1 = (bf16[256,2048]{1,0:T(8,128)(2,1)}, bf16[256,2048]{1,0:T(8,128)(2,1)}) custom-call(s32[1]{0:T(128)} %bitcast.core_ref, bf16[256,4096]{1,0:T(8,128)(2,1)} %gate_ref.3, bf16[256,4096]{1,0:T(8,128)(2,1)} %grad_ref.3, bf16[256,4096]{1,0:T(8,128)(2,1)} %gate_ref.3, bf16[256,4096]{1,0:T(8,128)(2,1)} %grad_ref.3), custom_call_target="tpu_custom_call" | custom-call | flops 4194304 | bytes 6291456 | tf_op jit(solution)/shard_map/gated_halves/pallas_call | solution.py:93
  22.5 5.7 %pack_weights.1 = (bf16[256,1024]{1,0:T(8,128)(2,1)}, f32[256,32]{1,0:T(8,128)}) custom-call(f32[256,32]{1,0:T(8,128)} %copy.27.logit_ref, s32[256,32]{1,0:T(8,128)} %fusion.1.slot_ref), custom_call_target="tpu_custom_call" | custom-call | flops 33554432 | bytes 1048576 | tf_op jit(solution)/shard_map/pack_weights/pallas_call | solution.py:66
  32.9 7.2 %slot_gradients.1 = bf16[2048,2176]{1,0:T(8,128)(2,1)} custom-call(s32[1]{0:T(128)} %bitcast.core_ref, f32[16,128]{1,0:T(8,128)} %convert_element_type.42.list_ref, bf16[256,1024]{1,0:T(8,128)(2,1)} %get-tuple-element.49.packed_ref, bf16[256,1024]{1,0:T(8,128)(2,1)} %copy-done.19, bf16[256,2048]{1,0:T(8,128)(2,1)} %get-tuple-element.44.gated_ref, ...), custom_call_target="tpu_custom_call" | custom-call | flops 2147483648 | bytes 14680064 | tf_op jit(solution)/shard_map/slot_gradients/pallas_call | solution.py:146
  40.8 5.0 %all-to-all-start = ((bf16[8,256,2176]{2,1,0:T(8,128)(2,1)}), bf16[8,256,2176]{2,1,0:T(8,128)(2,1)}, u32[]{:S(2)}, u32[]{:S(2)}) async-start(bf16[8,256,2176]{2,1,0:T(8,128)(2,1)} %bitcast.19), calls=%async_computation | async-start | bytes 17825792 | tf_op jit(solution)/shard_map/all_to_all | solution.py:471
  48.6 2.7 %collective-permute-start.9 = (bf16[512,768]{1,0:T(8,128)(2,1)S(1)}, bf16[512,768]{1,0:T(8,128)(2,1)}, u32[]{:S(2)}, u32[]{:S(2)}) collective-permute-start(bf16[512,768]{1,0:T(8,128)(2,1)S(1)} %pad_maximum_fusion.1.refs_0_), channel_id=1, source_target_pairs={{0,1},{1,0},{2,3},{3,2},{4,5},{5,4},{6,7},{7,6},{8,9},{9,8},{10,11... | collective-permute-start | bytes 2359304 | tf_op jit(solution)/shard_map/ppermute | solution.py:454
  54.8 12.9 %collective-permute-done.11.refs_5_ = bf16[512,512]{1,0:T(8,128)(2,1)S(1)} collective-permute-done((bf16[512,512]{1,0:T(8,128)(2,1)S(1)}, bf16[512,512]{1,0:T(8,128)(2,1)S(1)}, u32[]{:S(2)}, u32[]{:S(2)}) %collective-permute-start.11) | collective-permute-done | bytes 524320 | tf_op jit(solution)/shard_map/ppermute | solution.py:454
  68.0 34.8 %collective-permute-done.9.refs_1_ = bf16[512,768]{1,0:T(8,128)(2,1)} collective-permute-done((bf16[512,768]{1,0:T(8,128)(2,1)S(1)}, bf16[512,768]{1,0:T(8,128)(2,1)}, u32[]{:S(2)}, u32[]{:S(2)}) %collective-permute-start.9) | collective-permute-done | bytes 786464 | tf_op jit(solution)/shard_map/ppermute | solution.py:454
  102.8 7.2 %all-to-all-done = bf16[8,256,2176]{2,1,0:T(8,128)(2,1)} async-done(((bf16[8,256,2176]{2,1,0:T(8,128)(2,1)}), bf16[8,256,2176]{2,1,0:T(8,128)(2,1)}, u32[]{:S(2)}, u32[]{:S(2)}) %all-to-all-start) | async-done | bytes 8912928 | tf_op jit(solution)/shard_map/all_to_all | solution.py:471
  110.1 5.6 %select_rows.2 = bf16[1024,2048]{1,0:T(8,128)(2,1)} custom-call(s32[1]{0:T(128)} %bitcast.1.spot_ref, bf16[2048,2176]{1,0:T(8,128)(2,1)} %bitcast.11.id_ref.arrived_ref, bf16[512,768]{1,0:T(8,128)(2,1)} %copy-done.1, bf16[512,768]{1,0:T(8,128)(2,1)} %collective-permute-done.9.refs_1_, bf16[512,768]{1,0:T(8,128)(2,1)} %copy-done.2, ...), custom_call_target="tpu_custom_call" | custom-call | flops 570425344 | bytes 13369344 | tf_op jit(solution)/shard_map/select_rows/pallas_call | solution.py:212
  115.7 31.6 %all_to_all.36 = bf16[8,128,2048]{2,1,0:T(8,128)(2,1)} all-to-all(bf16[8,128,2048]{2,1,0:T(8,128)(2,1)} %bitcast.21), channel_id=1, replica_groups={{0,3,12,15,48,51,60,63},{1,2,13,14,49,50,61,62},{4,7,8,11,52,55,56,59},..., dimensions={0} | all-to-all | bytes 8388608 | tf_op jit(solution)/shard_map/all_to_all | solution.py:471
  147.3 6.9 %collective-permute-start.16 = (bf16[1024,2048]{1,0:T(8,128)(2,1)}, bf16[1024,2048]{1,0:T(8,128)(2,1)}, u32[]{:S(2)}, u32[]{:S(2)}) collective-permute-start(bf16[1024,2048]{1,0:T(8,128)(2,1)} %bitcast.13), channel_id=1, source_target_pairs={{0,64},{64,0},{1,65},{65,1},{2,66},{66,2},{3,67},{67,3},{4,68},{68... | collective-permute-start | bytes 12582920 | tf_op jit(solution)/shard_map/ppermute | solution.py:458
  154.2 4.0 %partial_sums.4 = (f32[512,768]{1,0:T(8,128)}, bf16[512,768]{1,0:T(8,128)(2,1)}) custom-call(s32[1]{0:T(128)} %bitcast.1.spot_ref, bf16[2048,2176]{1,0:T(8,128)(2,1)} %bitcast.11.id_ref.arrived_ref, bf16[2048,2176]{1,0:T(8,128)(2,1)} %bitcast.11.id_ref.arrived_ref), custom_call_target="tpu_custom_call" | custom-call | flops 402653184 | bytes 12582912 | tf_op jit(solution)/shard_map/partial_sums/pallas_call | solution.py:256
  158.5 3.9 %partial_sums.3 = (f32[512,768]{1,0:T(8,128)}, bf16[512,768]{1,0:T(8,128)(2,1)}) custom-call(s32[1]{0:T(128)} %bitcast.1.spot_ref, bf16[2048,2176]{1,0:T(8,128)(2,1)} %bitcast.11.id_ref.arrived_ref, bf16[2048,2176]{1,0:T(8,128)(2,1)} %bitcast.11.id_ref.arrived_ref), custom_call_target="tpu_custom_call" | custom-call | flops 402653184 | bytes 12582912 | tf_op jit(solution)/shard_map/partial_sums/pallas_call | solution.py:256
  162.5 3.8 %partial_sums.5 = (f32[512,640]{1,0:T(8,128)}, bf16[512,640]{1,0:T(8,128)(2,1)}) custom-call(s32[1]{0:T(128)} %bitcast.1.spot_ref, bf16[2048,2176]{1,0:T(8,128)(2,1)} %bitcast.11.id_ref.arrived_ref, bf16[2048,2176]{1,0:T(8,128)(2,1)} %bitcast.11.id_ref.arrived_ref), custom_call_target="tpu_custom_call" | custom-call | flops 335544320 | bytes 10485760 | tf_op jit(solution)/shard_map/partial_sums/pallas_call | solution.py:256
  166.8 5.7 %select_rows.3 = bf16[1024,2048]{1,0:T(8,128)(2,1)} custom-call(s32[1]{0:T(128)} %bitcast.1.spot_ref, bf16[2048,2176]{1,0:T(8,128)(2,1)} %bitcast.11.id_ref.arrived_ref, bf16[512,768]{1,0:T(8,128)(2,1)} %copy-done.1, bf16[512,768]{1,0:T(8,128)(2,1)} %collective-permute-done.9.refs_1_, bf16[512,768]{1,0:T(8,128)(2,1)} %copy-done.2, ...), custom_call_target="tpu_custom_call" | custom-call | flops 570425344 | bytes 13369344 | tf_op jit(solution)/shard_map/select_rows/pallas_call | solution.py:212
  172.5 4.6 %collective-permute-done.14 = bf16[512,640]{1,0:T(8,128)(2,1)S(1)} collective-permute-done((bf16[512,640]{1,0:T(8,128)(2,1)}, bf16[512,640]{1,0:T(8,128)(2,1)S(1)}, u32[]{:S(2)}, u32[]{:S(2)}) %collective-permute-start.14) | collective-permute-done | bytes 655392 | tf_op jit(solution)/shard_map/ppermute | solution.py:454
  187.4 4.9 %collective-permute-done.20 = bf16[256,640]{1,0:T(8,128)(2,1)S(1)} collective-permute-done((bf16[256,640]{1,0:T(8,128)(2,1)S(1)}, bf16[256,640]{1,0:T(8,128)(2,1)S(1)}, u32[]{:S(2)}, u32[]{:S(2)}) %collective-permute-start.20) | collective-permute-done | bytes 327712 | tf_op jit(solution)/shard_map/ppermute | solution.py:454
  193.2 4.6 %all-to-all-start.2 = ((bf16[8,128,2048]{2,1,0:T(8,128)(2,1)}), bf16[8,128,2048]{2,1,0:T(8,128)(2,1)}, u32[]{:S(2)}, u32[]{:S(2)}) async-start(bf16[8,128,2048]{2,1,0:T(8,128)(2,1)} %bitcast.20), calls=%async_computation.2 | async-start | bytes 8388608 | tf_op jit(solution)/shard_map/all_to_all | solution.py:471
  205.1 7.4 %read_and_scores.2 = (bf16[256,4096]{1,0:T(8,128)(2,1)}, bf16[256,4096]{1,0:T(8,128)(2,1)}, f32[256,1024]{1,0:T(8,128)}) custom-call(s32[1]{0:T(128)} %bitcast.core_ref, bf16[256,1024]{1,0:T(8,128)(2,1)} %get-tuple-element.49.packed_ref, bf16[1024,2048]{1,0:T(8,128)(2,1)} %collective-permute-done.16.fetched_ref, bf16[256,4096]{1,0:T(8,128)(2,1)} %gate_ref.3, ...), custom_call_target="tpu_custom_call" | custom-call | flops 2147483648 | bytes 9437184 | tf_op jit(solution)/shard_map/read_and_scores/pallas_call | solution.py:416
  212.6 8.0 %collective-permute-done.21 = bf16[128,640]{1,0:T(8,128)(2,1)} collective-permute-done((bf16[128,640]{1,0:T(8,128)(2,1)}, bf16[128,640]{1,0:T(8,128)(2,1)}, u32[]{:S(2)}, u32[]{:S(2)}) %collective-permute-start.21) | collective-permute-done | bytes 163872 | tf_op jit(solution)/shard_map/ppermute | solution.py:454
  225.6 8.0 %adam_rows.1 = (bf16[128,4096]{1,0:T(8,128)(2,1)}, f32[128,4096]{1,0:T(8,128)}, f32[128,4096]{1,0:T(8,128)}) custom-call(s32[1]{0:T(128)} %bitcast.core_ref, f32[128,2176]{1,0:T(8,128)} %copy-done, f32[128,2176]{1,0:T(8,128)} %copy-done, f32[128,2176]{1,0:T(8,128)} %copy-done.15, bf16[128,4096]{1,0:T(8,128)(2,1)} %value_ref.1, f32[128,4096]{1,0:T(8,128)} %first_ref.1, ...), custom_call_target="tpu_custom_call" | custom-call | flops 5242880 | bytes 14680064 | tf_op jit(solution)/shard_map/adam_rows/pallas_call | solution.py:302
  233.6 8.4 %read_and_scores.3 = (bf16[256,4096]{1,0:T(8,128)(2,1)}, bf16[256,4096]{1,0:T(8,128)(2,1)}, f32[32,256]{1,0:T(8,128)}) custom-call(s32[1]{0:T(128)} %bitcast.core_ref, bf16[256,1024]{1,0:T(8,128)(2,1)} %get-tuple-element.49.packed_ref, bf16[1024,2048]{1,0:T(8,128)(2,1)} %bitcast.15.fetched_ref, ...), custom_call_target="tpu_custom_call", output_to_operand_aliasing={{0}: (8, {}), {1}: (9, {})} | custom-call | flops 2147483648 | bytes 9437184 | tf_op jit(solution)/shard_map/read_and_scores/pallas_call | solution.py:416
  (131 shorter events, 47.0 us)
Async XLA Ops:
  1.4 18.7 %collective-permute-start.3 = (s32[16,64]{0,1:T(8,128)S(1)}, s32[16,64]{0,1:T(8,128)S(1)}, u32[]{:S(2)}, u32[]{:S(2)}) collective-permute-start(s32[16,64]{0,1:T(8,128)S(1)} %copy.28), channel_id=1, source_target_pairs={{0,64},{64,0},{1,65},{65,1},{2,66},{66,2},{3,67},{67,3},{4,68},{68... | collective-permute-start | bytes 12296 | tf_op jit(solution)/shard_map/ppermute | solution.py:458
  3.8 16.4 %collective-permute-start.2 = (bf16[128,512]{1,0:T(8,128)(2,1)S(1)}, bf16[128,512]{1,0:T(8,128)(2,1)S(1)}, u32[]{:S(2)}, u32[]{:S(2)}) collective-permute-start(bf16[128,512]{1,0:T(8,128)(2,1)S(1)} %constant_dynamic-slice_fusion.2), channel_id=1, source_target_pairs={{0,1},{1,0},{2,3},{3,2},{4,5},{5,4},{6,7},{7,6},{8,9},{9,8},{10,11... | collective-permute-start | bytes 393224 | tf_op jit(solution)/shard_map/ppermute | solution.py:454
  8.8 11.4 %collective-permute-start.1 = (bf16[128,768]{1,0:T(8,128)(2,1)S(1)}, bf16[128,768]{1,0:T(8,128)(2,1)S(1)}, u32[]{:S(2)}, u32[]{:S(2)}) collective-permute-start(bf16[128,768]{1,0:T(8,128)(2,1)S(1)} %get-tuple-element.82), channel_id=1, source_target_pairs={{0,4},{1,5},{2,6},{3,7},{4,0},{5,1},{6,2},{7,3},{8,12},{9,13},{10,... | collective-permute-start | bytes 589832 | tf_op jit(solution)/shard_map/ppermute | solution.py:454
  11.3 8.9 %collective-permute-start = (bf16[128,768]{1,0:T(8,128)(2,1)S(1)}, bf16[128,768]{1,0:T(8,128)(2,1)S(1)}, u32[]{:S(2)}, u32[]{:S(2)}) collective-permute-start(bf16[128,768]{1,0:T(8,128)(2,1)S(1)} %get-tuple-element.83), channel_id=1, source_target_pairs={{0,16},{1,17},{2,18},{3,19},{4,20},{5,21},{6,22},{7,23},{8,24},{9,... | collective-permute-start | bytes 589832 | tf_op jit(solution)/shard_map/ppermute | solution.py:454
  18.4 12.7 %collective-permute-start.5 = (bf16[256,2048]{1,0:T(8,128)(2,1)}, bf16[256,2048]{1,0:T(8,128)(2,1)S(1)}, u32[]{:S(2)}, u32[]{:S(2)}) collective-permute-start(bf16[256,2048]{1,0:T(8,128)(2,1)} %get-tuple-element.50), channel_id=1, source_target_pairs={{0,64},{64,0},{1,65},{65,1},{2,66},{66,2},{3,67},{67,3},{4,68},{68... | collective-permute-start | bytes 3145736 | tf_op jit(solution)/shard_map/ppermute | solution.py:458
  28.1 3.0 %collective-permute-start.4 = (bf16[256,1024]{1,0:T(8,128)(2,1)}, bf16[256,1024]{1,0:T(8,128)(2,1)S(1)}, u32[]{:S(2)}, u32[]{:S(2)}) collective-permute-start(bf16[256,1024]{1,0:T(8,128)(2,1)} %get-tuple-element.49.packed_ref), channel_id=1, source_target_pairs={{0,64},{64,0},{1,65},{65,1},{2,66},{66,2},{3,67},{67,3},{4,68},{68... | collective-permute-start | bytes 1572872 | tf_op jit(solution)/shard_map/ppermute | solution.py:458
  28.7 11.3 %collective-permute-start.8 = (bf16[256,512]{1,0:T(8,128)(2,1)}, bf16[256,512]{1,0:T(8,128)(2,1)}, u32[]{:S(2)}, u32[]{:S(2)}) collective-permute-start(bf16[256,512]{1,0:T(8,128)(2,1)} %pad_maximum_fusion.6), channel_id=1, source_target_pairs={{0,16},{1,17},{2,18},{3,19},{4,20},{5,21},{6,22},{7,23},{8,24},{9,... | collective-permute-start | bytes 786440 | tf_op jit(solution)/shard_map/ppermute | solution.py:454
  28.8 11.2 %collective-permute-start.7 = (bf16[256,768]{1,0:T(8,128)(2,1)}, bf16[256,768]{1,0:T(8,128)(2,1)S(1)}, u32[]{:S(2)}, u32[]{:S(2)}) collective-permute-start(bf16[256,768]{1,0:T(8,128)(2,1)} %pad_maximum_fusion.5), channel_id=1, source_target_pairs={{0,1},{1,0},{2,3},{3,2},{4,5},{5,4},{6,7},{7,6},{8,9},{9,8},{10,11... | collective-permute-start | bytes 1179656 | tf_op jit(solution)/shard_map/ppermute | solution.py:454
  28.9 11.2 %collective-permute-start.6 = (bf16[256,768]{1,0:T(8,128)(2,1)}, bf16[256,768]{1,0:T(8,128)(2,1)}, u32[]{:S(2)}, u32[]{:S(2)}) collective-permute-start(bf16[256,768]{1,0:T(8,128)(2,1)} %pad_maximum_fusion.4), channel_id=1, source_target_pairs={{0,4},{1,5},{2,6},{3,7},{4,0},{5,1},{6,2},{7,3},{8,12},{9,13},{10,... | collective-permute-start | bytes 1179656 | tf_op jit(solution)/shard_map/ppermute | solution.py:454
  40.8 69.2 %all-to-all-start = ((bf16[8,256,2176]{2,1,0:T(8,128)(2,1)}), bf16[8,256,2176]{2,1,0:T(8,128)(2,1)}, u32[]{:S(2)}, u32[]{:S(2)}) async-start(bf16[8,256,2176]{2,1,0:T(8,128)(2,1)} %bitcast.19), calls=%async_computation | async-start | bytes 17825792 | tf_op jit(solution)/shard_map/all_to_all | solution.py:471
  47.1 21.0 %collective-permute-start.10 = (bf16[512,768]{1,0:T(8,128)(2,1)S(1)}, bf16[512,768]{1,0:T(8,128)(2,1)S(1)}, u32[]{:S(2)}, u32[]{:S(2)}) collective-permute-start(bf16[512,768]{1,0:T(8,128)(2,1)S(1)} %pad_maximum_fusion.2.refs_2_), channel_id=1, source_target_pairs={{0,16},{1,17},{2,18},{3,19},{4,20},{5,21},{6,22},{7,23},{8,24},{9,... | collective-permute-start | bytes 2359304 | tf_op jit(solution)/shard_map/ppermute | solution.py:454
  48.6 54.3 %collective-permute-start.9 = (bf16[512,768]{1,0:T(8,128)(2,1)S(1)}, bf16[512,768]{1,0:T(8,128)(2,1)}, u32[]{:S(2)}, u32[]{:S(2)}) collective-permute-start(bf16[512,768]{1,0:T(8,128)(2,1)S(1)} %pad_maximum_fusion.1.refs_0_), channel_id=1, source_target_pairs={{0,1},{1,0},{2,3},{3,2},{4,5},{5,4},{6,7},{7,6},{8,9},{9,8},{10,11... | collective-permute-start | bytes 2359304 | tf_op jit(solution)/shard_map/ppermute | solution.py:454
  52.2 15.4 %collective-permute-start.11 = (bf16[512,512]{1,0:T(8,128)(2,1)S(1)}, bf16[512,512]{1,0:T(8,128)(2,1)S(1)}, u32[]{:S(2)}, u32[]{:S(2)}) collective-permute-start(bf16[512,512]{1,0:T(8,128)(2,1)S(1)} %pad_maximum_fusion.3.refs_4_), channel_id=1, source_target_pairs={{0,4},{1,5},{2,6},{3,7},{4,0},{5,1},{6,2},{7,3},{8,12},{9,13},{10,... | collective-permute-start | bytes 1572872 | tf_op jit(solution)/shard_map/ppermute | solution.py:454
  147.3 57.8 %collective-permute-start.16 = (bf16[1024,2048]{1,0:T(8,128)(2,1)}, bf16[1024,2048]{1,0:T(8,128)(2,1)}, u32[]{:S(2)}, u32[]{:S(2)}) collective-permute-start(bf16[1024,2048]{1,0:T(8,128)(2,1)} %bitcast.13), channel_id=1, source_target_pairs={{0,64},{64,0},{1,65},{65,1},{2,66},{66,2},{3,67},{67,3},{4,68},{68... | collective-permute-start | bytes 12582920 | tf_op jit(solution)/shard_map/ppermute | solution.py:458
  158.2 18.9 %collective-permute-start.13 = (bf16[512,768]{1,0:T(8,128)(2,1)}, bf16[512,768]{1,0:T(8,128)(2,1)}, u32[]{:S(2)}, u32[]{:S(2)}) collective-permute-start(bf16[512,768]{1,0:T(8,128)(2,1)} %get-tuple-element.62), channel_id=1, source_target_pairs={{0,16},{1,17},{2,18},{3,19},{4,20},{5,21},{6,22},{7,23},{8,24},{9,... | collective-permute-start | bytes 2359304 | tf_op jit(solution)/shard_map/ppermute | solution.py:454
  162.4 15.5 %collective-permute-start.12 = (bf16[512,768]{1,0:T(8,128)(2,1)}, bf16[512,768]{1,0:T(8,128)(2,1)}, u32[]{:S(2)}, u32[]{:S(2)}) collective-permute-start(bf16[512,768]{1,0:T(8,128)(2,1)} %get-tuple-element.61), channel_id=1, source_target_pairs={{0,1},{1,0},{2,3},{3,2},{4,5},{5,4},{6,7},{7,6},{8,9},{9,8},{10,11... | collective-permute-start | bytes 2359304 | tf_op jit(solution)/shard_map/ppermute | solution.py:454
  166.3 10.9 %collective-permute-start.14 = (bf16[512,640]{1,0:T(8,128)(2,1)}, bf16[512,640]{1,0:T(8,128)(2,1)S(1)}, u32[]{:S(2)}, u32[]{:S(2)}) collective-permute-start(bf16[512,640]{1,0:T(8,128)(2,1)} %get-tuple-element.63), channel_id=1, source_target_pairs={{0,4},{1,5},{2,6},{3,7},{4,0},{5,1},{6,2},{7,3},{8,12},{9,13},{10,... | collective-permute-start | bytes 1966088 | tf_op jit(solution)/shard_map/ppermute | solution.py:454
  180.9 11.5 %collective-permute-start.15 = (bf16[256,768]{1,0:T(8,128)(2,1)S(1)}, bf16[256,768]{1,0:T(8,128)(2,1)S(1)}, u32[]{:S(2)}, u32[]{:S(2)}) collective-permute-start(bf16[256,768]{1,0:T(8,128)(2,1)S(1)} %slice.135), channel_id=1, source_target_pairs={{0,4},{1,5},{2,6},{3,7},{4,0},{5,1},{6,2},{7,3},{8,12},{9,13},{10,... | collective-permute-start | bytes 1179656 | tf_op jit(solution)/shard_map/ppermute | solution.py:454
  181.5 10.8 %collective-permute-start.18 = (bf16[256,768]{1,0:T(8,128)(2,1)S(1)}, bf16[256,768]{1,0:T(8,128)(2,1)S(1)}, u32[]{:S(2)}, u32[]{:S(2)}) collective-permute-start(bf16[256,768]{1,0:T(8,128)(2,1)S(1)} %slice.134), channel_id=1, source_target_pairs={{0,1},{1,0},{2,3},{3,2},{4,5},{5,4},{6,7},{7,6},{8,9},{9,8},{10,11... | collective-permute-start | bytes 1179656 | tf_op jit(solution)/shard_map/ppermute | solution.py:454
  185.1 7.2 %collective-permute-start.20 = (bf16[256,640]{1,0:T(8,128)(2,1)S(1)}, bf16[256,640]{1,0:T(8,128)(2,1)S(1)}, u32[]{:S(2)}, u32[]{:S(2)}) collective-permute-start(bf16[256,640]{1,0:T(8,128)(2,1)S(1)} %slice.136), channel_id=1, source_target_pairs={{0,16},{1,17},{2,18},{3,19},{4,20},{5,21},{6,22},{7,23},{8,24},{9,... | collective-permute-start | bytes 983048 | tf_op jit(solution)/shard_map/ppermute | solution.py:454
  193.2 40.4 %all-to-all-start.2 = ((bf16[8,128,2048]{2,1,0:T(8,128)(2,1)}), bf16[8,128,2048]{2,1,0:T(8,128)(2,1)}, u32[]{:S(2)}, u32[]{:S(2)}) async-start(bf16[8,128,2048]{2,1,0:T(8,128)(2,1)} %bitcast.20), calls=%async_computation.2 | async-start | bytes 8388608 | tf_op jit(solution)/shard_map/all_to_all | solution.py:471
  200.0 20.6 %collective-permute-start.21 = (bf16[128,640]{1,0:T(8,128)(2,1)}, bf16[128,640]{1,0:T(8,128)(2,1)}, u32[]{:S(2)}, u32[]{:S(2)}) collective-permute-start(bf16[128,640]{1,0:T(8,128)(2,1)} %slice.139), channel_id=1, source_target_pairs={{0,1},{1,0},{2,3},{3,2},{4,5},{5,4},{6,7},{7,6},{8,9},{9,8},{10,11... | collective-permute-start | bytes 491528 | tf_op jit(solution)/shard_map/ppermute | solution.py:454
  200.3 20.2 %collective-permute-start.17 = (bf16[128,768]{1,0:T(8,128)(2,1)S(1)}, bf16[128,768]{1,0:T(8,128)(2,1)S(1)}, u32[]{:S(2)}, u32[]{:S(2)}) collective-permute-start(bf16[128,768]{1,0:T(8,128)(2,1)S(1)} %slice.138), channel_id=1, source_target_pairs={{0,16},{1,17},{2,18},{3,19},{4,20},{5,21},{6,22},{7,23},{8,24},{9,... | collective-permute-start | bytes 589832 | tf_op jit(solution)/shard_map/ppermute | solution.py:454
  202.9 17.6 %collective-permute-start.19 = (bf16[128,768]{1,0:T(8,128)(2,1)S(1)}, bf16[128,768]{1,0:T(8,128)(2,1)S(1)}, u32[]{:S(2)}, u32[]{:S(2)}) collective-permute-start(bf16[128,768]{1,0:T(8,128)(2,1)S(1)} %slice.137), channel_id=1, source_target_pairs={{0,4},{1,5},{2,6},{3,7},{4,0},{5,1},{6,2},{7,3},{8,12},{9,13},{10,... | collective-permute-start | bytes 589832 | tf_op jit(solution)/shard_map/ppermute | solution.py:454
  (28 other events, 362.0 us)

commit v4 on v3

--- a/solution.py
+++ b/solution.py
@@ -535,6 +535,7 @@
     totals = [keep + other.astype(jnp.float32) for (keep, _), other in zip(halves, received)]
     halves = [(total[:half], total[half:].astype(jnp.bfloat16)) for total in totals]
     received = [swap(send, order[1]) for (_, send), order in zip(halves, ORDERS)]
+    (fetched_theirs,) = after([send for _, send in halves], [fetched_theirs])
     (found,) = after([fetched_theirs, *received], [found])
     fetched = cube_exchange(found)
     fetched_other = swap_cores(fetched_theirs)

time: 243 us -> 225 us (0.926)
  blocking collectives: 31.6 us -> 0 us
  waiting for transfers between devices: 74.2 us -> 83.5 us
  starting transfers between devices: 47.2 us -> 52.8 us
  other arithmetic: 10.7 us -> 7.3 us
    all_to_all x1 -> x0, blocking collectives: 31.6 us -> none  [cube_exchange(): lax.all_to_all(x, ('batch', 'table'), split_axis=0, concat_axis=0, axis_i...]
    ppermute x18, waiting for transfers between devices: 65.6 us -> 74.9 us  [swap(): return lax.ppermute(x, ('batch', 'table'), pairs)]
    ppermute x18, starting transfers between devices: 28.6 us -> 33.5 us  [swap(): return lax.ppermute(x, ('batch', 'table'), pairs)]
    all_to_all x2 -> x3, starting transfers between devices: 9.6 us -> 14.3 us  [cube_exchange(): lax.all_to_all(x, ('batch', 'table'), split_axis=0, concat_axis=0, axis_i...]
    ppermute x5, starting transfers between devices: 8.99 us -> 5.02 us  [swap_cores(): return lax.ppermute(x, 'batch', [(0, 1), (1, 0)])]
    add x8, other arithmetic: 5.29 us -> 1.88 us  [local(): keep + other.astype(jnp.float32)]
    unnamed x57 -> x63, local copies, waits for them, and re-layouts: 8.79 us -> 9.99 us
    all_to_all x2 -> x3, waiting for transfers between devices: 7.24 us -> 7.25 us  [cube_exchange(): lax.all_to_all(x, ('batch', 'table'), split_axis=0, concat_axis=0, axis_i...]
  transfers between devices with their start and end apart: 25 -> 26, of which waited for: 8 -> 10; matrix products, arithmetic and copies ran while one was open for 7% -> 6% of each run, Pallas kernels for 21% -> 22%
where the time goes in v4:
time: 225 us; the launch traced here: 224 us
  waiting for transfers between devices  83.5 us (37%)
  Pallas kernels  64.1 us (28%)
  starting transfers between devices  52.8 us (23%)
  local copies, waits for them, and re-layouts  15.1 us (7%)
  other arithmetic  7.3 us (3%)
    ppermute x18, waiting for transfers between devices, swap(): return lax.ppermute(x, ('batch', 'table'), pairs)  74.9 us
    ppermute x18, starting transfers between devices, swap(): return lax.ppermute(x, ('batch', 'table'), pairs)  33.5 us
    pallas_call x2, Pallas kernels, read_call(): pl.pallas_call(functools.partial(read_kernel, own), grid_spec=pltpu.Prefe...  15.9 us
    all_to_all x3, starting transfers between devices, cube_exchange(): lax.all_to_all(x, ('batch', 'table'), split_axis=0, concat_axis=0, axis_i...  14.3 us
    pallas_call x3, Pallas kernels, partial_call(): pl.pallas_call(functools.partial(partial_kernel, chunk), grid=(1,), in_sp...  11.7 us
    pallas_call x2, Pallas kernels, select_call(): pl.pallas_call(functools.partial(select_kernel, group), grid=(len(ORDERS)...  11.3 us
    unnamed x63, local copies, waits for them, and re-layouts  9.99 us
    pallas_call x1, Pallas kernels, adam_call(): pl.pallas_call(adam_kernel, grid_spec=pltpu.PrefetchScalarGridSpec(num_sc...  8.04 us
  transfers between devices with their start and end apart: 26, of which 10 were waited for; matrix products, arithmetic and copies ran while one was open for 6% of the time, Pallas kernels for 22%

profile of v4, /device:TPU:1, one launch (start us, length us, event | category | flops | bytes accessed | tf_op | source)
XLA Modules:
  0.0 224.1 jit_solution(4180138356397561331)
XLA Ops:
  3.8 3.9 %collective-permute-start.2 = (bf16[128,512]{1,0:T(8,128)(2,1)S(1)}, bf16[128,512]{1,0:T(8,128)(2,1)S(1)}, u32[]{:S(2)}, u32[]{:S(2)}) collective-permute-start(bf16[128,512]{1,0:T(8,128)(2,1)S(1)} %constant_dynamic-slice_fusion.2), channel_id=1, source_target_pairs={{0,1},{1,0},{2,3},{3,2},{4,5},{5,4},{6,7},{7,6},{8,9},{9,8},{10,11... | collective-permute-start | bytes 393224 | tf_op jit(solution)/shard_map/ppermute | solution.py:454
  14.1 4.4 %gated_halves.1 = (bf16[256,2048]{1,0:T(8,128)(2,1)}, bf16[256,2048]{1,0:T(8,128)(2,1)}) custom-call(s32[1]{0:T(128)} %bitcast.core_ref, bf16[256,4096]{1,0:T(8,128)(2,1)} %gate_ref.3, bf16[256,4096]{1,0:T(8,128)(2,1)} %grad_ref.3, bf16[256,4096]{1,0:T(8,128)(2,1)} %gate_ref.3, bf16[256,4096]{1,0:T(8,128)(2,1)} %grad_ref.3), custom_call_target="tpu_custom_call" | custom-call | flops 4194304 | bytes 6291456 | tf_op jit(solution)/shard_map/gated_halves/pallas_call | solution.py:93
  22.4 5.7 %pack_weights.1 = (bf16[256,1024]{1,0:T(8,128)(2,1)}, f32[256,32]{1,0:T(8,128)}) custom-call(f32[256,32]{1,0:T(8,128)} %copy.27.logit_ref, s32[256,32]{1,0:T(8,128)} %fusion.1.slot_ref), custom_call_target="tpu_custom_call" | custom-call | flops 33554432 | bytes 1048576 | tf_op jit(solution)/shard_map/pack_weights/pallas_call | solution.py:66
  32.9 7.2 %slot_gradients.1 = bf16[2048,2176]{1,0:T(8,128)(2,1)} custom-call(s32[1]{0:T(128)} %bitcast.core_ref, f32[16,128]{1,0:T(8,128)} %convert_element_type.42.list_ref, bf16[256,1024]{1,0:T(8,128)(2,1)} %get-tuple-element.50.packed_ref, bf16[256,1024]{1,0:T(8,128)(2,1)} %copy-done.19, bf16[256,2048]{1,0:T(8,128)(2,1)} %get-tuple-element.45.gated_ref, ...), custom_call_target="tpu_custom_call" | custom-call | flops 2147483648 | bytes 14680064 | tf_op jit(solution)/shard_map/slot_gradients/pallas_call | solution.py:146
  40.8 5.0 %all-to-all-start = ((bf16[8,256,2176]{2,1,0:T(8,128)(2,1)}), bf16[8,256,2176]{2,1,0:T(8,128)(2,1)}, u32[]{:S(2)}, u32[]{:S(2)}) async-start(bf16[8,256,2176]{2,1,0:T(8,128)(2,1)} %bitcast.19), calls=%async_computation | async-start | bytes 17825792 | tf_op jit(solution)/shard_map/all_to_all | solution.py:471
  54.8 12.9 %collective-permute-done.11.refs_5_ = bf16[512,512]{1,0:T(8,128)(2,1)S(1)} collective-permute-done((bf16[512,512]{1,0:T(8,128)(2,1)S(1)}, bf16[512,512]{1,0:T(8,128)(2,1)S(1)}, u32[]{:S(2)}, u32[]{:S(2)}) %collective-permute-start.11) | collective-permute-done | bytes 524320 | tf_op jit(solution)/shard_map/ppermute | solution.py:454
  68.0 34.8 %collective-permute-done.9.refs_1_ = bf16[512,768]{1,0:T(8,128)(2,1)} collective-permute-done((bf16[512,768]{1,0:T(8,128)(2,1)S(1)}, bf16[512,768]{1,0:T(8,128)(2,1)}, u32[]{:S(2)}, u32[]{:S(2)}) %collective-permute-start.9) | collective-permute-done | bytes 786464 | tf_op jit(solution)/shard_map/ppermute | solution.py:454
  102.8 7.2 %all-to-all-done = bf16[8,256,2176]{2,1,0:T(8,128)(2,1)} async-done(((bf16[8,256,2176]{2,1,0:T(8,128)(2,1)}), bf16[8,256,2176]{2,1,0:T(8,128)(2,1)}, u32[]{:S(2)}, u32[]{:S(2)}) %all-to-all-start) | async-done | bytes 8912928 | tf_op jit(solution)/shard_map/all_to_all | solution.py:471
  110.1 5.7 %select_rows.2 = bf16[1024,2048]{1,0:T(8,128)(2,1)} custom-call(s32[1]{0:T(128)} %bitcast.1.spot_ref, bf16[2048,2176]{1,0:T(8,128)(2,1)} %bitcast.11.id_ref.arrived_ref, bf16[512,768]{1,0:T(8,128)(2,1)} %copy-done.1, bf16[512,768]{1,0:T(8,128)(2,1)} %collective-permute-done.9.refs_1_, bf16[512,768]{1,0:T(8,128)(2,1)} %copy-done.2, ...), custom_call_target="tpu_custom_call" | custom-call | flops 570425344 | bytes 13369344 | tf_op jit(solution)/shard_map/select_rows/pallas_call | solution.py:212
  115.7 4.5 %all-to-all-start.1 = ((bf16[8,128,2048]{2,1,0:T(8,128)(2,1)}), bf16[8,128,2048]{2,1,0:T(8,128)(2,1)}, u32[]{:S(2)}, u32[]{:S(2)}) async-start(bf16[8,128,2048]{2,1,0:T(8,128)(2,1)} %bitcast.21), calls=%async_computation.1 | async-start | bytes 8388608 | tf_op jit(solution)/shard_map/all_to_all | solution.py:471
  120.3 4.0 %partial_sums.4 = (f32[512,768]{1,0:T(8,128)}, bf16[512,768]{1,0:T(8,128)(2,1)}) custom-call(s32[1]{0:T(128)} %bitcast.1.spot_ref, bf16[2048,2176]{1,0:T(8,128)(2,1)} %bitcast.11.id_ref.arrived_ref, bf16[2048,2176]{1,0:T(8,128)(2,1)} %bitcast.11.id_ref.arrived_ref), custom_call_target="tpu_custom_call" | custom-call | flops 402653184 | bytes 12582912 | tf_op jit(solution)/shard_map/partial_sums/pallas_call | solution.py:256
  125.1 4.0 %partial_sums.3 = (f32[512,768]{1,0:T(8,128)}, bf16[512,768]{1,0:T(8,128)(2,1)}) custom-call(s32[1]{0:T(128)} %bitcast.1.spot_ref, bf16[2048,2176]{1,0:T(8,128)(2,1)} %bitcast.11.id_ref.arrived_ref, bf16[2048,2176]{1,0:T(8,128)(2,1)} %bitcast.11.id_ref.arrived_ref), custom_call_target="tpu_custom_call" | custom-call | flops 402653184 | bytes 12582912 | tf_op jit(solution)/shard_map/partial_sums/pallas_call | solution.py:256
  129.1 3.1 %collective-permute-start.12 = (bf16[512,768]{1,0:T(8,128)(2,1)}, bf16[512,768]{1,0:T(8,128)(2,1)S(1)}, u32[]{:S(2)}, u32[]{:S(2)}) collective-permute-start(bf16[512,768]{1,0:T(8,128)(2,1)} %get-tuple-element.62), channel_id=1, source_target_pairs={{0,1},{1,0},{2,3},{3,2},{4,5},{5,4},{6,7},{7,6},{8,9},{9,8},{10,11... | collective-permute-start | bytes 2359304 | tf_op jit(solution)/shard_map/ppermute | solution.py:454
  132.1 3.8 %partial_sums.5 = (f32[512,640]{1,0:T(8,128)}, bf16[512,640]{1,0:T(8,128)(2,1)}) custom-call(s32[1]{0:T(128)} %bitcast.1.spot_ref, bf16[2048,2176]{1,0:T(8,128)(2,1)} %bitcast.11.id_ref.arrived_ref, bf16[2048,2176]{1,0:T(8,128)(2,1)} %bitcast.11.id_ref.arrived_ref), custom_call_target="tpu_custom_call" | custom-call | flops 335544320 | bytes 10485760 | tf_op jit(solution)/shard_map/partial_sums/pallas_call | solution.py:256
  138.8 5.7 %select_rows.3 = bf16[1024,2048]{1,0:T(8,128)(2,1)} custom-call(s32[1]{0:T(128)} %bitcast.1.spot_ref, bf16[2048,2176]{1,0:T(8,128)(2,1)} %bitcast.11.id_ref.arrived_ref, bf16[512,768]{1,0:T(8,128)(2,1)} %copy-done.1, bf16[512,768]{1,0:T(8,128)(2,1)} %collective-permute-done.9.refs_1_, bf16[512,768]{1,0:T(8,128)(2,1)} %copy-done.2, ...), custom_call_target="tpu_custom_call" | custom-call | flops 570425344 | bytes 13369344 | tf_op jit(solution)/shard_map/select_rows/pallas_call | solution.py:212
  144.4 9.6 %collective-permute-done.14 = bf16[512,640]{1,0:T(8,128)(2,1)S(1)} collective-permute-done((bf16[512,640]{1,0:T(8,128)(2,1)}, bf16[512,640]{1,0:T(8,128)(2,1)S(1)}, u32[]{:S(2)}, u32[]{:S(2)}) %collective-permute-start.14) | collective-permute-done | bytes 655392 | tf_op jit(solution)/shard_map/ppermute | solution.py:454
  158.7 3.0 %collective-permute-start.16 = (bf16[1024,2048]{1,0:T(8,128)(2,1)}, bf16[1024,2048]{1,0:T(8,128)(2,1)}, u32[]{:S(2)}, u32[]{:S(2)}) collective-permute-start(bf16[1024,2048]{1,0:T(8,128)(2,1)} %bitcast.13), channel_id=1, source_target_pairs={{0,64},{64,0},{1,65},{65,1},{2,66},{66,2},{3,67},{67,3},{4,68},{68... | collective-permute-start | bytes 12582920 | tf_op jit(solution)/shard_map/ppermute | solution.py:458
  161.6 4.0 %collective-permute-start.15 = (bf16[256,768]{1,0:T(8,128)(2,1)}, bf16[256,768]{1,0:T(8,128)(2,1)S(1)}, u32[]{:S(2)}, u32[]{:S(2)}) collective-permute-start(bf16[256,768]{1,0:T(8,128)(2,1)} %slice.135), channel_id=1, source_target_pairs={{0,4},{1,5},{2,6},{3,7},{4,0},{5,1},{6,2},{7,3},{8,12},{9,13},{10,... | collective-permute-start | bytes 1179656 | tf_op jit(solution)/shard_map/ppermute | solution.py:454
  166.9 6.1 %collective-permute-done.20 = bf16[256,640]{1,0:T(8,128)(2,1)S(1)} collective-permute-done((bf16[256,640]{1,0:T(8,128)(2,1)}, bf16[256,640]{1,0:T(8,128)(2,1)S(1)}, u32[]{:S(2)}, u32[]{:S(2)}) %collective-permute-start.20) | collective-permute-done | bytes 327712 | tf_op jit(solution)/shard_map/ppermute | solution.py:454
  174.6 4.7 %all-to-all-start.2 = ((bf16[8,128,2048]{2,1,0:T(8,128)(2,1)}), bf16[8,128,2048]{2,1,0:T(8,128)(2,1)}, u32[]{:S(2)}, u32[]{:S(2)}) async-start(bf16[8,128,2048]{2,1,0:T(8,128)(2,1)} %bitcast.20), calls=%async_computation.2 | async-start | bytes 8388608 | tf_op jit(solution)/shard_map/all_to_all | solution.py:471
  185.6 7.5 %read_and_scores.2 = (bf16[256,4096]{1,0:T(8,128)(2,1)}, bf16[256,4096]{1,0:T(8,128)(2,1)}, f32[256,1024]{1,0:T(8,128)}) custom-call(s32[1]{0:T(128)} %bitcast.core_ref, bf16[256,1024]{1,0:T(8,128)(2,1)} %get-tuple-element.50.packed_ref, bf16[1024,2048]{1,0:T(8,128)(2,1)} %collective-permute-done.16.fetched_ref, bf16[256,4096]{1,0:T(8,128)(2,1)} %gate_ref.3, ...), custom_call_target="tpu_custom_call" | custom-call | flops 2147483648 | bytes 9437184 | tf_op jit(solution)/shard_map/read_and_scores/pallas_call | solution.py:416
  193.1 10.2 %collective-permute-done.21 = bf16[128,640]{1,0:T(8,128)(2,1)S(1)} collective-permute-done((bf16[128,640]{1,0:T(8,128)(2,1)S(1)}, bf16[128,640]{1,0:T(8,128)(2,1)S(1)}, u32[]{:S(2)}, u32[]{:S(2)}) %collective-permute-start.21) | collective-permute-done | bytes 163872 | tf_op jit(solution)/shard_map/ppermute | solution.py:454
  207.5 8.0 %adam_rows.1 = (bf16[128,4096]{1,0:T(8,128)(2,1)}, f32[128,4096]{1,0:T(8,128)}, f32[128,4096]{1,0:T(8,128)}) custom-call(s32[1]{0:T(128)} %bitcast.core_ref, f32[128,2176]{1,0:T(8,128)} %copy-done, f32[128,2176]{1,0:T(8,128)} %copy-done, f32[128,2176]{1,0:T(8,128)} %copy-done.15, bf16[128,4096]{1,0:T(8,128)(2,1)} %value_ref.1, f32[128,4096]{1,0:T(8,128)} %first_ref.1, ...), custom_call_target="tpu_custom_call" | custom-call | flops 5242880 | bytes 14680064 | tf_op jit(solution)/shard_map/adam_rows/pallas_call | solution.py:302
  215.5 8.4 %read_and_scores.3 = (bf16[256,4096]{1,0:T(8,128)(2,1)}, bf16[256,4096]{1,0:T(8,128)(2,1)}, f32[32,256]{1,0:T(8,128)}) custom-call(s32[1]{0:T(128)} %bitcast.core_ref, bf16[256,1024]{1,0:T(8,128)(2,1)} %get-tuple-element.50.packed_ref, bf16[1024,2048]{1,0:T(8,128)(2,1)} %bitcast.15.fetched_ref, ...), custom_call_target="tpu_custom_call", output_to_operand_aliasing={{0}: (8, {}), {1}: (9, {})} | custom-call | flops 2147483648 | bytes 9437184 | tf_op jit(solution)/shard_map/read_and_scores/pallas_call | solution.py:416
  (138 shorter events, 49.7 us)
Async XLA Ops:
  1.4 18.6 %collective-permute-start.3 = (s32[16,64]{0,1:T(8,128)S(1)}, s32[16,64]{0,1:T(8,128)S(1)}, u32[]{:S(2)}, u32[]{:S(2)}) collective-permute-start(s32[16,64]{0,1:T(8,128)S(1)} %copy.28), channel_id=1, source_target_pairs={{0,64},{64,0},{1,65},{65,1},{2,66},{66,2},{3,67},{67,3},{4,68},{68... | collective-permute-start | bytes 12296 | tf_op jit(solution)/shard_map/ppermute | solution.py:458
  3.8 16.4 %collective-permute-start.2 = (bf16[128,512]{1,0:T(8,128)(2,1)S(1)}, bf16[128,512]{1,0:T(8,128)(2,1)S(1)}, u32[]{:S(2)}, u32[]{:S(2)}) collective-permute-start(bf16[128,512]{1,0:T(8,128)(2,1)S(1)} %constant_dynamic-slice_fusion.2), channel_id=1, source_target_pairs={{0,1},{1,0},{2,3},{3,2},{4,5},{5,4},{6,7},{7,6},{8,9},{9,8},{10,11... | collective-permute-start | bytes 393224 | tf_op jit(solution)/shard_map/ppermute | solution.py:454
  8.8 11.4 %collective-permute-start.1 = (bf16[128,768]{1,0:T(8,128)(2,1)S(1)}, bf16[128,768]{1,0:T(8,128)(2,1)S(1)}, u32[]{:S(2)}, u32[]{:S(2)}) collective-permute-start(bf16[128,768]{1,0:T(8,128)(2,1)S(1)} %get-tuple-element.84), channel_id=1, source_target_pairs={{0,4},{1,5},{2,6},{3,7},{4,0},{5,1},{6,2},{7,3},{8,12},{9,13},{10,... | collective-permute-start | bytes 589832 | tf_op jit(solution)/shard_map/ppermute | solution.py:454
  11.3 8.9 %collective-permute-start = (bf16[128,768]{1,0:T(8,128)(2,1)S(1)}, bf16[128,768]{1,0:T(8,128)(2,1)S(1)}, u32[]{:S(2)}, u32[]{:S(2)}) collective-permute-start(bf16[128,768]{1,0:T(8,128)(2,1)S(1)} %get-tuple-element.85), channel_id=1, source_target_pairs={{0,16},{1,17},{2,18},{3,19},{4,20},{5,21},{6,22},{7,23},{8,24},{9,... | collective-permute-start | bytes 589832 | tf_op jit(solution)/shard_map/ppermute | solution.py:454
  18.4 12.7 %collective-permute-start.5 = (bf16[256,2048]{1,0:T(8,128)(2,1)}, bf16[256,2048]{1,0:T(8,128)(2,1)S(1)}, u32[]{:S(2)}, u32[]{:S(2)}) collective-permute-start(bf16[256,2048]{1,0:T(8,128)(2,1)} %get-tuple-element.51), channel_id=1, source_target_pairs={{0,64},{64,0},{1,65},{65,1},{2,66},{66,2},{3,67},{67,3},{4,68},{68... | collective-permute-start | bytes 3145736 | tf_op jit(solution)/shard_map/ppermute | solution.py:458
  28.7 11.3 %collective-permute-start.8 = (bf16[256,512]{1,0:T(8,128)(2,1)}, bf16[256,512]{1,0:T(8,128)(2,1)}, u32[]{:S(2)}, u32[]{:S(2)}) collective-permute-start(bf16[256,512]{1,0:T(8,128)(2,1)} %pad_maximum_fusion.6), channel_id=1, source_target_pairs={{0,16},{1,17},{2,18},{3,19},{4,20},{5,21},{6,22},{7,23},{8,24},{9,... | collective-permute-start | bytes 786440 | tf_op jit(solution)/shard_map/ppermute | solution.py:454
  28.8 11.2 %collective-permute-start.7 = (bf16[256,768]{1,0:T(8,128)(2,1)}, bf16[256,768]{1,0:T(8,128)(2,1)S(1)}, u32[]{:S(2)}, u32[]{:S(2)}) collective-permute-start(bf16[256,768]{1,0:T(8,128)(2,1)} %pad_maximum_fusion.5), channel_id=1, source_target_pairs={{0,1},{1,0},{2,3},{3,2},{4,5},{5,4},{6,7},{7,6},{8,9},{9,8},{10,11... | collective-permute-start | bytes 1179656 | tf_op jit(solution)/shard_map/ppermute | solution.py:454
  28.9 11.2 %collective-permute-start.6 = (bf16[256,768]{1,0:T(8,128)(2,1)}, bf16[256,768]{1,0:T(8,128)(2,1)}, u32[]{:S(2)}, u32[]{:S(2)}) collective-permute-start(bf16[256,768]{1,0:T(8,128)(2,1)} %pad_maximum_fusion.4), channel_id=1, source_target_pairs={{0,4},{1,5},{2,6},{3,7},{4,0},{5,1},{6,2},{7,3},{8,12},{9,13},{10,... | collective-permute-start | bytes 1179656 | tf_op jit(solution)/shard_map/ppermute | solution.py:454
  40.8 69.2 %all-to-all-start = ((bf16[8,256,2176]{2,1,0:T(8,128)(2,1)}), bf16[8,256,2176]{2,1,0:T(8,128)(2,1)}, u32[]{:S(2)}, u32[]{:S(2)}) async-start(bf16[8,256,2176]{2,1,0:T(8,128)(2,1)} %bitcast.19), calls=%async_computation | async-start | bytes 17825792 | tf_op jit(solution)/shard_map/all_to_all | solution.py:471
  47.1 21.0 %collective-permute-start.10 = (bf16[512,768]{1,0:T(8,128)(2,1)S(1)}, bf16[512,768]{1,0:T(8,128)(2,1)S(1)}, u32[]{:S(2)}, u32[]{:S(2)}) collective-permute-start(bf16[512,768]{1,0:T(8,128)(2,1)S(1)} %pad_maximum_fusion.2.refs_2_), channel_id=1, source_target_pairs={{0,16},{1,17},{2,18},{3,19},{4,20},{5,21},{6,22},{7,23},{8,24},{9,... | collective-permute-start | bytes 2359304 | tf_op jit(solution)/shard_map/ppermute | solution.py:454
  48.6 54.3 %collective-permute-start.9 = (bf16[512,768]{1,0:T(8,128)(2,1)S(1)}, bf16[512,768]{1,0:T(8,128)(2,1)}, u32[]{:S(2)}, u32[]{:S(2)}) collective-permute-start(bf16[512,768]{1,0:T(8,128)(2,1)S(1)} %pad_maximum_fusion.1.refs_0_), channel_id=1, source_target_pairs={{0,1},{1,0},{2,3},{3,2},{4,5},{5,4},{6,7},{7,6},{8,9},{9,8},{10,11... | collective-permute-start | bytes 2359304 | tf_op jit(solution)/shard_map/ppermute | solution.py:454
  52.2 15.4 %collective-permute-start.11 = (bf16[512,512]{1,0:T(8,128)(2,1)S(1)}, bf16[512,512]{1,0:T(8,128)(2,1)S(1)}, u32[]{:S(2)}, u32[]{:S(2)}) collective-permute-start(bf16[512,512]{1,0:T(8,128)(2,1)S(1)} %pad_maximum_fusion.3.refs_4_), channel_id=1, source_target_pairs={{0,4},{1,5},{2,6},{3,7},{4,0},{5,1},{6,2},{7,3},{8,12},{9,13},{10,... | collective-permute-start | bytes 1572872 | tf_op jit(solution)/shard_map/ppermute | solution.py:454
  115.7 42.9 %all-to-all-start.1 = ((bf16[8,128,2048]{2,1,0:T(8,128)(2,1)}), bf16[8,128,2048]{2,1,0:T(8,128)(2,1)}, u32[]{:S(2)}, u32[]{:S(2)}) async-start(bf16[8,128,2048]{2,1,0:T(8,128)(2,1)} %bitcast.21), calls=%async_computation.1 | async-start | bytes 8388608 | tf_op jit(solution)/shard_map/all_to_all | solution.py:471
  124.3 29.8 %collective-permute-start.13 = (bf16[512,768]{1,0:T(8,128)(2,1)}, bf16[512,768]{1,0:T(8,128)(2,1)S(1)}, u32[]{:S(2)}, u32[]{:S(2)}) collective-permute-start(bf16[512,768]{1,0:T(8,128)(2,1)} %get-tuple-element.63), channel_id=1, source_target_pairs={{0,16},{1,17},{2,18},{3,19},{4,20},{5,21},{6,22},{7,23},{8,24},{9,... | collective-permute-start | bytes 2359304 | tf_op jit(solution)/shard_map/ppermute | solution.py:454
  129.1 25.4 %collective-permute-start.12 = (bf16[512,768]{1,0:T(8,128)(2,1)}, bf16[512,768]{1,0:T(8,128)(2,1)S(1)}, u32[]{:S(2)}, u32[]{:S(2)}) collective-permute-start(bf16[512,768]{1,0:T(8,128)(2,1)} %get-tuple-element.62), channel_id=1, source_target_pairs={{0,1},{1,0},{2,3},{3,2},{4,5},{5,4},{6,7},{7,6},{8,9},{9,8},{10,11... | collective-permute-start | bytes 2359304 | tf_op jit(solution)/shard_map/ppermute | solution.py:454
  135.9 18.1 %collective-permute-start.14 = (bf16[512,640]{1,0:T(8,128)(2,1)}, bf16[512,640]{1,0:T(8,128)(2,1)S(1)}, u32[]{:S(2)}, u32[]{:S(2)}) collective-permute-start(bf16[512,640]{1,0:T(8,128)(2,1)} %get-tuple-element.64), channel_id=1, source_target_pairs={{0,4},{1,5},{2,6},{3,7},{4,0},{5,1},{6,2},{7,3},{8,12},{9,13},{10,... | collective-permute-start | bytes 1966088 | tf_op jit(solution)/shard_map/ppermute | solution.py:454
  158.7 27.0 %collective-permute-start.16 = (bf16[1024,2048]{1,0:T(8,128)(2,1)}, bf16[1024,2048]{1,0:T(8,128)(2,1)}, u32[]{:S(2)}, u32[]{:S(2)}) collective-permute-start(bf16[1024,2048]{1,0:T(8,128)(2,1)} %bitcast.13), channel_id=1, source_target_pairs={{0,64},{64,0},{1,65},{65,1},{2,66},{66,2},{3,67},{67,3},{4,68},{68... | collective-permute-start | bytes 12582920 | tf_op jit(solution)/shard_map/ppermute | solution.py:458
  161.6 11.3 %collective-permute-start.15 = (bf16[256,768]{1,0:T(8,128)(2,1)}, bf16[256,768]{1,0:T(8,128)(2,1)S(1)}, u32[]{:S(2)}, u32[]{:S(2)}) collective-permute-start(bf16[256,768]{1,0:T(8,128)(2,1)} %slice.135), channel_id=1, source_target_pairs={{0,4},{1,5},{2,6},{3,7},{4,0},{5,1},{6,2},{7,3},{8,12},{9,13},{10,... | collective-permute-start | bytes 1179656 | tf_op jit(solution)/shard_map/ppermute | solution.py:454
  165.6 7.8 %collective-permute-start.18 = (bf16[256,768]{1,0:T(8,128)(2,1)S(1)}, bf16[256,768]{1,0:T(8,128)(2,1)S(1)}, u32[]{:S(2)}, u32[]{:S(2)}) collective-permute-start(bf16[256,768]{1,0:T(8,128)(2,1)S(1)} %slice.134), channel_id=1, source_target_pairs={{0,1},{1,0},{2,3},{3,2},{4,5},{5,4},{6,7},{7,6},{8,9},{9,8},{10,11... | collective-permute-start | bytes 1179656 | tf_op jit(solution)/shard_map/ppermute | solution.py:454
  165.6 7.3 %collective-permute-start.20 = (bf16[256,640]{1,0:T(8,128)(2,1)}, bf16[256,640]{1,0:T(8,128)(2,1)S(1)}, u32[]{:S(2)}, u32[]{:S(2)}) collective-permute-start(bf16[256,640]{1,0:T(8,128)(2,1)} %slice.136), channel_id=1, source_target_pairs={{0,16},{1,17},{2,18},{3,19},{4,20},{5,21},{6,22},{7,23},{8,24},{9,... | collective-permute-start | bytes 983048 | tf_op jit(solution)/shard_map/ppermute | solution.py:454
  174.6 41.0 %all-to-all-start.2 = ((bf16[8,128,2048]{2,1,0:T(8,128)(2,1)}), bf16[8,128,2048]{2,1,0:T(8,128)(2,1)}, u32[]{:S(2)}, u32[]{:S(2)}) async-start(bf16[8,128,2048]{2,1,0:T(8,128)(2,1)} %bitcast.20), calls=%async_computation.2 | async-start | bytes 8388608 | tf_op jit(solution)/shard_map/all_to_all | solution.py:471
  181.3 22.0 %collective-permute-start.21 = (bf16[128,640]{1,0:T(8,128)(2,1)S(1)}, bf16[128,640]{1,0:T(8,128)(2,1)S(1)}, u32[]{:S(2)}, u32[]{:S(2)}) collective-permute-start(bf16[128,640]{1,0:T(8,128)(2,1)S(1)} %slice.139), channel_id=1, source_target_pairs={{0,1},{1,0},{2,3},{3,2},{4,5},{5,4},{6,7},{7,6},{8,9},{9,8},{10,11... | collective-permute-start | bytes 491528 | tf_op jit(solution)/shard_map/ppermute | solution.py:454
  184.1 19.3 %collective-permute-start.17 = (bf16[128,768]{1,0:T(8,128)(2,1)S(1)}, bf16[128,768]{1,0:T(8,128)(2,1)S(1)}, u32[]{:S(2)}, u32[]{:S(2)}) collective-permute-start(bf16[128,768]{1,0:T(8,128)(2,1)S(1)} %slice.138), channel_id=1, source_target_pairs={{0,16},{1,17},{2,18},{3,19},{4,20},{5,21},{6,22},{7,23},{8,24},{9,... | collective-permute-start | bytes 589832 | tf_op jit(solution)/shard_map/ppermute | solution.py:454
  185.5 17.9 %collective-permute-start.19 = (bf16[128,768]{1,0:T(8,128)(2,1)S(1)}, bf16[128,768]{1,0:T(8,128)(2,1)S(1)}, u32[]{:S(2)}, u32[]{:S(2)}) collective-permute-start(bf16[128,768]{1,0:T(8,128)(2,1)S(1)} %slice.137), channel_id=1, source_target_pairs={{0,4},{1,5},{2,6},{3,7},{4,0},{5,1},{6,2},{7,3},{8,12},{9,13},{10,... | collective-permute-start | bytes 589832 | tf_op jit(solution)/shard_map/ppermute | solution.py:454
  (32 other events, 379.4 us)

commit v5 on v2

--- a/solution.py
+++ b/solution.py
@@ -515,10 +515,12 @@
     lists = lists.reshape(2 * CUBE, ROW_BLOCK).astype(jnp.float32)
 
     lists = lists[None]
+    (which_late,) = after([lists], [which])
     crossed = swap(lists, 0, 1)
-    gated, gated_theirs = gated_call(which, gate_pre, out_grad)
+    gated, gated_theirs = gated_call(which_late, gate_pre, out_grad)
     gated_other = swap_cores(gated_theirs)
-    crossed, *swapped = after([gated], [crossed, *swapped])
+    swapped = after([gated], swapped)
+    (crossed,) = after([gated], [crossed])
     lists = jnp.concatenate([lists, crossed], axis=0)
     crossed = swap(lists, 1, 1)
     parts = [jnp.concatenate(pair, axis=0) for pair in zip(parts, swapped)]
@@ -531,13 +533,15 @@
     lists = jnp.concatenate([lists, crossed], axis=0)
     crossed = swap(lists, 2, 1)
     slot_grad = slot_grad_call(which, packed, packed_other, gated, gated_other)
-    crossed, *swapped = after([slot_grad], [crossed, *swapped])
-    lists = jnp.concatenate([lists, crossed], axis=0)
-    (slot_grad,) = after(swapped, [slot_grad])
+    swapped = after([slot_grad], swapped)
+    (crossed,) = after([slot_grad], [crossed])
+    (slot_grad,) = after([crossed, *swapped], [slot_grad])
     arrived = cube_exchange(slot_grad)
     parts = [jnp.concatenate(pair, axis=0) for pair in zip(parts, swapped)]
     swapped = [swap(part, order[2]) for part, order in zip(parts, ORDERS)]
     gathered = [half for pair in zip(parts, swapped) for half in pair]
+
+    lists = jnp.concatenate([lists, crossed], axis=0)
     own_cube = sum(bit * (one // 2) for bit, one in zip(BITS, shifted))
     lists = lists.reshape(CUBE, CUBE, 2, ROW_BLOCK)
     lists = lax.dynamic_slice(lists, (0, own_cube, 0, 0), (CUBE, 1, 2, ROW_BLOCK))
@@ -546,24 +550,28 @@
         lists = jnp.where(shifted[axis] // 2 == 0, lists, jnp.flip(lists, axis))
     ids = spread_call(lists.reshape(2 * CUBE, ROW_BLOCK))
     found_other = select_call(1, spot, ids, gathered, half_width)
-    found = select_call(0, spot, ids, gathered, half_width)
-    (arrived,) = after([found, found_other], [arrived])
+    (arrived,) = after([found_other], [arrived])
     (found_other,) = after([arrived], [found_other])
     fetched_theirs = cube_exchange(found_other)
+
     halves = [partial_call(chunk, spot, ids, arrived, row_count) for chunk in range(len(ORDERS))]
+    (ids,) = after([keep for keep, _ in halves], [ids])
+    found = select_call(0, spot, ids, gathered, half_width)
     received = [swap(send, order[2]) for (_, send), order in zip(halves, ORDERS)]
-    (fetched_theirs,) = after(received, [fetched_theirs])
-    (found,) = after([fetched_theirs], [found])
+    received = after([found], received)
+    half = CUBE // 4 * row_count
+    totals = [keep + other.astype(jnp.float32) for (keep, _), other in zip(halves, received)]
+    halves = [(total[:half], total[half:].astype(jnp.bfloat16)) for total in totals]
+    received = [swap(send, order[1]) for (_, send), order in zip(halves, ORDERS)]
+    (fetched_theirs,) = after([send for _, send in halves], [fetched_theirs])
+    (found,) = after([fetched_theirs, *received], [found])
     fetched = cube_exchange(found)
     fetched_other = swap_cores(fetched_theirs)
 
-    half = CUBE // 4 * row_count
-    for step in (1, 0):
-        totals = [keep + other.astype(jnp.float32) for (keep, _), other in zip(halves, received)]
-        halves = [(total[:half], total[half:].astype(jnp.bfloat16)) for total in totals]
-        received = [swap(send, order[step]) for (_, send), order in zip(halves, ORDERS)]
-        half //= 2
-    (fetched_other,) = after([send for _, send in halves], [fetched_other])
+    half //= 2
+    totals = [keep + other.astype(jnp.float32) for (keep, _), other in zip(halves, received)]
+    halves = [(total[:half], total[half:].astype(jnp.bfloat16)) for total in totals]
+    received = [swap(send, order[0]) for (_, send), order in zip(halves, ORDERS)]
     layer_out, gate_grad, score = read_call(which, packed, fetched_other, gate_pre, out_grad)
     received = after([score], received)
     totals = [keep + other.astype(jnp.float32) for (keep, _), other in zip(halves, received)]

time: 230 us -> 224 us (0.974)
  waiting for transfers between devices: 90.2 us -> 79 us
  local copies, waits for them, and re-layouts: 8.91 us -> 16.3 us
  other arithmetic: 8.44 us -> 5.88 us
    ppermute x21, waiting for transfers between devices: 84.2 us -> 77.6 us  [swap(): return lax.ppermute(x, ('batch', 'table'), pairs)]
    unnamed x35 -> x59, local copies, waits for them, and re-layouts: 5.13 us -> 11 us
    all_to_all x3, waiting for transfers between devices: 4.6 us -> 0.01 us  [cube_exchange(): lax.all_to_all(x, ('batch', 'table'), split_axis=0, concat_axis=0, axis_i...]
    ppermute x21, starting transfers between devices: 32.7 us -> 35.2 us  [swap(): return lax.ppermute(x, ('batch', 'table'), pairs)]
    add x8, other arithmetic: 4.44 us -> 1.88 us  [local(): keep + other.astype(jnp.float32)]
  transfers between devices with their start and end apart: 29 -> 29, of which waited for: 9 -> 10; matrix products, arithmetic and copies ran while one was open for 6% -> 6% of each run, Pallas kernels for 25% -> 26%
where the time goes in v5:
time: 224 us; the launch traced here: 223 us
  waiting for transfers between devices  79 us (35%)
  Pallas kernels  65.6 us (29%)
  starting transfers between devices  54.7 us (24%)
  local copies, waits for them, and re-layouts  16.3 us (7%)
  other arithmetic  5.88 us (3%)
    ppermute x21, waiting for transfers between devices, swap(): return lax.ppermute(x, ('batch', 'table'), pairs)  77.6 us
    ppermute x21, starting transfers between devices, swap(): return lax.ppermute(x, ('batch', 'table'), pairs)  35.2 us
    pallas_call x2, Pallas kernels, read_call(): pl.pallas_call(functools.partial(read_kernel, own), grid_spec=pltpu.Prefe...  15.9 us
    all_to_all x3, starting transfers between devices, cube_exchange(): lax.all_to_all(x, ('batch', 'table'), split_axis=0, concat_axis=0, axis_i...  14.2 us
    pallas_call x3, Pallas kernels, partial_call(): pl.pallas_call(functools.partial(partial_kernel, chunk), grid=(1,), in_sp...  11.4 us
    pallas_call x2, Pallas kernels, select_call(): pl.pallas_call(functools.partial(select_kernel, group), grid=(len(ORDERS)...  11.3 us
    unnamed x59, local copies, waits for them, and re-layouts  11 us
    pallas_call x1, Pallas kernels, adam_call(): pl.pallas_call(adam_kernel, grid_spec=pltpu.PrefetchScalarGridSpec(num_sc...  8.04 us
  transfers between devices with their start and end apart: 29, of which 10 were waited for; matrix products, arithmetic and copies ran while one was open for 6% of the time, Pallas kernels for 26%

profile of v5, /device:TPU:1, one launch (start us, length us, event | category | flops | bytes accessed | tf_op | source)
XLA Modules:
  0.0 222.8 jit_solution(3791608982742896463)
XLA Ops:
  3.8 3.9 %collective-permute-start.3 = (bf16[128,512]{1,0:T(8,128)(2,1)S(1)}, bf16[128,512]{1,0:T(8,128)(2,1)S(1)}, u32[]{:S(2)}, u32[]{:S(2)}) collective-permute-start(bf16[128,512]{1,0:T(8,128)(2,1)S(1)} %constant_dynamic-slice_fusion.2), channel_id=1, source_target_pairs={{0,1},{1,0},{2,3},{3,2},{4,5},{5,4},{6,7},{7,6},{8,9},{9,8},{10,11... | collective-permute-start | bytes 393224 | tf_op jit(solution)/shard_map/ppermute | solution.py:463
  16.9 4.4 %gated_halves.1 = (bf16[256,2048]{1,0:T(8,128)(2,1)}, bf16[256,2048]{1,0:T(8,128)(2,1)}) custom-call(s32[1]{0:T(128)} %bitcast.core_ref, bf16[256,4096]{1,0:T(8,128)(2,1)} %gate_ref.3, bf16[256,4096]{1,0:T(8,128)(2,1)} %grad_ref.3, bf16[256,4096]{1,0:T(8,128)(2,1)} %gate_ref.3, bf16[256,4096]{1,0:T(8,128)(2,1)} %grad_ref.3), custom_call_target="tpu_custom_call" | custom-call | flops 4194304 | bytes 6291456 | tf_op jit(solution)/shard_map/gated_halves/pallas_call | solution.py:92
  22.8 5.7 %pack_weights.1 = (bf16[256,1024]{1,0:T(8,128)(2,1)}, f32[256,32]{1,0:T(8,128)}) custom-call(f32[256,32]{1,0:T(8,128)} %copy.29.logit_ref, s32[256,32]{1,0:T(8,128)} %fusion.1.slot_ref), custom_call_target="tpu_custom_call" | custom-call | flops 33554432 | bytes 1048576 | tf_op jit(solution)/shard_map/pack_weights/pallas_call | solution.py:65
  37.4 7.2 %slot_gradients.1 = bf16[2048,2048]{1,0:T(8,128)(2,1)} custom-call(s32[1]{0:T(128)} %bitcast.core_ref, bf16[256,1024]{1,0:T(8,128)(2,1)} %get-tuple-element.55.packed_ref, bf16[256,1024]{1,0:T(8,128)(2,1)} %copy-done.19, bf16[256,2048]{1,0:T(8,128)(2,1)} %get-tuple-element.50.gated_ref, bf16[256,2048]{1,0:T(8,128)(2,1)} %copy-done.16), custom_call_target="tpu_custom_call" | custom-call | flops 2147483648 | bytes 14680064 | tf_op jit(solution)/shard_map/slot_gradients/pallas_call | solution.py:139
  45.4 5.0 %all-to-all-start = ((bf16[8,256,2048]{2,1,0:T(8,128)(2,1)}), bf16[8,256,2048]{2,1,0:T(8,128)(2,1)}, u32[]{:S(2)}, u32[]{:S(2)}) async-start(bf16[8,256,2048]{2,1,0:T(8,128)(2,1)} %bitcast.28), calls=%async_computation | async-start | bytes 16777216 | tf_op jit(solution)/shard_map/all_to_all | solution.py:480
  53.4 3.1 %collective-permute-start.12 = (bf16[512,768]{1,0:T(8,128)(2,1)S(1)}, bf16[512,768]{1,0:T(8,128)(2,1)}, u32[]{:S(2)}, u32[]{:S(2)}) collective-permute-start(bf16[512,768]{1,0:T(8,128)(2,1)S(1)} %pad_maximum_fusion.1.refs_0_), channel_id=1, source_target_pairs={{0,1},{1,0},{2,3},{3,2},{4,5},{5,4},{6,7},{7,6},{8,9},{9,8},{10,11... | collective-permute-start | bytes 2359304 | tf_op jit(solution)/shard_map/ppermute | solution.py:463
  62.7 10.3 %collective-permute-done.14.refs_5_ = bf16[512,512]{1,0:T(8,128)(2,1)S(1)} collective-permute-done((bf16[512,512]{1,0:T(8,128)(2,1)S(1)}, bf16[512,512]{1,0:T(8,128)(2,1)S(1)}, u32[]{:S(2)}, u32[]{:S(2)}) %collective-permute-start.14) | collective-permute-done | bytes 524320 | tf_op jit(solution)/shard_map/ppermute | solution.py:463
  73.0 34.7 %collective-permute-done.12.refs_1_ = bf16[512,768]{1,0:T(8,128)(2,1)} collective-permute-done((bf16[512,768]{1,0:T(8,128)(2,1)S(1)}, bf16[512,768]{1,0:T(8,128)(2,1)}, u32[]{:S(2)}, u32[]{:S(2)}) %collective-permute-start.12) | collective-permute-done | bytes 786464 | tf_op jit(solution)/shard_map/ppermute | solution.py:463
  107.7 5.6 %select_rows.2 = bf16[1024,2048]{1,0:T(8,128)(2,1)} custom-call(s32[1]{0:T(128)} %bitcast.9.spot_ref, bf16[2048,128]{1,0:T(8,128)(2,1)} %spread_lists.1.id_ref, bf16[512,768]{1,0:T(8,128)(2,1)} %copy-done.2, bf16[512,768]{1,0:T(8,128)(2,1)} %collective-permute-done.12.refs_1_, bf16[512,768]{1,0:T(8,128)(2,1)} %copy-done.1, bf16[512,768]{1,0:T(8,128)(2,1)} %copy-done.5, ...), custom_call_target="tpu_custom_call" | custom-call | flops 570425344 | bytes 13369344 | tf_op jit(solution)/shard_map/select_rows/pallas_call | solution.py:221
  113.4 4.5 %all-to-all-start.1 = ((bf16[8,128,2048]{2,1,0:T(8,128)(2,1)}), bf16[8,128,2048]{2,1,0:T(8,128)(2,1)}, u32[]{:S(2)}, u32[]{:S(2)}) async-start(bf16[8,128,2048]{2,1,0:T(8,128)(2,1)} %bitcast.30), calls=%async_computation.1 | async-start | bytes 8388608 | tf_op jit(solution)/shard_map/all_to_all | solution.py:480
  117.9 3.9 %partial_sums.4 = (f32[512,768]{1,0:T(8,128)}, bf16[512,768]{1,0:T(8,128)(2,1)}) custom-call(s32[1]{0:T(128)} %bitcast.9.spot_ref, bf16[2048,128]{1,0:T(8,128)(2,1)} %spread_lists.1.id_ref, bf16[2048,2048]{1,0:T(8,128)(2,1)} %bitcast.19.arrived_ref), custom_call_target="tpu_custom_call" | custom-call | flops 402653184 | bytes 12582912 | tf_op jit(solution)/shard_map/partial_sums/pallas_call | solution.py:265
  121.8 3.9 %partial_sums.3 = (f32[512,768]{1,0:T(8,128)}, bf16[512,768]{1,0:T(8,128)(2,1)}) custom-call(s32[1]{0:T(128)} %bitcast.9.spot_ref, bf16[2048,128]{1,0:T(8,128)(2,1)} %spread_lists.1.id_ref, bf16[2048,2048]{1,0:T(8,128)(2,1)} %bitcast.19.arrived_ref), custom_call_target="tpu_custom_call" | custom-call | flops 402653184 | bytes 12582912 | tf_op jit(solution)/shard_map/partial_sums/pallas_call | solution.py:265
  125.8 3.5 %collective-permute-start.15 = (bf16[512,768]{1,0:T(8,128)(2,1)}, bf16[512,768]{1,0:T(8,128)(2,1)S(1)}, u32[]{:S(2)}, u32[]{:S(2)}) collective-permute-start(bf16[512,768]{1,0:T(8,128)(2,1)} %get-tuple-element.69), channel_id=1, source_target_pairs={{0,1},{1,0},{2,3},{3,2},{4,5},{5,4},{6,7},{7,6},{8,9},{9,8},{10,11... | collective-permute-start | bytes 2359304 | tf_op jit(solution)/shard_map/ppermute | solution.py:463
  129.3 3.6 %partial_sums.5 = (f32[512,640]{1,0:T(8,128)}, bf16[512,640]{1,0:T(8,128)(2,1)}) custom-call(s32[1]{0:T(128)} %bitcast.9.spot_ref, bf16[2048,128]{1,0:T(8,128)(2,1)} %spread_lists.1.id_ref, bf16[2048,2048]{1,0:T(8,128)(2,1)} %bitcast.19.arrived_ref), custom_call_target="tpu_custom_call" | custom-call | flops 335544320 | bytes 10485760 | tf_op jit(solution)/shard_map/partial_sums/pallas_call | solution.py:265
  135.4 5.6 %select_rows.3 = bf16[1024,2048]{1,0:T(8,128)(2,1)} custom-call(s32[1]{0:T(128)} %bitcast.9.spot_ref, bf16[2048,128]{1,0:T(8,128)(2,1)} %spread_lists.1.id_ref, bf16[512,768]{1,0:T(8,128)(2,1)} %copy-done.2, bf16[512,768]{1,0:T(8,128)(2,1)} %collective-permute-done.12.refs_1_, bf16[512,768]{1,0:T(8,128)(2,1)} %copy-done.1, bf16[512,768]{1,0:T(8,128)(2,1)} %copy-done.5, ...), custom_call_target="tpu_custom_call" | custom-call | flops 570425344 | bytes 13369344 | tf_op jit(solution)/shard_map/select_rows/pallas_call | solution.py:221
  141.0 10.5 %collective-permute-done.17 = bf16[512,640]{1,0:T(8,128)(2,1)S(1)} collective-permute-done((bf16[512,640]{1,0:T(8,128)(2,1)}, bf16[512,640]{1,0:T(8,128)(2,1)S(1)}, u32[]{:S(2)}, u32[]{:S(2)}) %collective-permute-start.17) | collective-permute-done | bytes 655392 | tf_op jit(solution)/shard_map/ppermute | solution.py:463
  157.8 3.1 %collective-permute-start.19 = (bf16[1024,2048]{1,0:T(8,128)(2,1)}, bf16[1024,2048]{1,0:T(8,128)(2,1)}, u32[]{:S(2)}, u32[]{:S(2)}) collective-permute-start(bf16[1024,2048]{1,0:T(8,128)(2,1)} %bitcast.21), channel_id=1, source_target_pairs={{0,64},{64,0},{1,65},{65,1},{2,66},{66,2},{3,67},{67,3},{4,68},{68... | collective-permute-start | bytes 12582920 | tf_op jit(solution)/shard_map/ppermute | solution.py:467
  160.9 3.0 %collective-permute-start.18 = (bf16[256,768]{1,0:T(8,128)(2,1)}, bf16[256,768]{1,0:T(8,128)(2,1)S(1)}, u32[]{:S(2)}, u32[]{:S(2)}) collective-permute-start(bf16[256,768]{1,0:T(8,128)(2,1)} %slice.135), channel_id=1, source_target_pairs={{0,4},{1,5},{2,6},{3,7},{4,0},{5,1},{6,2},{7,3},{8,12},{9,13},{10,... | collective-permute-start | bytes 1179656 | tf_op jit(solution)/shard_map/ppermute | solution.py:463
  166.7 4.9 %collective-permute-done.23 = bf16[256,640]{1,0:T(8,128)(2,1)S(1)} collective-permute-done((bf16[256,640]{1,0:T(8,128)(2,1)}, bf16[256,640]{1,0:T(8,128)(2,1)S(1)}, u32[]{:S(2)}, u32[]{:S(2)}) %collective-permute-start.23) | collective-permute-done | bytes 327712 | tf_op jit(solution)/shard_map/ppermute | solution.py:463
  173.1 4.7 %all-to-all-start.2 = ((bf16[8,128,2048]{2,1,0:T(8,128)(2,1)}), bf16[8,128,2048]{2,1,0:T(8,128)(2,1)}, u32[]{:S(2)}, u32[]{:S(2)}) async-start(bf16[8,128,2048]{2,1,0:T(8,128)(2,1)} %bitcast.29), calls=%async_computation.2 | async-start | bytes 8388608 | tf_op jit(solution)/shard_map/all_to_all | solution.py:480
  184.8 7.5 %read_and_scores.2 = (bf16[256,4096]{1,0:T(8,128)(2,1)}, bf16[256,4096]{1,0:T(8,128)(2,1)}, f32[256,1024]{1,0:T(8,128)}) custom-call(s32[1]{0:T(128)} %bitcast.core_ref, bf16[256,1024]{1,0:T(8,128)(2,1)} %get-tuple-element.55.packed_ref, bf16[1024,2048]{1,0:T(8,128)(2,1)} %collective-permute-done.19.fetched_ref, bf16[256,4096]{1,0:T(8,128)(2,1)} %gate_ref.3, ...), custom_call_target="tpu_custom_call" | custom-call | flops 2147483648 | bytes 9437184 | tf_op jit(solution)/shard_map/read_and_scores/pallas_call | solution.py:425
  192.3 9.8 %collective-permute-done.24 = bf16[128,640]{1,0:T(8,128)(2,1)S(1)} collective-permute-done((bf16[128,640]{1,0:T(8,128)(2,1)S(1)}, bf16[128,640]{1,0:T(8,128)(2,1)S(1)}, u32[]{:S(2)}, u32[]{:S(2)}) %collective-permute-start.24) | collective-permute-done | bytes 163872 | tf_op jit(solution)/shard_map/ppermute | solution.py:463
  206.2 8.0 %adam_rows.1 = (bf16[128,4096]{1,0:T(8,128)(2,1)}, f32[128,4096]{1,0:T(8,128)}, f32[128,4096]{1,0:T(8,128)}) custom-call(s32[1]{0:T(128)} %bitcast.core_ref, f32[128,2176]{1,0:T(8,128)} %copy-done, f32[128,2176]{1,0:T(8,128)} %copy-done, f32[128,2176]{1,0:T(8,128)} %copy-done.15, bf16[128,4096]{1,0:T(8,128)(2,1)} %value_ref.1, f32[128,4096]{1,0:T(8,128)} %first_ref.1, ...), custom_call_target="tpu_custom_call" | custom-call | flops 5242880 | bytes 14680064 | tf_op jit(solution)/shard_map/adam_rows/pallas_call | solution.py:311
  214.3 8.4 %read_and_scores.3 = (bf16[256,4096]{1,0:T(8,128)(2,1)}, bf16[256,4096]{1,0:T(8,128)(2,1)}, f32[32,256]{1,0:T(8,128)}) custom-call(s32[1]{0:T(128)} %bitcast.core_ref, bf16[256,1024]{1,0:T(8,128)(2,1)} %get-tuple-element.55.packed_ref, bf16[1024,2048]{1,0:T(8,128)(2,1)} %bitcast.23.fetched_ref, ...), custom_call_target="tpu_custom_call", output_to_operand_aliasing={{0}: (8, {}), {1}: (9, {})} | custom-call | flops 2147483648 | bytes 9437184 | tf_op jit(solution)/shard_map/read_and_scores/pallas_call | solution.py:425
  (152 shorter events, 56.4 us)
Async XLA Ops:
  1.4 15.0 %collective-permute-start = (s32[16,64]{0,1:T(8,128)S(1)}, s32[16,64]{0,1:T(8,128)S(1)}, u32[]{:S(2)}, u32[]{:S(2)}) collective-permute-start(s32[16,64]{0,1:T(8,128)S(1)} %copy.21), channel_id=1, source_target_pairs={{0,64},{64,0},{1,65},{65,1},{2,66},{66,2},{3,67},{67,3},{4,68},{68... | collective-permute-start | bytes 12296 | tf_op jit(solution)/shard_map/ppermute | solution.py:467
  3.8 18.2 %collective-permute-start.3 = (bf16[128,512]{1,0:T(8,128)(2,1)S(1)}, bf16[128,512]{1,0:T(8,128)(2,1)S(1)}, u32[]{:S(2)}, u32[]{:S(2)}) collective-permute-start(bf16[128,512]{1,0:T(8,128)(2,1)S(1)} %constant_dynamic-slice_fusion.2), channel_id=1, source_target_pairs={{0,1},{1,0},{2,3},{3,2},{4,5},{5,4},{6,7},{7,6},{8,9},{9,8},{10,11... | collective-permute-start | bytes 393224 | tf_op jit(solution)/shard_map/ppermute | solution.py:463
  8.8 13.3 %collective-permute-start.2 = (bf16[128,768]{1,0:T(8,128)(2,1)S(1)}, bf16[128,768]{1,0:T(8,128)(2,1)S(1)}, u32[]{:S(2)}, u32[]{:S(2)}) collective-permute-start(bf16[128,768]{1,0:T(8,128)(2,1)S(1)} %get-tuple-element.92), channel_id=1, source_target_pairs={{0,4},{1,5},{2,6},{3,7},{4,0},{5,1},{6,2},{7,3},{8,12},{9,13},{10,... | collective-permute-start | bytes 589832 | tf_op jit(solution)/shard_map/ppermute | solution.py:463
  11.3 10.7 %collective-permute-start.1 = (bf16[128,768]{1,0:T(8,128)(2,1)S(1)}, bf16[128,768]{1,0:T(8,128)(2,1)S(1)}, u32[]{:S(2)}, u32[]{:S(2)}) collective-permute-start(bf16[128,768]{1,0:T(8,128)(2,1)S(1)} %get-tuple-element.93), channel_id=1, source_target_pairs={{0,16},{1,17},{2,18},{3,19},{4,20},{5,21},{6,22},{7,23},{8,24},{9,... | collective-permute-start | bytes 589832 | tf_op jit(solution)/shard_map/ppermute | solution.py:463
  21.2 15.2 %collective-permute-start.7 = (bf16[256,2048]{1,0:T(8,128)(2,1)}, bf16[256,2048]{1,0:T(8,128)(2,1)S(1)}, u32[]{:S(2)}, u32[]{:S(2)}) collective-permute-start(bf16[256,2048]{1,0:T(8,128)(2,1)} %get-tuple-element.58), channel_id=1, source_target_pairs={{0,64},{64,0},{1,65},{65,1},{2,66},{66,2},{3,67},{67,3},{4,68},{68... | collective-permute-start | bytes 3145736 | tf_op jit(solution)/shard_map/ppermute | solution.py:467
  31.5 13.1 %collective-permute-start.10 = (bf16[256,768]{1,0:T(8,128)(2,1)S(1)}, bf16[256,768]{1,0:T(8,128)(2,1)}, u32[]{:S(2)}, u32[]{:S(2)}) collective-permute-start(bf16[256,768]{1,0:T(8,128)(2,1)S(1)} %pad_maximum_fusion.5), channel_id=1, source_target_pairs={{0,1},{1,0},{2,3},{3,2},{4,5},{5,4},{6,7},{7,6},{8,9},{9,8},{10,11... | collective-permute-start | bytes 1179656 | tf_op jit(solution)/shard_map/ppermute | solution.py:463
  31.5 13.1 %collective-permute-start.9 = (bf16[256,768]{1,0:T(8,128)(2,1)S(1)}, bf16[256,768]{1,0:T(8,128)(2,1)S(1)}, u32[]{:S(2)}, u32[]{:S(2)}) collective-permute-start(bf16[256,768]{1,0:T(8,128)(2,1)S(1)} %pad_maximum_fusion.4), channel_id=1, source_target_pairs={{0,4},{1,5},{2,6},{3,7},{4,0},{5,1},{6,2},{7,3},{8,12},{9,13},{10,... | collective-permute-start | bytes 1179656 | tf_op jit(solution)/shard_map/ppermute | solution.py:463
  34.3 10.3 %collective-permute-start.11 = (bf16[256,512]{1,0:T(8,128)(2,1)}, bf16[256,512]{1,0:T(8,128)(2,1)}, u32[]{:S(2)}, u32[]{:S(2)}) collective-permute-start(bf16[256,512]{1,0:T(8,128)(2,1)} %pad_maximum_fusion.6), channel_id=1, source_target_pairs={{0,16},{1,17},{2,18},{3,19},{4,20},{5,21},{6,22},{7,23},{8,24},{9,... | collective-permute-start | bytes 786440 | tf_op jit(solution)/shard_map/ppermute | solution.py:463
  35.6 9.0 %collective-permute-start.8 = (f32[4,16,128]{2,1,0:T(8,128)S(1)}, f32[4,16,128]{2,1,0:T(8,128)S(1)}, u32[]{:S(2)}, u32[]{:S(2)}) collective-permute-start(f32[4,16,128]{2,1,0:T(8,128)S(1)} %pad_maximum_fusion.7), channel_id=1, source_target_pairs={{0,3},{1,2},{2,1},{3,0},{4,7},{5,6},{6,5},{7,4},{8,11},{9,10},{10,... | collective-permute-start | bytes 98312 | tf_op jit(solution)/shard_map/ppermute | solution.py:463
  45.4 68.0 %all-to-all-start = ((bf16[8,256,2048]{2,1,0:T(8,128)(2,1)}), bf16[8,256,2048]{2,1,0:T(8,128)(2,1)}, u32[]{:S(2)}, u32[]{:S(2)}) async-start(bf16[8,256,2048]{2,1,0:T(8,128)(2,1)} %bitcast.28), calls=%async_computation | async-start | bytes 16777216 | tf_op jit(solution)/shard_map/all_to_all | solution.py:480
  51.9 21.1 %collective-permute-start.13 = (bf16[512,768]{1,0:T(8,128)(2,1)S(1)}, bf16[512,768]{1,0:T(8,128)(2,1)S(1)}, u32[]{:S(2)}, u32[]{:S(2)}) collective-permute-start(bf16[512,768]{1,0:T(8,128)(2,1)S(1)} %pad_maximum_fusion.2.refs_2_), channel_id=1, source_target_pairs={{0,16},{1,17},{2,18},{3,19},{4,20},{5,21},{6,22},{7,23},{8,24},{9,... | collective-permute-start | bytes 2359304 | tf_op jit(solution)/shard_map/ppermute | solution.py:463
  53.4 54.3 %collective-permute-start.12 = (bf16[512,768]{1,0:T(8,128)(2,1)S(1)}, bf16[512,768]{1,0:T(8,128)(2,1)}, u32[]{:S(2)}, u32[]{:S(2)}) collective-permute-start(bf16[512,768]{1,0:T(8,128)(2,1)S(1)} %pad_maximum_fusion.1.refs_0_), channel_id=1, source_target_pairs={{0,1},{1,0},{2,3},{3,2},{4,5},{5,4},{6,7},{7,6},{8,9},{9,8},{10,11... | collective-permute-start | bytes 2359304 | tf_op jit(solution)/shard_map/ppermute | solution.py:463
  57.6 15.4 %collective-permute-start.14 = (bf16[512,512]{1,0:T(8,128)(2,1)S(1)}, bf16[512,512]{1,0:T(8,128)(2,1)S(1)}, u32[]{:S(2)}, u32[]{:S(2)}) collective-permute-start(bf16[512,512]{1,0:T(8,128)(2,1)S(1)} %pad_maximum_fusion.3.refs_4_), channel_id=1, source_target_pairs={{0,4},{1,5},{2,6},{3,7},{4,0},{5,1},{6,2},{7,3},{8,12},{9,13},{10,... | collective-permute-start | bytes 1572872 | tf_op jit(solution)/shard_map/ppermute | solution.py:463
  113.4 44.5 %all-to-all-start.1 = ((bf16[8,128,2048]{2,1,0:T(8,128)(2,1)}), bf16[8,128,2048]{2,1,0:T(8,128)(2,1)}, u32[]{:S(2)}, u32[]{:S(2)}) async-start(bf16[8,128,2048]{2,1,0:T(8,128)(2,1)} %bitcast.30), calls=%async_computation.1 | async-start | bytes 8388608 | tf_op jit(solution)/shard_map/all_to_all | solution.py:480
  121.8 29.7 %collective-permute-start.16 = (bf16[512,768]{1,0:T(8,128)(2,1)}, bf16[512,768]{1,0:T(8,128)(2,1)S(1)}, u32[]{:S(2)}, u32[]{:S(2)}) collective-permute-start(bf16[512,768]{1,0:T(8,128)(2,1)} %get-tuple-element.70), channel_id=1, source_target_pairs={{0,16},{1,17},{2,18},{3,19},{4,20},{5,21},{6,22},{7,23},{8,24},{9,... | collective-permute-start | bytes 2359304 | tf_op jit(solution)/shard_map/ppermute | solution.py:463
  125.8 27.8 %collective-permute-start.15 = (bf16[512,768]{1,0:T(8,128)(2,1)}, bf16[512,768]{1,0:T(8,128)(2,1)S(1)}, u32[]{:S(2)}, u32[]{:S(2)}) collective-permute-start(bf16[512,768]{1,0:T(8,128)(2,1)} %get-tuple-element.69), channel_id=1, source_target_pairs={{0,1},{1,0},{2,3},{3,2},{4,5},{5,4},{6,7},{7,6},{8,9},{9,8},{10,11... | collective-permute-start | bytes 2359304 | tf_op jit(solution)/shard_map/ppermute | solution.py:463
  132.9 18.7 %collective-permute-start.17 = (bf16[512,640]{1,0:T(8,128)(2,1)}, bf16[512,640]{1,0:T(8,128)(2,1)S(1)}, u32[]{:S(2)}, u32[]{:S(2)}) collective-permute-start(bf16[512,640]{1,0:T(8,128)(2,1)} %get-tuple-element.71), channel_id=1, source_target_pairs={{0,4},{1,5},{2,6},{3,7},{4,0},{5,1},{6,2},{7,3},{8,12},{9,13},{10,... | collective-permute-start | bytes 1966088 | tf_op jit(solution)/shard_map/ppermute | solution.py:463
  157.8 27.0 %collective-permute-start.19 = (bf16[1024,2048]{1,0:T(8,128)(2,1)}, bf16[1024,2048]{1,0:T(8,128)(2,1)}, u32[]{:S(2)}, u32[]{:S(2)}) collective-permute-start(bf16[1024,2048]{1,0:T(8,128)(2,1)} %bitcast.21), channel_id=1, source_target_pairs={{0,64},{64,0},{1,65},{65,1},{2,66},{66,2},{3,67},{67,3},{4,68},{68... | collective-permute-start | bytes 12582920 | tf_op jit(solution)/shard_map/ppermute | solution.py:467
  160.9 10.6 %collective-permute-start.18 = (bf16[256,768]{1,0:T(8,128)(2,1)}, bf16[256,768]{1,0:T(8,128)(2,1)S(1)}, u32[]{:S(2)}, u32[]{:S(2)}) collective-permute-start(bf16[256,768]{1,0:T(8,128)(2,1)} %slice.135), channel_id=1, source_target_pairs={{0,4},{1,5},{2,6},{3,7},{4,0},{5,1},{6,2},{7,3},{8,12},{9,13},{10,... | collective-permute-start | bytes 1179656 | tf_op jit(solution)/shard_map/ppermute | solution.py:463
  163.9 7.8 %collective-permute-start.21 = (bf16[256,768]{1,0:T(8,128)(2,1)S(1)}, bf16[256,768]{1,0:T(8,128)(2,1)S(1)}, u32[]{:S(2)}, u32[]{:S(2)}) collective-permute-start(bf16[256,768]{1,0:T(8,128)(2,1)S(1)} %slice.134), channel_id=1, source_target_pairs={{0,1},{1,0},{2,3},{3,2},{4,5},{5,4},{6,7},{7,6},{8,9},{9,8},{10,11... | collective-permute-start | bytes 1179656 | tf_op jit(solution)/shard_map/ppermute | solution.py:463
  173.1 41.1 %all-to-all-start.2 = ((bf16[8,128,2048]{2,1,0:T(8,128)(2,1)}), bf16[8,128,2048]{2,1,0:T(8,128)(2,1)}, u32[]{:S(2)}, u32[]{:S(2)}) async-start(bf16[8,128,2048]{2,1,0:T(8,128)(2,1)} %bitcast.29), calls=%async_computation.2 | async-start | bytes 8388608 | tf_op jit(solution)/shard_map/all_to_all | solution.py:480
  179.9 22.2 %collective-permute-start.24 = (bf16[128,640]{1,0:T(8,128)(2,1)S(1)}, bf16[128,640]{1,0:T(8,128)(2,1)S(1)}, u32[]{:S(2)}, u32[]{:S(2)}) collective-permute-start(bf16[128,640]{1,0:T(8,128)(2,1)S(1)} %slice.139), channel_id=1, source_target_pairs={{0,1},{1,0},{2,3},{3,2},{4,5},{5,4},{6,7},{7,6},{8,9},{9,8},{10,11... | collective-permute-start | bytes 491528 | tf_op jit(solution)/shard_map/ppermute | solution.py:463
  182.4 19.7 %collective-permute-start.20 = (bf16[128,768]{1,0:T(8,128)(2,1)S(1)}, bf16[128,768]{1,0:T(8,128)(2,1)S(1)}, u32[]{:S(2)}, u32[]{:S(2)}) collective-permute-start(bf16[128,768]{1,0:T(8,128)(2,1)S(1)} %slice.138), channel_id=1, source_target_pairs={{0,16},{1,17},{2,18},{3,19},{4,20},{5,21},{6,22},{7,23},{8,24},{9,... | collective-permute-start | bytes 589832 | tf_op jit(solution)/shard_map/ppermute | solution.py:463
  184.6 17.5 %collective-permute-start.22 = (bf16[128,768]{1,0:T(8,128)(2,1)S(1)}, bf16[128,768]{1,0:T(8,128)(2,1)S(1)}, u32[]{:S(2)}, u32[]{:S(2)}) collective-permute-start(bf16[128,768]{1,0:T(8,128)(2,1)S(1)} %slice.137), channel_id=1, source_target_pairs={{0,4},{1,5},{2,6},{3,7},{4,0},{5,1},{6,2},{7,3},{8,12},{9,13},{10,... | collective-permute-start | bytes 589832 | tf_op jit(solution)/shard_map/ppermute | solution.py:463
  (33 other events, 309.3 us)

commit v6 on v5

--- a/solution.py
+++ b/solution.py
@@ -563,7 +563,7 @@
     totals = [keep + other.astype(jnp.float32) for (keep, _), other in zip(halves, received)]
     halves = [(total[:half], total[half:].astype(jnp.bfloat16)) for total in totals]
     received = [swap(send, order[1]) for (_, send), order in zip(halves, ORDERS)]
-    (fetched_theirs,) = after([send for _, send in halves], [fetched_theirs])
+    (fetched_theirs,) = after(received, [fetched_theirs])
     (found,) = after([fetched_theirs, *received], [found])
     fetched = cube_exchange(found)
     fetched_other = swap_cores(fetched_theirs)

time: 224 us -> 226 us (level)
  other arithmetic: 5.88 us -> 9.29 us
    add x8, other arithmetic: 1.88 us -> 5.28 us  [local(): keep + other.astype(jnp.float32)]
    ppermute x5, starting transfers between devices: 5.18 us -> 2.07 us  [swap_cores(): return lax.ppermute(x, 'batch', [(0, 1), (1, 0)])]
    ppermute x21, starting transfers between devices: 35.2 us -> 37.7 us  [swap(): return lax.ppermute(x, ('batch', 'table'), pairs)]
    unnamed x59 -> x55, local copies, waits for them, and re-layouts: 11 us -> 11 us
  transfers between devices with their start and end apart: 29 -> 29, of which waited for: 10 -> 9; matrix products, arithmetic and copies ran while one was open for 6% -> 7% of each run, Pallas kernels for 26% -> 25%
where the time goes in v6:
time: 226 us; the launch traced here: 225 us
  waiting for transfers between devices  79 us (35%)
  Pallas kernels  65.6 us (29%)
  starting transfers between devices  53.9 us (24%)
  local copies, waits for them, and re-layouts  15.5 us (7%)
  other arithmetic  9.29 us (4%)
    ppermute x21, waiting for transfers between devices, swap(): return lax.ppermute(x, ('batch', 'table'), pairs)  77.6 us
    ppermute x21, starting transfers between devices, swap(): return lax.ppermute(x, ('batch', 'table'), pairs)  37.7 us
    pallas_call x2, Pallas kernels, read_call(): pl.pallas_call(functools.partial(read_kernel, own), grid_spec=pltpu.Prefe...  15.9 us
    all_to_all x3, starting transfers between devices, cube_exchange(): lax.all_to_all(x, ('batch', 'table'), split_axis=0, concat_axis=0, axis_i...  14.1 us
    pallas_call x3, Pallas kernels, partial_call(): pl.pallas_call(functools.partial(partial_kernel, chunk), grid=(1,), in_sp...  11.4 us
    pallas_call x2, Pallas kernels, select_call(): pl.pallas_call(functools.partial(select_kernel, group), grid=(len(ORDERS)...  11.3 us
    unnamed x55, local copies, waits for them, and re-layouts  11 us
    pallas_call x1, Pallas kernels, adam_call(): pl.pallas_call(adam_kernel, grid_spec=pltpu.PrefetchScalarGridSpec(num_sc...  8.04 us
  transfers between devices with their start and end apart: 29, of which 9 were waited for; matrix products, arithmetic and copies ran while one was open for 7% of the time, Pallas kernels for 25%

profile of v6, /device:TPU:1, one launch (start us, length us, event | category | flops | bytes accessed | tf_op | source)
XLA Modules:
  0.0 224.8 jit_solution(13078264358168239614)
XLA Ops:
  3.8 3.9 %collective-permute-start.3 = (bf16[128,512]{1,0:T(8,128)(2,1)S(1)}, bf16[128,512]{1,0:T(8,128)(2,1)S(1)}, u32[]{:S(2)}, u32[]{:S(2)}) collective-permute-start(bf16[128,512]{1,0:T(8,128)(2,1)S(1)} %constant_dynamic-slice_fusion.2), channel_id=1, source_target_pairs={{0,1},{1,0},{2,3},{3,2},{4,5},{5,4},{6,7},{7,6},{8,9},{9,8},{10,11... | collective-permute-start | bytes 393224 | tf_op jit(solution)/shard_map/ppermute | solution.py:463
  11.3 2.7 %collective-permute-start.1 = (bf16[128,768]{1,0:T(8,128)(2,1)S(1)}, bf16[128,768]{1,0:T(8,128)(2,1)S(1)}, u32[]{:S(2)}, u32[]{:S(2)}) collective-permute-start(bf16[128,768]{1,0:T(8,128)(2,1)S(1)} %get-tuple-element.93), channel_id=1, source_target_pairs={{0,16},{1,17},{2,18},{3,19},{4,20},{5,21},{6,22},{7,23},{8,24},{9,... | collective-permute-start | bytes 589832 | tf_op jit(solution)/shard_map/ppermute | solution.py:463
  16.9 4.4 %gated_halves.1 = (bf16[256,2048]{1,0:T(8,128)(2,1)}, bf16[256,2048]{1,0:T(8,128)(2,1)}) custom-call(s32[1]{0:T(128)} %bitcast.core_ref, bf16[256,4096]{1,0:T(8,128)(2,1)} %gate_ref.3, bf16[256,4096]{1,0:T(8,128)(2,1)} %grad_ref.3, bf16[256,4096]{1,0:T(8,128)(2,1)} %gate_ref.3, bf16[256,4096]{1,0:T(8,128)(2,1)} %grad_ref.3), custom_call_target="tpu_custom_call" | custom-call | flops 4194304 | bytes 6291456 | tf_op jit(solution)/shard_map/gated_halves/pallas_call | solution.py:92
  22.8 5.7 %pack_weights.1 = (bf16[256,1024]{1,0:T(8,128)(2,1)}, f32[256,32]{1,0:T(8,128)}) custom-call(f32[256,32]{1,0:T(8,128)} %copy.29.logit_ref, s32[256,32]{1,0:T(8,128)} %fusion.1.slot_ref), custom_call_target="tpu_custom_call" | custom-call | flops 33554432 | bytes 1048576 | tf_op jit(solution)/shard_map/pack_weights/pallas_call | solution.py:65
  37.4 7.2 %slot_gradients.1 = bf16[2048,2048]{1,0:T(8,128)(2,1)} custom-call(s32[1]{0:T(128)} %bitcast.core_ref, bf16[256,1024]{1,0:T(8,128)(2,1)} %get-tuple-element.55.packed_ref, bf16[256,1024]{1,0:T(8,128)(2,1)} %copy-done.20, bf16[256,2048]{1,0:T(8,128)(2,1)} %get-tuple-element.50.gated_ref, bf16[256,2048]{1,0:T(8,128)(2,1)} %copy-done.16), custom_call_target="tpu_custom_call" | custom-call | flops 2147483648 | bytes 14680064 | tf_op jit(solution)/shard_map/slot_gradients/pallas_call | solution.py:139
  45.4 5.0 %all-to-all-start = ((bf16[8,256,2048]{2,1,0:T(8,128)(2,1)}), bf16[8,256,2048]{2,1,0:T(8,128)(2,1)}, u32[]{:S(2)}, u32[]{:S(2)}) async-start(bf16[8,256,2048]{2,1,0:T(8,128)(2,1)} %bitcast.28), calls=%async_computation | async-start | bytes 16777216 | tf_op jit(solution)/shard_map/all_to_all | solution.py:480
  53.4 3.1 %collective-permute-start.12 = (bf16[512,768]{1,0:T(8,128)(2,1)S(1)}, bf16[512,768]{1,0:T(8,128)(2,1)}, u32[]{:S(2)}, u32[]{:S(2)}) collective-permute-start(bf16[512,768]{1,0:T(8,128)(2,1)S(1)} %pad_maximum_fusion.1.refs_0_), channel_id=1, source_target_pairs={{0,1},{1,0},{2,3},{3,2},{4,5},{5,4},{6,7},{7,6},{8,9},{9,8},{10,11... | collective-permute-start | bytes 2359304 | tf_op jit(solution)/shard_map/ppermute | solution.py:463
  62.7 10.3 %collective-permute-done.14.refs_5_ = bf16[512,512]{1,0:T(8,128)(2,1)S(1)} collective-permute-done((bf16[512,512]{1,0:T(8,128)(2,1)S(1)}, bf16[512,512]{1,0:T(8,128)(2,1)S(1)}, u32[]{:S(2)}, u32[]{:S(2)}) %collective-permute-start.14) | collective-permute-done | bytes 524320 | tf_op jit(solution)/shard_map/ppermute | solution.py:463
  73.0 34.7 %collective-permute-done.12.refs_1_ = bf16[512,768]{1,0:T(8,128)(2,1)} collective-permute-done((bf16[512,768]{1,0:T(8,128)(2,1)S(1)}, bf16[512,768]{1,0:T(8,128)(2,1)}, u32[]{:S(2)}, u32[]{:S(2)}) %collective-permute-start.12) | collective-permute-done | bytes 786464 | tf_op jit(solution)/shard_map/ppermute | solution.py:463
  107.7 5.6 %select_rows.2 = bf16[1024,2048]{1,0:T(8,128)(2,1)} custom-call(s32[1]{0:T(128)} %bitcast.9.spot_ref, bf16[2048,128]{1,0:T(8,128)(2,1)} %spread_lists.1.id_ref, bf16[512,768]{1,0:T(8,128)(2,1)} %copy-done.2, bf16[512,768]{1,0:T(8,128)(2,1)} %collective-permute-done.12.refs_1_, bf16[512,768]{1,0:T(8,128)(2,1)} %copy-done.1, bf16[512,768]{1,0:T(8,128)(2,1)} %copy-done.5, ...), custom_call_target="tpu_custom_call" | custom-call | flops 570425344 | bytes 13369344 | tf_op jit(solution)/shard_map/select_rows/pallas_call | solution.py:221
  113.4 4.5 %all-to-all-start.1 = ((bf16[8,128,2048]{2,1,0:T(8,128)(2,1)}), bf16[8,128,2048]{2,1,0:T(8,128)(2,1)}, u32[]{:S(2)}, u32[]{:S(2)}) async-start(bf16[8,128,2048]{2,1,0:T(8,128)(2,1)} %bitcast.30), calls=%async_computation.1 | async-start | bytes 8388608 | tf_op jit(solution)/shard_map/all_to_all | solution.py:480
  117.9 3.9 %partial_sums.4 = (f32[512,768]{1,0:T(8,128)}, bf16[512,768]{1,0:T(8,128)(2,1)}) custom-call(s32[1]{0:T(128)} %bitcast.9.spot_ref, bf16[2048,128]{1,0:T(8,128)(2,1)} %spread_lists.1.id_ref, bf16[2048,2048]{1,0:T(8,128)(2,1)} %bitcast.19.arrived_ref), custom_call_target="tpu_custom_call" | custom-call | flops 402653184 | bytes 12582912 | tf_op jit(solution)/shard_map/partial_sums/pallas_call | solution.py:265
  121.8 3.9 %partial_sums.3 = (f32[512,768]{1,0:T(8,128)}, bf16[512,768]{1,0:T(8,128)(2,1)}) custom-call(s32[1]{0:T(128)} %bitcast.9.spot_ref, bf16[2048,128]{1,0:T(8,128)(2,1)} %spread_lists.1.id_ref, bf16[2048,2048]{1,0:T(8,128)(2,1)} %bitcast.19.arrived_ref), custom_call_target="tpu_custom_call" | custom-call | flops 402653184 | bytes 12582912 | tf_op jit(solution)/shard_map/partial_sums/pallas_call | solution.py:265
  125.7 3.5 %collective-permute-start.15 = (bf16[512,768]{1,0:T(8,128)(2,1)}, bf16[512,768]{1,0:T(8,128)(2,1)}, u32[]{:S(2)}, u32[]{:S(2)}) collective-permute-start(bf16[512,768]{1,0:T(8,128)(2,1)} %get-tuple-element.69), channel_id=1, source_target_pairs={{0,1},{1,0},{2,3},{3,2},{4,5},{5,4},{6,7},{7,6},{8,9},{9,8},{10,11... | collective-permute-start | bytes 2359304 | tf_op jit(solution)/shard_map/ppermute | solution.py:463
  129.3 3.6 %partial_sums.5 = (f32[512,640]{1,0:T(8,128)}, bf16[512,640]{1,0:T(8,128)(2,1)}) custom-call(s32[1]{0:T(128)} %bitcast.9.spot_ref, bf16[2048,128]{1,0:T(8,128)(2,1)} %spread_lists.1.id_ref, bf16[2048,2048]{1,0:T(8,128)(2,1)} %bitcast.19.arrived_ref), custom_call_target="tpu_custom_call" | custom-call | flops 335544320 | bytes 10485760 | tf_op jit(solution)/shard_map/partial_sums/pallas_call | solution.py:265
  135.4 5.6 %select_rows.3 = bf16[1024,2048]{1,0:T(8,128)(2,1)} custom-call(s32[1]{0:T(128)} %bitcast.9.spot_ref, bf16[2048,128]{1,0:T(8,128)(2,1)} %spread_lists.1.id_ref, bf16[512,768]{1,0:T(8,128)(2,1)} %copy-done.2, bf16[512,768]{1,0:T(8,128)(2,1)} %collective-permute-done.12.refs_1_, bf16[512,768]{1,0:T(8,128)(2,1)} %copy-done.1, bf16[512,768]{1,0:T(8,128)(2,1)} %copy-done.5, ...), custom_call_target="tpu_custom_call" | custom-call | flops 570425344 | bytes 13369344 | tf_op jit(solution)/shard_map/select_rows/pallas_call | solution.py:221
  141.0 10.5 %collective-permute-done.17 = bf16[512,640]{1,0:T(8,128)(2,1)S(1)} collective-permute-done((bf16[512,640]{1,0:T(8,128)(2,1)}, bf16[512,640]{1,0:T(8,128)(2,1)S(1)}, u32[]{:S(2)}, u32[]{:S(2)}) %collective-permute-start.17) | collective-permute-done | bytes 655392 | tf_op jit(solution)/shard_map/ppermute | solution.py:463
  156.5 6.2 %collective-permute-start.18 = (bf16[256,768]{1,0:T(8,128)(2,1)S(1)}, bf16[256,768]{1,0:T(8,128)(2,1)S(1)}, u32[]{:S(2)}, u32[]{:S(2)}) collective-permute-start(bf16[256,768]{1,0:T(8,128)(2,1)S(1)} %slice.135), channel_id=1, source_target_pairs={{0,4},{1,5},{2,6},{3,7},{4,0},{5,1},{6,2},{7,3},{8,12},{9,13},{10,... | collective-permute-start | bytes 1179656 | tf_op jit(solution)/shard_map/ppermute | solution.py:463
  166.1 5.5 %collective-permute-done.20 = bf16[256,640]{1,0:T(8,128)(2,1)S(1)} collective-permute-done((bf16[256,640]{1,0:T(8,128)(2,1)S(1)}, bf16[256,640]{1,0:T(8,128)(2,1)S(1)}, u32[]{:S(2)}, u32[]{:S(2)}) %collective-permute-start.20) | collective-permute-done | bytes 327712 | tf_op jit(solution)/shard_map/ppermute | solution.py:463
  173.1 4.6 %all-to-all-start.2 = ((bf16[8,128,2048]{2,1,0:T(8,128)(2,1)}), bf16[8,128,2048]{2,1,0:T(8,128)(2,1)}, u32[]{:S(2)}, u32[]{:S(2)}) async-start(bf16[8,128,2048]{2,1,0:T(8,128)(2,1)} %bitcast.29), calls=%async_computation.2 | async-start | bytes 8388608 | tf_op jit(solution)/shard_map/all_to_all | solution.py:480
  184.6 7.5 %read_and_scores.2 = (bf16[256,4096]{1,0:T(8,128)(2,1)}, bf16[256,4096]{1,0:T(8,128)(2,1)}, f32[256,1024]{1,0:T(8,128)}) custom-call(s32[1]{0:T(128)} %bitcast.core_ref, bf16[256,1024]{1,0:T(8,128)(2,1)} %get-tuple-element.55.packed_ref, bf16[1024,2048]{1,0:T(8,128)(2,1)} %collective-permute-done.21.fetched_ref, bf16[256,4096]{1,0:T(8,128)(2,1)} %gate_ref.3, ...), custom_call_target="tpu_custom_call" | custom-call | flops 2147483648 | bytes 9437184 | tf_op jit(solution)/shard_map/read_and_scores/pallas_call | solution.py:425
  192.1 11.1 %collective-permute-done.24 = bf16[128,640]{1,0:T(8,128)(2,1)} collective-permute-done((bf16[128,640]{1,0:T(8,128)(2,1)}, bf16[128,640]{1,0:T(8,128)(2,1)}, u32[]{:S(2)}, u32[]{:S(2)}) %collective-permute-start.24) | collective-permute-done | bytes 163872 | tf_op jit(solution)/shard_map/ppermute | solution.py:463
  208.2 8.0 %adam_rows.1 = (bf16[128,4096]{1,0:T(8,128)(2,1)}, f32[128,4096]{1,0:T(8,128)}, f32[128,4096]{1,0:T(8,128)}) custom-call(s32[1]{0:T(128)} %bitcast.core_ref, f32[128,2176]{1,0:T(8,128)} %copy-done, f32[128,2176]{1,0:T(8,128)} %copy-done, f32[128,2176]{1,0:T(8,128)} %copy-done.15, bf16[128,4096]{1,0:T(8,128)(2,1)} %value_ref.1, f32[128,4096]{1,0:T(8,128)} %first_ref.1, ...), custom_call_target="tpu_custom_call" | custom-call | flops 5242880 | bytes 14680064 | tf_op jit(solution)/shard_map/adam_rows/pallas_call | solution.py:311
  216.3 8.4 %read_and_scores.3 = (bf16[256,4096]{1,0:T(8,128)(2,1)}, bf16[256,4096]{1,0:T(8,128)(2,1)}, f32[32,256]{1,0:T(8,128)}) custom-call(s32[1]{0:T(128)} %bitcast.core_ref, bf16[256,1024]{1,0:T(8,128)(2,1)} %get-tuple-element.55.packed_ref, bf16[1024,2048]{1,0:T(8,128)(2,1)} %bitcast.23.fetched_ref, ...), custom_call_target="tpu_custom_call", output_to_operand_aliasing={{0}: (8, {}), {1}: (9, {})} | custom-call | flops 2147483648 | bytes 9437184 | tf_op jit(solution)/shard_map/read_and_scores/pallas_call | solution.py:425
  (148 shorter events, 53.7 us)
Async XLA Ops:
  1.4 15.0 %collective-permute-start = (s32[16,64]{0,1:T(8,128)S(1)}, s32[16,64]{0,1:T(8,128)S(1)}, u32[]{:S(2)}, u32[]{:S(2)}) collective-permute-start(s32[16,64]{0,1:T(8,128)S(1)} %copy.21), channel_id=1, source_target_pairs={{0,64},{64,0},{1,65},{65,1},{2,66},{66,2},{3,67},{67,3},{4,68},{68... | collective-permute-start | bytes 12296 | tf_op jit(solution)/shard_map/ppermute | solution.py:467
  3.8 18.2 %collective-permute-start.3 = (bf16[128,512]{1,0:T(8,128)(2,1)S(1)}, bf16[128,512]{1,0:T(8,128)(2,1)S(1)}, u32[]{:S(2)}, u32[]{:S(2)}) collective-permute-start(bf16[128,512]{1,0:T(8,128)(2,1)S(1)} %constant_dynamic-slice_fusion.2), channel_id=1, source_target_pairs={{0,1},{1,0},{2,3},{3,2},{4,5},{5,4},{6,7},{7,6},{8,9},{9,8},{10,11... | collective-permute-start | bytes 393224 | tf_op jit(solution)/shard_map/ppermute | solution.py:463
  8.8 13.3 %collective-permute-start.2 = (bf16[128,768]{1,0:T(8,128)(2,1)S(1)}, bf16[128,768]{1,0:T(8,128)(2,1)S(1)}, u32[]{:S(2)}, u32[]{:S(2)}) collective-permute-start(bf16[128,768]{1,0:T(8,128)(2,1)S(1)} %get-tuple-element.92), channel_id=1, source_target_pairs={{0,4},{1,5},{2,6},{3,7},{4,0},{5,1},{6,2},{7,3},{8,12},{9,13},{10,... | collective-permute-start | bytes 589832 | tf_op jit(solution)/shard_map/ppermute | solution.py:463
  11.3 10.7 %collective-permute-start.1 = (bf16[128,768]{1,0:T(8,128)(2,1)S(1)}, bf16[128,768]{1,0:T(8,128)(2,1)S(1)}, u32[]{:S(2)}, u32[]{:S(2)}) collective-permute-start(bf16[128,768]{1,0:T(8,128)(2,1)S(1)} %get-tuple-element.93), channel_id=1, source_target_pairs={{0,16},{1,17},{2,18},{3,19},{4,20},{5,21},{6,22},{7,23},{8,24},{9,... | collective-permute-start | bytes 589832 | tf_op jit(solution)/shard_map/ppermute | solution.py:463
  21.2 15.2 %collective-permute-start.7 = (bf16[256,2048]{1,0:T(8,128)(2,1)}, bf16[256,2048]{1,0:T(8,128)(2,1)S(1)}, u32[]{:S(2)}, u32[]{:S(2)}) collective-permute-start(bf16[256,2048]{1,0:T(8,128)(2,1)} %get-tuple-element.58), channel_id=1, source_target_pairs={{0,64},{64,0},{1,65},{65,1},{2,66},{66,2},{3,67},{67,3},{4,68},{68... | collective-permute-start | bytes 3145736 | tf_op jit(solution)/shard_map/ppermute | solution.py:467
  31.5 13.1 %collective-permute-start.10 = (bf16[256,768]{1,0:T(8,128)(2,1)S(1)}, bf16[256,768]{1,0:T(8,128)(2,1)}, u32[]{:S(2)}, u32[]{:S(2)}) collective-permute-start(bf16[256,768]{1,0:T(8,128)(2,1)S(1)} %pad_maximum_fusion.5), channel_id=1, source_target_pairs={{0,1},{1,0},{2,3},{3,2},{4,5},{5,4},{6,7},{7,6},{8,9},{9,8},{10,11... | collective-permute-start | bytes 1179656 | tf_op jit(solution)/shard_map/ppermute | solution.py:463
  31.5 13.1 %collective-permute-start.9 = (bf16[256,768]{1,0:T(8,128)(2,1)S(1)}, bf16[256,768]{1,0:T(8,128)(2,1)S(1)}, u32[]{:S(2)}, u32[]{:S(2)}) collective-permute-start(bf16[256,768]{1,0:T(8,128)(2,1)S(1)} %pad_maximum_fusion.4), channel_id=1, source_target_pairs={{0,4},{1,5},{2,6},{3,7},{4,0},{5,1},{6,2},{7,3},{8,12},{9,13},{10,... | collective-permute-start | bytes 1179656 | tf_op jit(solution)/shard_map/ppermute | solution.py:463
  34.3 10.3 %collective-permute-start.11 = (bf16[256,512]{1,0:T(8,128)(2,1)}, bf16[256,512]{1,0:T(8,128)(2,1)}, u32[]{:S(2)}, u32[]{:S(2)}) collective-permute-start(bf16[256,512]{1,0:T(8,128)(2,1)} %pad_maximum_fusion.6), channel_id=1, source_target_pairs={{0,16},{1,17},{2,18},{3,19},{4,20},{5,21},{6,22},{7,23},{8,24},{9,... | collective-permute-start | bytes 786440 | tf_op jit(solution)/shard_map/ppermute | solution.py:463
  35.6 9.0 %collective-permute-start.8 = (f32[4,16,128]{2,1,0:T(8,128)S(1)}, f32[4,16,128]{2,1,0:T(8,128)S(1)}, u32[]{:S(2)}, u32[]{:S(2)}) collective-permute-start(f32[4,16,128]{2,1,0:T(8,128)S(1)} %pad_maximum_fusion.7), channel_id=1, source_target_pairs={{0,3},{1,2},{2,1},{3,0},{4,7},{5,6},{6,5},{7,4},{8,11},{9,10},{10,... | collective-permute-start | bytes 98312 | tf_op jit(solution)/shard_map/ppermute | solution.py:463
  45.4 68.0 %all-to-all-start = ((bf16[8,256,2048]{2,1,0:T(8,128)(2,1)}), bf16[8,256,2048]{2,1,0:T(8,128)(2,1)}, u32[]{:S(2)}, u32[]{:S(2)}) async-start(bf16[8,256,2048]{2,1,0:T(8,128)(2,1)} %bitcast.28), calls=%async_computation | async-start | bytes 16777216 | tf_op jit(solution)/shard_map/all_to_all | solution.py:480
  51.9 21.1 %collective-permute-start.13 = (bf16[512,768]{1,0:T(8,128)(2,1)S(1)}, bf16[512,768]{1,0:T(8,128)(2,1)S(1)}, u32[]{:S(2)}, u32[]{:S(2)}) collective-permute-start(bf16[512,768]{1,0:T(8,128)(2,1)S(1)} %pad_maximum_fusion.2.refs_2_), channel_id=1, source_target_pairs={{0,16},{1,17},{2,18},{3,19},{4,20},{5,21},{6,22},{7,23},{8,24},{9,... | collective-permute-start | bytes 2359304 | tf_op jit(solution)/shard_map/ppermute | solution.py:463
  53.4 54.3 %collective-permute-start.12 = (bf16[512,768]{1,0:T(8,128)(2,1)S(1)}, bf16[512,768]{1,0:T(8,128)(2,1)}, u32[]{:S(2)}, u32[]{:S(2)}) collective-permute-start(bf16[512,768]{1,0:T(8,128)(2,1)S(1)} %pad_maximum_fusion.1.refs_0_), channel_id=1, source_target_pairs={{0,1},{1,0},{2,3},{3,2},{4,5},{5,4},{6,7},{7,6},{8,9},{9,8},{10,11... | collective-permute-start | bytes 2359304 | tf_op jit(solution)/shard_map/ppermute | solution.py:463
  57.6 15.4 %collective-permute-start.14 = (bf16[512,512]{1,0:T(8,128)(2,1)S(1)}, bf16[512,512]{1,0:T(8,128)(2,1)S(1)}, u32[]{:S(2)}, u32[]{:S(2)}) collective-permute-start(bf16[512,512]{1,0:T(8,128)(2,1)S(1)} %pad_maximum_fusion.3.refs_4_), channel_id=1, source_target_pairs={{0,4},{1,5},{2,6},{3,7},{4,0},{5,1},{6,2},{7,3},{8,12},{9,13},{10,... | collective-permute-start | bytes 1572872 | tf_op jit(solution)/shard_map/ppermute | solution.py:463
  113.4 59.7 %all-to-all-start.1 = ((bf16[8,128,2048]{2,1,0:T(8,128)(2,1)}), bf16[8,128,2048]{2,1,0:T(8,128)(2,1)}, u32[]{:S(2)}, u32[]{:S(2)}) async-start(bf16[8,128,2048]{2,1,0:T(8,128)(2,1)} %bitcast.30), calls=%async_computation.1 | async-start | bytes 8388608 | tf_op jit(solution)/shard_map/all_to_all | solution.py:480
  121.8 29.7 %collective-permute-start.16 = (bf16[512,768]{1,0:T(8,128)(2,1)}, bf16[512,768]{1,0:T(8,128)(2,1)S(1)}, u32[]{:S(2)}, u32[]{:S(2)}) collective-permute-start(bf16[512,768]{1,0:T(8,128)(2,1)} %get-tuple-element.70), channel_id=1, source_target_pairs={{0,16},{1,17},{2,18},{3,19},{4,20},{5,21},{6,22},{7,23},{8,24},{9,... | collective-permute-start | bytes 2359304 | tf_op jit(solution)/shard_map/ppermute | solution.py:463
  125.7 27.8 %collective-permute-start.15 = (bf16[512,768]{1,0:T(8,128)(2,1)}, bf16[512,768]{1,0:T(8,128)(2,1)}, u32[]{:S(2)}, u32[]{:S(2)}) collective-permute-start(bf16[512,768]{1,0:T(8,128)(2,1)} %get-tuple-element.69), channel_id=1, source_target_pairs={{0,1},{1,0},{2,3},{3,2},{4,5},{5,4},{6,7},{7,6},{8,9},{9,8},{10,11... | collective-permute-start | bytes 2359304 | tf_op jit(solution)/shard_map/ppermute | solution.py:463
  132.9 18.7 %collective-permute-start.17 = (bf16[512,640]{1,0:T(8,128)(2,1)}, bf16[512,640]{1,0:T(8,128)(2,1)S(1)}, u32[]{:S(2)}, u32[]{:S(2)}) collective-permute-start(bf16[512,640]{1,0:T(8,128)(2,1)} %get-tuple-element.71), channel_id=1, source_target_pairs={{0,4},{1,5},{2,6},{3,7},{4,0},{5,1},{6,2},{7,3},{8,12},{9,13},{10,... | collective-permute-start | bytes 1966088 | tf_op jit(solution)/shard_map/ppermute | solution.py:463
  156.5 15.2 %collective-permute-start.18 = (bf16[256,768]{1,0:T(8,128)(2,1)S(1)}, bf16[256,768]{1,0:T(8,128)(2,1)S(1)}, u32[]{:S(2)}, u32[]{:S(2)}) collective-permute-start(bf16[256,768]{1,0:T(8,128)(2,1)S(1)} %slice.135), channel_id=1, source_target_pairs={{0,4},{1,5},{2,6},{3,7},{4,0},{5,1},{6,2},{7,3},{8,12},{9,13},{10,... | collective-permute-start | bytes 1179656 | tf_op jit(solution)/shard_map/ppermute | solution.py:463
  162.6 10.5 %collective-permute-start.19 = (bf16[256,768]{1,0:T(8,128)(2,1)S(1)}, bf16[256,768]{1,0:T(8,128)(2,1)S(1)}, u32[]{:S(2)}, u32[]{:S(2)}) collective-permute-start(bf16[256,768]{1,0:T(8,128)(2,1)S(1)} %slice.134), channel_id=1, source_target_pairs={{0,1},{1,0},{2,3},{3,2},{4,5},{5,4},{6,7},{7,6},{8,9},{9,8},{10,11... | collective-permute-start | bytes 1179656 | tf_op jit(solution)/shard_map/ppermute | solution.py:463
  173.1 11.5 %collective-permute-start.21 = (bf16[1024,2048]{1,0:T(8,128)(2,1)}, bf16[1024,2048]{1,0:T(8,128)(2,1)}, u32[]{:S(2)}, u32[]{:S(2)}) collective-permute-start(bf16[1024,2048]{1,0:T(8,128)(2,1)} %bitcast.21), channel_id=1, source_target_pairs={{0,64},{64,0},{1,65},{65,1},{2,66},{66,2},{3,67},{67,3},{4,68},{68... | collective-permute-start | bytes 12582920 | tf_op jit(solution)/shard_map/ppermute | solution.py:467
  173.1 43.2 %all-to-all-start.2 = ((bf16[8,128,2048]{2,1,0:T(8,128)(2,1)}), bf16[8,128,2048]{2,1,0:T(8,128)(2,1)}, u32[]{:S(2)}, u32[]{:S(2)}) async-start(bf16[8,128,2048]{2,1,0:T(8,128)(2,1)} %bitcast.29), calls=%async_computation.2 | async-start | bytes 8388608 | tf_op jit(solution)/shard_map/all_to_all | solution.py:480
  179.9 23.3 %collective-permute-start.24 = (bf16[128,640]{1,0:T(8,128)(2,1)}, bf16[128,640]{1,0:T(8,128)(2,1)}, u32[]{:S(2)}, u32[]{:S(2)}) collective-permute-start(bf16[128,640]{1,0:T(8,128)(2,1)} %slice.139), channel_id=1, source_target_pairs={{0,1},{1,0},{2,3},{3,2},{4,5},{5,4},{6,7},{7,6},{8,9},{9,8},{10,11... | collective-permute-start | bytes 491528 | tf_op jit(solution)/shard_map/ppermute | solution.py:463
  182.1 21.1 %collective-permute-start.22 = (bf16[128,768]{1,0:T(8,128)(2,1)S(1)}, bf16[128,768]{1,0:T(8,128)(2,1)S(1)}, u32[]{:S(2)}, u32[]{:S(2)}) collective-permute-start(bf16[128,768]{1,0:T(8,128)(2,1)S(1)} %slice.138), channel_id=1, source_target_pairs={{0,16},{1,17},{2,18},{3,19},{4,20},{5,21},{6,22},{7,23},{8,24},{9,... | collective-permute-start | bytes 589832 | tf_op jit(solution)/shard_map/ppermute | solution.py:463
  184.4 18.8 %collective-permute-start.23 = (bf16[128,768]{1,0:T(8,128)(2,1)S(1)}, bf16[128,768]{1,0:T(8,128)(2,1)S(1)}, u32[]{:S(2)}, u32[]{:S(2)}) collective-permute-start(bf16[128,768]{1,0:T(8,128)(2,1)S(1)} %slice.137), channel_id=1, source_target_pairs={{0,4},{1,5},{2,6},{3,7},{4,0},{5,1},{6,2},{7,3},{8,12},{9,13},{10,... | collective-permute-start | bytes 589832 | tf_op jit(solution)/shard_map/ppermute | solution.py:463
  (31 other events, 315.6 us)

commit v7 on v5

--- a/solution.py
+++ b/solution.py
@@ -526,7 +526,7 @@
     parts = [jnp.concatenate(pair, axis=0) for pair in zip(parts, swapped)]
     swapped = [swap(part, order[1]) for part, order in zip(parts, ORDERS)]
     slot = (slot_of_pick % table_size) * capacity + slot_of_pick // table_size
-    (slot,) = after(parts, [slot])
+    (slot,) = after([*parts, lists], [slot])
     packed, weight = pack_call(pick_logits, slot, slot_count)
     packed_other = swap_cores(packed)
     (crossed,) = after([packed], [crossed])

time: 224 us -> 221 us (0.987)
    unnamed x59 -> x60, local copies, waits for them, and re-layouts: 11 us -> 11 us
where the time goes in v7:
time: 221 us; the launch traced here: 220 us
  waiting for transfers between devices  76.9 us (35%)
  Pallas kernels  65.6 us (30%)
  starting transfers between devices  53.9 us (24%)
  local copies, waits for them, and re-layouts  16.4 us (7%)
  other arithmetic  5.88 us (3%)
    ppermute x21, waiting for transfers between devices, swap(): return lax.ppermute(x, ('batch', 'table'), pairs)  75.5 us
    ppermute x21, starting transfers between devices, swap(): return lax.ppermute(x, ('batch', 'table'), pairs)  34 us
    pallas_call x2, Pallas kernels, read_call(): pl.pallas_call(functools.partial(read_kernel, own), grid_spec=pltpu.Prefe...  15.9 us
    all_to_all x3, starting transfers between devices, cube_exchange(): lax.all_to_all(x, ('batch', 'table'), split_axis=0, concat_axis=0, axis_i...  14.2 us
    pallas_call x3, Pallas kernels, partial_call(): pl.pallas_call(functools.partial(partial_kernel, chunk), grid=(1,), in_sp...  11.4 us
    pallas_call x2, Pallas kernels, select_call(): pl.pallas_call(functools.partial(select_kernel, group), grid=(len(ORDERS)...  11.3 us
    unnamed x60, local copies, waits for them, and re-layouts  11 us
    pallas_call x1, Pallas kernels, adam_call(): pl.pallas_call(adam_kernel, grid_spec=pltpu.PrefetchScalarGridSpec(num_sc...  8.04 us
  transfers between devices with their start and end apart: 29, of which 10 were waited for; matrix products, arithmetic and copies ran while one was open for 6% of the time, Pallas kernels for 26%

profile of v7, /device:TPU:1, one launch (start us, length us, event | category | flops | bytes accessed | tf_op | source)
XLA Modules:
  0.0 220.1 jit_solution(13096119331765642300)
XLA Ops:
  3.8 3.9 %collective-permute-start.3 = (bf16[128,512]{1,0:T(8,128)(2,1)S(1)}, bf16[128,512]{1,0:T(8,128)(2,1)S(1)}, u32[]{:S(2)}, u32[]{:S(2)}) collective-permute-start(bf16[128,512]{1,0:T(8,128)(2,1)S(1)} %constant_dynamic-slice_fusion.2), channel_id=1, source_target_pairs={{0,1},{1,0},{2,3},{3,2},{4,5},{5,4},{6,7},{7,6},{8,9},{9,8},{10,11... | collective-permute-start | bytes 393224 | tf_op jit(solution)/shard_map/ppermute | solution.py:463
  11.3 2.7 %collective-permute-start.1 = (bf16[128,768]{1,0:T(8,128)(2,1)S(1)}, bf16[128,768]{1,0:T(8,128)(2,1)S(1)}, u32[]{:S(2)}, u32[]{:S(2)}) collective-permute-start(bf16[128,768]{1,0:T(8,128)(2,1)S(1)} %get-tuple-element.93), channel_id=1, source_target_pairs={{0,16},{1,17},{2,18},{3,19},{4,20},{5,21},{6,22},{7,23},{8,24},{9,... | collective-permute-start | bytes 589832 | tf_op jit(solution)/shard_map/ppermute | solution.py:463
  17.7 4.4 %gated_halves.1 = (bf16[256,2048]{1,0:T(8,128)(2,1)}, bf16[256,2048]{1,0:T(8,128)(2,1)}) custom-call(s32[1]{0:T(128)} %bitcast.core_ref, bf16[256,4096]{1,0:T(8,128)(2,1)} %gate_ref.3, bf16[256,4096]{1,0:T(8,128)(2,1)} %grad_ref.3, bf16[256,4096]{1,0:T(8,128)(2,1)} %gate_ref.3, bf16[256,4096]{1,0:T(8,128)(2,1)} %grad_ref.3), custom_call_target="tpu_custom_call" | custom-call | flops 4194304 | bytes 6291456 | tf_op jit(solution)/shard_map/gated_halves/pallas_call | solution.py:92
  23.0 5.7 %pack_weights.1 = (bf16[256,1024]{1,0:T(8,128)(2,1)}, f32[256,32]{1,0:T(8,128)}) custom-call(f32[256,32]{1,0:T(8,128)} %copy.29.logit_ref, s32[256,32]{1,0:T(8,128)} %fusion.1.slot_ref), custom_call_target="tpu_custom_call" | custom-call | flops 33554432 | bytes 1048576 | tf_op jit(solution)/shard_map/pack_weights/pallas_call | solution.py:65
  31.2 2.9 %collective-permute-done.5 = f32[2,16,128]{2,1,0:T(8,128)S(1)} collective-permute-done((f32[2,16,128]{2,1,0:T(8,128)S(1)}, f32[2,16,128]{2,1,0:T(8,128)S(1)}, u32[]{:S(2)}, u32[]{:S(2)}) %collective-permute-start.5) | collective-permute-done | bytes 16416 | tf_op jit(solution)/shard_map/ppermute | solution.py:463
  36.6 7.2 %slot_gradients.1 = bf16[2048,2048]{1,0:T(8,128)(2,1)} custom-call(s32[1]{0:T(128)} %bitcast.core_ref, bf16[256,1024]{1,0:T(8,128)(2,1)} %get-tuple-element.56.packed_ref, bf16[256,1024]{1,0:T(8,128)(2,1)} %copy-done.19, bf16[256,2048]{1,0:T(8,128)(2,1)} %get-tuple-element.50.gated_ref, bf16[256,2048]{1,0:T(8,128)(2,1)} %copy-done.16), custom_call_target="tpu_custom_call" | custom-call | flops 2147483648 | bytes 14680064 | tf_op jit(solution)/shard_map/slot_gradients/pallas_call | solution.py:139
  44.6 5.0 %all-to-all-start = ((bf16[8,256,2048]{2,1,0:T(8,128)(2,1)}), bf16[8,256,2048]{2,1,0:T(8,128)(2,1)}, u32[]{:S(2)}, u32[]{:S(2)}) async-start(bf16[8,256,2048]{2,1,0:T(8,128)(2,1)} %bitcast.28), calls=%async_computation | async-start | bytes 16777216 | tf_op jit(solution)/shard_map/all_to_all | solution.py:480
  60.3 10.4 %collective-permute-done.14.refs_5_ = bf16[512,512]{1,0:T(8,128)(2,1)S(1)} collective-permute-done((bf16[512,512]{1,0:T(8,128)(2,1)S(1)}, bf16[512,512]{1,0:T(8,128)(2,1)S(1)}, u32[]{:S(2)}, u32[]{:S(2)}) %collective-permute-start.14) | collective-permute-done | bytes 524320 | tf_op jit(solution)/shard_map/ppermute | solution.py:463
  71.1 34.3 %collective-permute-done.12.refs_1_ = bf16[512,768]{1,0:T(8,128)(2,1)} collective-permute-done((bf16[512,768]{1,0:T(8,128)(2,1)S(1)}, bf16[512,768]{1,0:T(8,128)(2,1)}, u32[]{:S(2)}, u32[]{:S(2)}) %collective-permute-start.12) | collective-permute-done | bytes 786464 | tf_op jit(solution)/shard_map/ppermute | solution.py:463
  105.4 5.6 %select_rows.2 = bf16[1024,2048]{1,0:T(8,128)(2,1)} custom-call(s32[1]{0:T(128)} %bitcast.9.spot_ref, bf16[2048,128]{1,0:T(8,128)(2,1)} %spread_lists.1.id_ref, bf16[512,768]{1,0:T(8,128)(2,1)} %copy-done.2, bf16[512,768]{1,0:T(8,128)(2,1)} %collective-permute-done.12.refs_1_, bf16[512,768]{1,0:T(8,128)(2,1)} %copy-done.1, bf16[512,768]{1,0:T(8,128)(2,1)} %copy-done.5, ...), custom_call_target="tpu_custom_call" | custom-call | flops 570425344 | bytes 13369344 | tf_op jit(solution)/shard_map/select_rows/pallas_call | solution.py:221
  111.0 4.5 %all-to-all-start.1 = ((bf16[8,128,2048]{2,1,0:T(8,128)(2,1)}), bf16[8,128,2048]{2,1,0:T(8,128)(2,1)}, u32[]{:S(2)}, u32[]{:S(2)}) async-start(bf16[8,128,2048]{2,1,0:T(8,128)(2,1)} %bitcast.30), calls=%async_computation.1 | async-start | bytes 8388608 | tf_op jit(solution)/shard_map/all_to_all | solution.py:480
  115.6 3.9 %partial_sums.4 = (f32[512,768]{1,0:T(8,128)}, bf16[512,768]{1,0:T(8,128)(2,1)}) custom-call(s32[1]{0:T(128)} %bitcast.9.spot_ref, bf16[2048,128]{1,0:T(8,128)(2,1)} %spread_lists.1.id_ref, bf16[2048,2048]{1,0:T(8,128)(2,1)} %bitcast.19.arrived_ref), custom_call_target="tpu_custom_call" | custom-call | flops 402653184 | bytes 12582912 | tf_op jit(solution)/shard_map/partial_sums/pallas_call | solution.py:265
  119.6 3.9 %partial_sums.3 = (f32[512,768]{1,0:T(8,128)}, bf16[512,768]{1,0:T(8,128)(2,1)}) custom-call(s32[1]{0:T(128)} %bitcast.9.spot_ref, bf16[2048,128]{1,0:T(8,128)(2,1)} %spread_lists.1.id_ref, bf16[2048,2048]{1,0:T(8,128)(2,1)} %bitcast.19.arrived_ref), custom_call_target="tpu_custom_call" | custom-call | flops 402653184 | bytes 12582912 | tf_op jit(solution)/shard_map/partial_sums/pallas_call | solution.py:265
  123.5 3.5 %collective-permute-start.15 = (bf16[512,768]{1,0:T(8,128)(2,1)}, bf16[512,768]{1,0:T(8,128)(2,1)S(1)}, u32[]{:S(2)}, u32[]{:S(2)}) collective-permute-start(bf16[512,768]{1,0:T(8,128)(2,1)} %get-tuple-element.69), channel_id=1, source_target_pairs={{0,1},{1,0},{2,3},{3,2},{4,5},{5,4},{6,7},{7,6},{8,9},{9,8},{10,11... | collective-permute-start | bytes 2359304 | tf_op jit(solution)/shard_map/ppermute | solution.py:463
  127.1 3.6 %partial_sums.5 = (f32[512,640]{1,0:T(8,128)}, bf16[512,640]{1,0:T(8,128)(2,1)}) custom-call(s32[1]{0:T(128)} %bitcast.9.spot_ref, bf16[2048,128]{1,0:T(8,128)(2,1)} %spread_lists.1.id_ref, bf16[2048,2048]{1,0:T(8,128)(2,1)} %bitcast.19.arrived_ref), custom_call_target="tpu_custom_call" | custom-call | flops 335544320 | bytes 10485760 | tf_op jit(solution)/shard_map/partial_sums/pallas_call | solution.py:265
  133.1 5.6 %select_rows.3 = bf16[1024,2048]{1,0:T(8,128)(2,1)} custom-call(s32[1]{0:T(128)} %bitcast.9.spot_ref, bf16[2048,128]{1,0:T(8,128)(2,1)} %spread_lists.1.id_ref, bf16[512,768]{1,0:T(8,128)(2,1)} %copy-done.2, bf16[512,768]{1,0:T(8,128)(2,1)} %collective-permute-done.12.refs_1_, bf16[512,768]{1,0:T(8,128)(2,1)} %copy-done.1, bf16[512,768]{1,0:T(8,128)(2,1)} %copy-done.5, ...), custom_call_target="tpu_custom_call" | custom-call | flops 570425344 | bytes 13369344 | tf_op jit(solution)/shard_map/select_rows/pallas_call | solution.py:221
  138.7 10.4 %collective-permute-done.17 = bf16[512,640]{1,0:T(8,128)(2,1)S(1)} collective-permute-done((bf16[512,640]{1,0:T(8,128)(2,1)}, bf16[512,640]{1,0:T(8,128)(2,1)S(1)}, u32[]{:S(2)}, u32[]{:S(2)}) %collective-permute-start.17) | collective-permute-done | bytes 655392 | tf_op jit(solution)/shard_map/ppermute | solution.py:463
  154.4 3.6 %collective-permute-start.19 = (bf16[1024,2048]{1,0:T(8,128)(2,1)}, bf16[1024,2048]{1,0:T(8,128)(2,1)}, u32[]{:S(2)}, u32[]{:S(2)}) collective-permute-start(bf16[1024,2048]{1,0:T(8,128)(2,1)} %bitcast.21), channel_id=1, source_target_pairs={{0,64},{64,0},{1,65},{65,1},{2,66},{66,2},{3,67},{67,3},{4,68},{68... | collective-permute-start | bytes 12582920 | tf_op jit(solution)/shard_map/ppermute | solution.py:467
  162.7 5.5 %collective-permute-done.23 = bf16[256,640]{1,0:T(8,128)(2,1)S(1)} collective-permute-done((bf16[256,640]{1,0:T(8,128)(2,1)}, bf16[256,640]{1,0:T(8,128)(2,1)S(1)}, u32[]{:S(2)}, u32[]{:S(2)}) %collective-permute-start.23) | collective-permute-done | bytes 327712 | tf_op jit(solution)/shard_map/ppermute | solution.py:463
  169.8 4.7 %all-to-all-start.2 = ((bf16[8,128,2048]{2,1,0:T(8,128)(2,1)}), bf16[8,128,2048]{2,1,0:T(8,128)(2,1)}, u32[]{:S(2)}, u32[]{:S(2)}) async-start(bf16[8,128,2048]{2,1,0:T(8,128)(2,1)} %bitcast.29), calls=%async_computation.2 | async-start | bytes 8388608 | tf_op jit(solution)/shard_map/all_to_all | solution.py:480
  181.6 7.5 %read_and_scores.2 = (bf16[256,4096]{1,0:T(8,128)(2,1)}, bf16[256,4096]{1,0:T(8,128)(2,1)}, f32[256,1024]{1,0:T(8,128)}) custom-call(s32[1]{0:T(128)} %bitcast.core_ref, bf16[256,1024]{1,0:T(8,128)(2,1)} %get-tuple-element.56.packed_ref, bf16[1024,2048]{1,0:T(8,128)(2,1)} %collective-permute-done.19.fetched_ref, bf16[256,4096]{1,0:T(8,128)(2,1)} %gate_ref.3, ...), custom_call_target="tpu_custom_call" | custom-call | flops 2147483648 | bytes 9437184 | tf_op jit(solution)/shard_map/read_and_scores/pallas_call | solution.py:425
  189.1 10.4 %collective-permute-done.24 = bf16[128,640]{1,0:T(8,128)(2,1)S(1)} collective-permute-done((bf16[128,640]{1,0:T(8,128)(2,1)S(1)}, bf16[128,640]{1,0:T(8,128)(2,1)S(1)}, u32[]{:S(2)}, u32[]{:S(2)}) %collective-permute-start.24) | collective-permute-done | bytes 163872 | tf_op jit(solution)/shard_map/ppermute | solution.py:463
  203.6 8.0 %adam_rows.1 = (bf16[128,4096]{1,0:T(8,128)(2,1)}, f32[128,4096]{1,0:T(8,128)}, f32[128,4096]{1,0:T(8,128)}) custom-call(s32[1]{0:T(128)} %bitcast.core_ref, f32[128,2176]{1,0:T(8,128)} %copy-done, f32[128,2176]{1,0:T(8,128)} %copy-done, f32[128,2176]{1,0:T(8,128)} %copy-done.15, bf16[128,4096]{1,0:T(8,128)(2,1)} %value_ref.1, f32[128,4096]{1,0:T(8,128)} %first_ref.1, ...), custom_call_target="tpu_custom_call" | custom-call | flops 5242880 | bytes 14680064 | tf_op jit(solution)/shard_map/adam_rows/pallas_call | solution.py:311
  211.6 8.4 %read_and_scores.3 = (bf16[256,4096]{1,0:T(8,128)(2,1)}, bf16[256,4096]{1,0:T(8,128)(2,1)}, f32[32,256]{1,0:T(8,128)}) custom-call(s32[1]{0:T(128)} %bitcast.core_ref, bf16[256,1024]{1,0:T(8,128)(2,1)} %get-tuple-element.56.packed_ref, bf16[1024,2048]{1,0:T(8,128)(2,1)} %bitcast.23.fetched_ref, ...), custom_call_target="tpu_custom_call", output_to_operand_aliasing={{0}: (8, {}), {1}: (9, {})} | custom-call | flops 2147483648 | bytes 9437184 | tf_op jit(solution)/shard_map/read_and_scores/pallas_call | solution.py:425
  (153 shorter events, 53.1 us)
Async XLA Ops:
  1.4 15.8 %collective-permute-start = (s32[16,64]{0,1:T(8,128)S(1)}, s32[16,64]{0,1:T(8,128)S(1)}, u32[]{:S(2)}, u32[]{:S(2)}) collective-permute-start(s32[16,64]{0,1:T(8,128)S(1)} %copy.21), channel_id=1, source_target_pairs={{0,64},{64,0},{1,65},{65,1},{2,66},{66,2},{3,67},{67,3},{4,68},{68... | collective-permute-start | bytes 12296 | tf_op jit(solution)/shard_map/ppermute | solution.py:467
  3.8 18.3 %collective-permute-start.3 = (bf16[128,512]{1,0:T(8,128)(2,1)S(1)}, bf16[128,512]{1,0:T(8,128)(2,1)S(1)}, u32[]{:S(2)}, u32[]{:S(2)}) collective-permute-start(bf16[128,512]{1,0:T(8,128)(2,1)S(1)} %constant_dynamic-slice_fusion.2), channel_id=1, source_target_pairs={{0,1},{1,0},{2,3},{3,2},{4,5},{5,4},{6,7},{7,6},{8,9},{9,8},{10,11... | collective-permute-start | bytes 393224 | tf_op jit(solution)/shard_map/ppermute | solution.py:463
  8.8 13.4 %collective-permute-start.2 = (bf16[128,768]{1,0:T(8,128)(2,1)S(1)}, bf16[128,768]{1,0:T(8,128)(2,1)S(1)}, u32[]{:S(2)}, u32[]{:S(2)}) collective-permute-start(bf16[128,768]{1,0:T(8,128)(2,1)S(1)} %get-tuple-element.92), channel_id=1, source_target_pairs={{0,4},{1,5},{2,6},{3,7},{4,0},{5,1},{6,2},{7,3},{8,12},{9,13},{10,... | collective-permute-start | bytes 589832 | tf_op jit(solution)/shard_map/ppermute | solution.py:463
  11.3 10.8 %collective-permute-start.1 = (bf16[128,768]{1,0:T(8,128)(2,1)S(1)}, bf16[128,768]{1,0:T(8,128)(2,1)S(1)}, u32[]{:S(2)}, u32[]{:S(2)}) collective-permute-start(bf16[128,768]{1,0:T(8,128)(2,1)S(1)} %get-tuple-element.93), channel_id=1, source_target_pairs={{0,16},{1,17},{2,18},{3,19},{4,20},{5,21},{6,22},{7,23},{8,24},{9,... | collective-permute-start | bytes 589832 | tf_op jit(solution)/shard_map/ppermute | solution.py:463
  22.1 13.5 %collective-permute-start.7 = (bf16[256,2048]{1,0:T(8,128)(2,1)}, bf16[256,2048]{1,0:T(8,128)(2,1)S(1)}, u32[]{:S(2)}, u32[]{:S(2)}) collective-permute-start(bf16[256,2048]{1,0:T(8,128)(2,1)} %get-tuple-element.58), channel_id=1, source_target_pairs={{0,64},{64,0},{1,65},{65,1},{2,66},{66,2},{3,67},{67,3},{4,68},{68... | collective-permute-start | bytes 3145736 | tf_op jit(solution)/shard_map/ppermute | solution.py:467
  29.1 14.7 %collective-permute-start.10 = (bf16[256,768]{1,0:T(8,128)(2,1)S(1)}, bf16[256,768]{1,0:T(8,128)(2,1)}, u32[]{:S(2)}, u32[]{:S(2)}) collective-permute-start(bf16[256,768]{1,0:T(8,128)(2,1)S(1)} %pad_maximum_fusion.5), channel_id=1, source_target_pairs={{0,1},{1,0},{2,3},{3,2},{4,5},{5,4},{6,7},{7,6},{8,9},{9,8},{10,11... | collective-permute-start | bytes 1179656 | tf_op jit(solution)/shard_map/ppermute | solution.py:463
  29.1 14.7 %collective-permute-start.9 = (bf16[256,768]{1,0:T(8,128)(2,1)S(1)}, bf16[256,768]{1,0:T(8,128)(2,1)S(1)}, u32[]{:S(2)}, u32[]{:S(2)}) collective-permute-start(bf16[256,768]{1,0:T(8,128)(2,1)S(1)} %pad_maximum_fusion.4), channel_id=1, source_target_pairs={{0,4},{1,5},{2,6},{3,7},{4,0},{5,1},{6,2},{7,3},{8,12},{9,13},{10,... | collective-permute-start | bytes 1179656 | tf_op jit(solution)/shard_map/ppermute | solution.py:463
  34.1 9.8 %collective-permute-start.11 = (bf16[256,512]{1,0:T(8,128)(2,1)}, bf16[256,512]{1,0:T(8,128)(2,1)}, u32[]{:S(2)}, u32[]{:S(2)}) collective-permute-start(bf16[256,512]{1,0:T(8,128)(2,1)} %pad_maximum_fusion.6), channel_id=1, source_target_pairs={{0,16},{1,17},{2,18},{3,19},{4,20},{5,21},{6,22},{7,23},{8,24},{9,... | collective-permute-start | bytes 786440 | tf_op jit(solution)/shard_map/ppermute | solution.py:463
  34.9 9.0 %collective-permute-start.8 = (f32[4,16,128]{2,1,0:T(8,128)S(1)}, f32[4,16,128]{2,1,0:T(8,128)S(1)}, u32[]{:S(2)}, u32[]{:S(2)}) collective-permute-start(f32[4,16,128]{2,1,0:T(8,128)S(1)} %pad_maximum_fusion.7), channel_id=1, source_target_pairs={{0,3},{1,2},{2,1},{3,0},{4,7},{5,6},{6,5},{7,4},{8,11},{9,10},{10,... | collective-permute-start | bytes 98312 | tf_op jit(solution)/shard_map/ppermute | solution.py:463
  44.6 66.5 %all-to-all-start = ((bf16[8,256,2048]{2,1,0:T(8,128)(2,1)}), bf16[8,256,2048]{2,1,0:T(8,128)(2,1)}, u32[]{:S(2)}, u32[]{:S(2)}) async-start(bf16[8,256,2048]{2,1,0:T(8,128)(2,1)} %bitcast.28), calls=%async_computation | async-start | bytes 16777216 | tf_op jit(solution)/shard_map/all_to_all | solution.py:480
  51.1 20.0 %collective-permute-start.13 = (bf16[512,768]{1,0:T(8,128)(2,1)S(1)}, bf16[512,768]{1,0:T(8,128)(2,1)S(1)}, u32[]{:S(2)}, u32[]{:S(2)}) collective-permute-start(bf16[512,768]{1,0:T(8,128)(2,1)S(1)} %pad_maximum_fusion.2.refs_2_), channel_id=1, source_target_pairs={{0,16},{1,17},{2,18},{3,19},{4,20},{5,21},{6,22},{7,23},{8,24},{9,... | collective-permute-start | bytes 2359304 | tf_op jit(solution)/shard_map/ppermute | solution.py:463
  53.2 52.2 %collective-permute-start.12 = (bf16[512,768]{1,0:T(8,128)(2,1)S(1)}, bf16[512,768]{1,0:T(8,128)(2,1)}, u32[]{:S(2)}, u32[]{:S(2)}) collective-permute-start(bf16[512,768]{1,0:T(8,128)(2,1)S(1)} %pad_maximum_fusion.1.refs_0_), channel_id=1, source_target_pairs={{0,1},{1,0},{2,3},{3,2},{4,5},{5,4},{6,7},{7,6},{8,9},{9,8},{10,11... | collective-permute-start | bytes 2359304 | tf_op jit(solution)/shard_map/ppermute | solution.py:463
  55.3 15.4 %collective-permute-start.14 = (bf16[512,512]{1,0:T(8,128)(2,1)S(1)}, bf16[512,512]{1,0:T(8,128)(2,1)S(1)}, u32[]{:S(2)}, u32[]{:S(2)}) collective-permute-start(bf16[512,512]{1,0:T(8,128)(2,1)S(1)} %pad_maximum_fusion.3.refs_4_), channel_id=1, source_target_pairs={{0,4},{1,5},{2,6},{3,7},{4,0},{5,1},{6,2},{7,3},{8,12},{9,13},{10,... | collective-permute-start | bytes 1572872 | tf_op jit(solution)/shard_map/ppermute | solution.py:463
  111.0 43.4 %all-to-all-start.1 = ((bf16[8,128,2048]{2,1,0:T(8,128)(2,1)}), bf16[8,128,2048]{2,1,0:T(8,128)(2,1)}, u32[]{:S(2)}, u32[]{:S(2)}) async-start(bf16[8,128,2048]{2,1,0:T(8,128)(2,1)} %bitcast.30), calls=%async_computation.1 | async-start | bytes 8388608 | tf_op jit(solution)/shard_map/all_to_all | solution.py:480
  119.5 29.5 %collective-permute-start.16 = (bf16[512,768]{1,0:T(8,128)(2,1)}, bf16[512,768]{1,0:T(8,128)(2,1)S(1)}, u32[]{:S(2)}, u32[]{:S(2)}) collective-permute-start(bf16[512,768]{1,0:T(8,128)(2,1)} %get-tuple-element.70), channel_id=1, source_target_pairs={{0,16},{1,17},{2,18},{3,19},{4,20},{5,21},{6,22},{7,23},{8,24},{9,... | collective-permute-start | bytes 2359304 | tf_op jit(solution)/shard_map/ppermute | solution.py:463
  123.5 26.7 %collective-permute-start.15 = (bf16[512,768]{1,0:T(8,128)(2,1)}, bf16[512,768]{1,0:T(8,128)(2,1)S(1)}, u32[]{:S(2)}, u32[]{:S(2)}) collective-permute-start(bf16[512,768]{1,0:T(8,128)(2,1)} %get-tuple-element.69), channel_id=1, source_target_pairs={{0,1},{1,0},{2,3},{3,2},{4,5},{5,4},{6,7},{7,6},{8,9},{9,8},{10,11... | collective-permute-start | bytes 2359304 | tf_op jit(solution)/shard_map/ppermute | solution.py:463
  130.6 18.5 %collective-permute-start.17 = (bf16[512,640]{1,0:T(8,128)(2,1)}, bf16[512,640]{1,0:T(8,128)(2,1)S(1)}, u32[]{:S(2)}, u32[]{:S(2)}) collective-permute-start(bf16[512,640]{1,0:T(8,128)(2,1)} %get-tuple-element.71), channel_id=1, source_target_pairs={{0,4},{1,5},{2,6},{3,7},{4,0},{5,1},{6,2},{7,3},{8,12},{9,13},{10,... | collective-permute-start | bytes 1966088 | tf_op jit(solution)/shard_map/ppermute | solution.py:463
  154.4 27.1 %collective-permute-start.19 = (bf16[1024,2048]{1,0:T(8,128)(2,1)}, bf16[1024,2048]{1,0:T(8,128)(2,1)}, u32[]{:S(2)}, u32[]{:S(2)}) collective-permute-start(bf16[1024,2048]{1,0:T(8,128)(2,1)} %bitcast.21), channel_id=1, source_target_pairs={{0,64},{64,0},{1,65},{65,1},{2,66},{66,2},{3,67},{67,3},{4,68},{68... | collective-permute-start | bytes 12582920 | tf_op jit(solution)/shard_map/ppermute | solution.py:467
  158.0 10.1 %collective-permute-start.18 = (bf16[256,768]{1,0:T(8,128)(2,1)}, bf16[256,768]{1,0:T(8,128)(2,1)S(1)}, u32[]{:S(2)}, u32[]{:S(2)}) collective-permute-start(bf16[256,768]{1,0:T(8,128)(2,1)} %slice.135), channel_id=1, source_target_pairs={{0,4},{1,5},{2,6},{3,7},{4,0},{5,1},{6,2},{7,3},{8,12},{9,13},{10,... | collective-permute-start | bytes 1179656 | tf_op jit(solution)/shard_map/ppermute | solution.py:463
  160.5 7.8 %collective-permute-start.21 = (bf16[256,768]{1,0:T(8,128)(2,1)S(1)}, bf16[256,768]{1,0:T(8,128)(2,1)S(1)}, u32[]{:S(2)}, u32[]{:S(2)}) collective-permute-start(bf16[256,768]{1,0:T(8,128)(2,1)S(1)} %slice.134), channel_id=1, source_target_pairs={{0,1},{1,0},{2,3},{3,2},{4,5},{5,4},{6,7},{7,6},{8,9},{9,8},{10,11... | collective-permute-start | bytes 1179656 | tf_op jit(solution)/shard_map/ppermute | solution.py:463
  169.8 41.8 %all-to-all-start.2 = ((bf16[8,128,2048]{2,1,0:T(8,128)(2,1)}), bf16[8,128,2048]{2,1,0:T(8,128)(2,1)}, u32[]{:S(2)}, u32[]{:S(2)}) async-start(bf16[8,128,2048]{2,1,0:T(8,128)(2,1)} %bitcast.29), calls=%async_computation.2 | async-start | bytes 8388608 | tf_op jit(solution)/shard_map/all_to_all | solution.py:480
  176.5 22.9 %collective-permute-start.24 = (bf16[128,640]{1,0:T(8,128)(2,1)S(1)}, bf16[128,640]{1,0:T(8,128)(2,1)S(1)}, u32[]{:S(2)}, u32[]{:S(2)}) collective-permute-start(bf16[128,640]{1,0:T(8,128)(2,1)S(1)} %slice.139), channel_id=1, source_target_pairs={{0,1},{1,0},{2,3},{3,2},{4,5},{5,4},{6,7},{7,6},{8,9},{9,8},{10,11... | collective-permute-start | bytes 491528 | tf_op jit(solution)/shard_map/ppermute | solution.py:463
  179.1 20.4 %collective-permute-start.20 = (bf16[128,768]{1,0:T(8,128)(2,1)S(1)}, bf16[128,768]{1,0:T(8,128)(2,1)S(1)}, u32[]{:S(2)}, u32[]{:S(2)}) collective-permute-start(bf16[128,768]{1,0:T(8,128)(2,1)S(1)} %slice.138), channel_id=1, source_target_pairs={{0,16},{1,17},{2,18},{3,19},{4,20},{5,21},{6,22},{7,23},{8,24},{9,... | collective-permute-start | bytes 589832 | tf_op jit(solution)/shard_map/ppermute | solution.py:463
  181.4 18.1 %collective-permute-start.22 = (bf16[128,768]{1,0:T(8,128)(2,1)S(1)}, bf16[128,768]{1,0:T(8,128)(2,1)S(1)}, u32[]{:S(2)}, u32[]{:S(2)}) collective-permute-start(bf16[128,768]{1,0:T(8,128)(2,1)S(1)} %slice.137), channel_id=1, source_target_pairs={{0,4},{1,5},{2,6},{3,7},{4,0},{5,1},{6,2},{7,3},{8,12},{9,13},{10,... | collective-permute-start | bytes 589832 | tf_op jit(solution)/shard_map/ppermute | solution.py:463
  (33 other events, 306.7 us)
